TPU v7x, 32 devices: a whole 2x2x4 slice. The times are simulated.
32 devices in a mesh: groups: 2 (over y), tile: 4 (over z), sect: 2 (over x), chan: 2 (over core).
Axes of the slice: x: 2, y: 2, z: 4, core: 2. Of those that a mesh axis runs over, the one named last changes fastest.
Arguments:
- fine: bfloat16 [4, 2, 192, 64, 256], P(('groups', 'chan'), 'sect', 'tile'), parts along dimension 0, may hold values from -6 to 6
- conv_spatial: bfloat16 [4, 256, 256], replicated, may hold values from -0.375 to 0.375
- conv_mix: bfloat16 [5, 64, 64], replicated, may hold values from -0.3125 to 0.3125
- neighbours: int32 [2, 192, 5], P('sect', 'tile'), may hold values from 0 to 191, as said below
- fine_codes: int32 [2, 192, 5], P('sect', 'tile'), may hold values from 0 to 3
- restrict: bfloat16 [4, 256, 16], replicated, may hold values from -0.375 to 0.375
- restrict_codes: int32 [2, 192], P('sect', 'tile'), may hold values from 0 to 3
- route: int32 [2, 192], P('sect'), may hold values from 0 to 191, as said below
- coarse_spatial: bfloat16 [4, 256, 256], replicated, may hold values from -0.375 to 0.375
- coarse_mix: bfloat16 [4, 64, 64], replicated, may hold values from -0.375 to 0.375
- coarse_codes: int32 [2, 12, 3], P('sect', 'tile'), may hold values from 0 to 3
Outputs:
- fine_skip: bfloat16 [4, 2, 192, 64, 256], P(('groups', 'chan'), 'sect', 'tile'), parts along dimension 0
- coarse_out: bfloat16 [4, 2, 12, 64, 256], P(('groups', 'chan'), 'sect', 'tile'), parts along dimension 0
There are 2 independent parts, one for each index of `groups`. A program takes and returns all parts, laid end to end along the dimension named above; an argument that names none is the same for every part. Nothing has to cross between parts.
Inputs may be any that keep to these rules, and one draw needn't show every extreme that they name: (neighbours[s, b, t] - b) modulo 192 lies within -2 .. 2. `route`: each row is a permutation of the coarse slots; the fine blocks of each aligned run of 48 (one tile device) go exactly 12 to the slots of each aligned block of 48 slots.
All inputs are finite; a program needn't handle non-finite values.
Results may differ from a plain program's by a relative error of at most 0.0062.
Values may be sent and summed in bfloat16 or wider, within the bound.
No kernel may reach another device: no remote copies, remote signals or barrier semaphores. Data moves between devices by JAX's collectives and lax.ppermute only.
A program may use at most 128 MiB of HBM per device.

v0:
```python
import jax
import jax.numpy as jnp
from jax import lax
from jax.sharding import PartitionSpec as P

CH = 64
FB = 256
CQ = 16
PIECES = 16
TAPS = 5
ROTATIONS = 4
RIM = 2


def extended_2(cells, sides, width):
    for axis, dim in sides:
        count = lax.axis_size(axis)
        head = lax.slice_in_dim(cells, 0, width, axis=dim)
        tail = lax.slice_in_dim(cells, cells.shape[dim] - width, cells.shape[dim], axis=dim)
        cells = jnp.concatenate(
            [
                lax.ppermute(tail, axis, [(i, (i + 1) % count) for i in range(count)]),
                cells,
                lax.ppermute(head, axis, [((i + 1) % count, i) for i in range(count)]),
            ],
            axis=dim,
        )
    return cells


def shifted(value, axis, steps):
    count = lax.axis_size(axis)
    pairs = [(source, (source + steps) % count) for source in range(count)]
    return lax.ppermute(value, axis, pairs)


def rotated_product(rows, spatial_table, codes, form):
    selected = None
    for rotation in range(spatial_table.shape[0]):
        product_rot = jnp.einsum(
            form, rows, spatial_table[rotation], preferred_element_type=jnp.float32
        )
        if selected is None:
            selected = product_rot
        else:
            selected = jnp.where((codes == rotation)[:, None, None], product_rot, selected)
    return selected.astype(jnp.bfloat16)


def per_device(
    fine,
    conv_spatial,
    conv_mix,
    neighbours,
    fine_codes,
    restrict,
    restrict_codes,
    route,
    coarse_spatial,
    coarse_mix,
    coarse_codes,
):
    block_rows = fine[0, 0]
    count = block_rows.shape[0]
    section_blocks = route.shape[1]
    own_index = lax.axis_index("tile")
    extended = extended_2(block_rows, (("tile", 0),), RIM)
    local_rows = (neighbours[0] - own_index * count + RIM) % section_blocks
    mixed = jnp.zeros(block_rows.shape, jnp.float32)
    for term_index in range(TAPS):
        rows = jnp.take(extended, local_rows[:, term_index], axis=0)
        term = rotated_product(rows, conv_spatial, fine_codes[0, :, term_index], "bcf,fg->bcg")
        mixed = mixed + jnp.einsum(
            "dc,bcg->bdg", conv_mix[term_index], term, preferred_element_type=jnp.float32
        )
    fine_skip = (block_rows.astype(jnp.float32) + jax.nn.silu(mixed)).astype(jnp.bfloat16)
    stacked = restrict.transpose(1, 0, 2).reshape(FB, ROTATIONS * CQ)
    all_pieces = jnp.einsum("bcf,fk->bck", fine_skip, stacked, preferred_element_type=jnp.float32)
    all_pieces = all_pieces.reshape(count, CH, ROTATIONS, CQ)
    one_hot = (
        restrict_codes[0][:, None] == jnp.arange(ROTATIONS, dtype=jnp.int32)[None, :]
    ).astype(jnp.float32)
    piece = jnp.einsum("bcrq,br->bcq", all_pieces, one_hot).astype(jnp.bfloat16)
    width = piece.shape[1] * piece.shape[2]
    flat_piece = piece.reshape(count, width)
    table = route[0]
    gathered = lax.all_gather(flat_piece, "tile", axis=0, tiled=True)
    inverse = jnp.argsort(table)
    selected_rows = lax.dynamic_slice_in_dim(inverse, own_index * count, count)
    placed = jnp.take(gathered, selected_rows, axis=0)
    coarse_count = count // PIECES
    coarse = (
        placed.reshape(coarse_count, PIECES, CH, CQ)
        .transpose(0, 2, 1, 3)
        .reshape(coarse_count, CH, PIECES * CQ)
    )
    coarse_ext = extended_2(coarse, (("tile", 0),), 1)
    seam = shifted(coarse, "sect", 1)
    total = jnp.einsum("dc,ncg->ndg", coarse_mix[0], coarse, preferred_element_type=jnp.float32)
    for edge_index, beside in enumerate([coarse_ext[:-2], coarse_ext[2:], seam]):
        edge = rotated_product(
            beside, coarse_spatial, coarse_codes[0, :, edge_index], "ncg,ge->nce"
        )
        total = total + jnp.einsum(
            "dc,nce->nde", coarse_mix[edge_index + 1], edge, preferred_element_type=jnp.float32
        )
    coarse_out = (coarse.astype(jnp.float32) + jax.nn.silu(total)).astype(jnp.bfloat16)
    return (fine_skip[None, None], coarse_out[None, None])


def solution(mesh):
    placed = (
        P(("groups", "chan"), "sect", "tile", None, None),
        P(),
        P(),
        P("sect", "tile", None),
        P("sect", "tile", None),
        P(),
        P("sect", "tile"),
        P("sect", None),
        P(),
        P(),
        P("sect", "tile", None),
    )
    return jax.shard_map(
        per_device,
        mesh=mesh,
        in_specs=placed,
        out_specs=(
            P(("groups", "chan"), "sect", "tile", None, None),
            P(("groups", "chan"), "sect", "tile", None, None),
        ),
        check_vma=False,
    )
```

profile of v0, /device:TPU:0, one launch (start us, length us, event | category | flops | bytes accessed | tf_op | source)
XLA Modules:
  0.0 111.9 jit_solution(6174996889581949122)
XLA Ops:
  1.5 3.1 %collective-permute-start = (bf16[2,64,256]{2,1,0:T(8,128)(2,1)S(1)}, bf16[2,64,256]{2,1,0:T(8,128)(2,1)S(1)}, u32[]{:S(2)}, u32[]{:S(2)}) collective-permute-start(bf16[2,64,256]{2,1,0:T(8,128)(2,1)S(1)} %get-tuple-element.26), channel_id=1, source_target_pairs={{0,4},{4,8},{8,12},{12,0},{1,5},{5,9},{9,13},{13,1},{2,6},{6,10},{... | collective-permute-start | bytes 196616 | tf_op jit(solution)/shard_map/ppermute | solution.py:22
  4.6 2.1 %collective-permute-start.1 = (bf16[2,64,256]{2,1,0:T(8,128)(2,1)S(1)}, bf16[2,64,256]{2,1,0:T(8,128)(2,1)S(1)}, u32[]{:S(2)}, u32[]{:S(2)}) collective-permute-start(bf16[2,64,256]{2,1,0:T(8,128)(2,1)S(1)} %get-tuple-element.27), channel_id=1, source_target_pairs={{4,0},{8,4},{12,8},{0,12},{5,1},{9,5},{13,9},{1,13},{6,2},{10,6},{... | collective-permute-start | bytes 196616 | tf_op jit(solution)/shard_map/ppermute | solution.py:24
  6.7 3.8 %sort.17 = (s32[192]{0:T(256)}, s32[192]{0:T(256)S(1)}) sort(s32[192]{0:T(256)} %bitcast.250, s32[192]{0:T(256)S(1)} %iota.8), dimensions={0}, to_apply=%region_0.2 | sort | flops 1536 | bytes 3072 | tf_op jit(solution)/shard_map/jit(argsort)/sort | solution.py:88
  15.3 2.9 %fusion.81 = bf16[48,64,256]{2,1,0:T(8,128)(2,1)} fusion(bf16[4,256,256]{2,1,0:T(8,128)(2,1)} %param.14, bf16[48,64,256]{2,1,0:T(8,128)(2,1)S(1)} %gather_fusion.1, pred[48]{0:T(512)(128)(4,1)S(1)} %get-tuple-element.36), kind=kOutput, calls=%fused_computation.112 | convolution fusion | flops 403439616 | bytes 3276848 | tf_op jit(solution)/shard_map/bcf,fg->bcg/dot_general | solution.py:40
  18.2 1.8 %fusion.71 = bf16[48,64,256]{2,1,0:T(8,128)(2,1)} fusion(bf16[4,256,256]{2,1,0:T(8,128)(2,1)S(1)} %copy-done.15, bf16[48,64,256]{2,1,0:T(8,128)(2,1)S(1)} %gather_fusion.1, pred[48]{0:T(512)(128)(4,1)S(1)} %get-tuple-element.36), kind=kOutput, calls=%fused_computation.102 | convolution fusion | flops 403439616 | bytes 3277312 | tf_op jit(solution)/shard_map/bcf,fg->bcg/dot_general | solution.py:40
  20.0 1.8 %fusion.61 = bf16[48,64,256]{2,1,0:T(8,128)(2,1)} fusion(bf16[4,256,256]{2,1,0:T(8,128)(2,1)S(1)} %copy-done.15, bf16[48,64,256]{2,1,0:T(8,128)(2,1)S(1)} %gather_fusion.1, pred[48]{0:T(512)(128)(4,1)S(1)} %get-tuple-element.36), kind=kOutput, calls=%fused_computation.92 | convolution fusion | flops 403439616 | bytes 3277312 | tf_op jit(solution)/shard_map/bcf,fg->bcg/dot_general | solution.py:40
  22.5 3.0 %fusion.79 = bf16[48,64,256]{2,1,0:T(8,128)(2,1)} fusion(bf16[4,256,256]{2,1,0:T(8,128)(2,1)} %param.14, bf16[48,64,256]{2,1,0:T(8,128)(2,1)S(1)} %gather_fusion.2, pred[48]{0:T(512)(128)(4,1)S(1)} %get-tuple-element.34), kind=kOutput, calls=%fused_computation.110 | convolution fusion | flops 403439616 | bytes 3276848 | tf_op jit(solution)/shard_map/bcf,fg->bcg/dot_general | solution.py:40
  25.4 1.9 %fusion.69 = bf16[48,64,256]{2,1,0:T(8,128)(2,1)} fusion(bf16[4,256,256]{2,1,0:T(8,128)(2,1)S(1)} %copy-done.16, bf16[48,64,256]{2,1,0:T(8,128)(2,1)S(1)} %gather_fusion.2, pred[48]{0:T(512)(128)(4,1)S(1)} %get-tuple-element.34), kind=kOutput, calls=%fused_computation.100 | convolution fusion | flops 403439616 | bytes 3277312 | tf_op jit(solution)/shard_map/bcf,fg->bcg/dot_general | solution.py:40
  29.7 2.9 %fusion.77 = bf16[48,64,256]{2,1,0:T(8,128)(2,1)} fusion(bf16[4,256,256]{2,1,0:T(8,128)(2,1)} %param.14, bf16[48,64,256]{2,1,0:T(8,128)(2,1)S(1)} %gather_fusion.3, pred[48]{0:T(512)(128)(4,1)S(1)} %get-tuple-element.32), kind=kOutput, calls=%fused_computation.108 | convolution fusion | flops 403439616 | bytes 3276848 | tf_op jit(solution)/shard_map/bcf,fg->bcg/dot_general | solution.py:40
  32.6 1.8 %fusion.67 = bf16[48,64,256]{2,1,0:T(8,128)(2,1)} fusion(bf16[4,256,256]{2,1,0:T(8,128)(2,1)S(1)} %copy-done.17, bf16[48,64,256]{2,1,0:T(8,128)(2,1)S(1)} %gather_fusion.3, pred[48]{0:T(512)(128)(4,1)S(1)} %get-tuple-element.32), kind=kOutput, calls=%fused_computation.98 | convolution fusion | flops 403439616 | bytes 3277312 | tf_op jit(solution)/shard_map/bcf,fg->bcg/dot_general | solution.py:40
  36.9 2.9 %fusion.75 = bf16[48,64,256]{2,1,0:T(8,128)(2,1)} fusion(bf16[4,256,256]{2,1,0:T(8,128)(2,1)} %param.14, bf16[48,64,256]{2,1,0:T(8,128)(2,1)S(1)} %gather_fusion.4, pred[48]{0:T(512)(128)(4,1)S(1)} %get-tuple-element.30), kind=kOutput, calls=%fused_computation.106 | convolution fusion | flops 403439616 | bytes 3276848 | tf_op jit(solution)/shard_map/bcf,fg->bcg/dot_general | solution.py:40
  39.8 1.8 %fusion.65 = bf16[48,64,256]{2,1,0:T(8,128)(2,1)} fusion(bf16[4,256,256]{2,1,0:T(8,128)(2,1)S(1)} %copy-done.18, bf16[48,64,256]{2,1,0:T(8,128)(2,1)S(1)} %gather_fusion.4, pred[48]{0:T(512)(128)(4,1)S(1)} %get-tuple-element.30), kind=kOutput, calls=%fused_computation.96 | convolution fusion | flops 403439616 | bytes 3277312 | tf_op jit(solution)/shard_map/bcf,fg->bcg/dot_general | solution.py:40
  44.0 2.9 %fusion.73 = bf16[48,64,256]{2,1,0:T(8,128)(2,1)} fusion(bf16[4,256,256]{2,1,0:T(8,128)(2,1)} %param.14, bf16[48,64,256]{2,1,0:T(8,128)(2,1)S(1)} %gather_fusion.5, pred[48]{0:T(512)(128)(4,1)S(1)} %get-tuple-element.16), kind=kOutput, calls=%fused_computation.104 | convolution fusion | flops 403439616 | bytes 3276848 | tf_op jit(solution)/shard_map/bcf,fg->bcg/dot_general | solution.py:40
  46.9 1.8 %fusion.63 = bf16[48,64,256]{2,1,0:T(8,128)(2,1)} fusion(bf16[4,256,256]{2,1,0:T(8,128)(2,1)S(1)} %copy-done.19, bf16[48,64,256]{2,1,0:T(8,128)(2,1)S(1)} %gather_fusion.5, pred[48]{0:T(512)(128)(4,1)S(1)} %get-tuple-element.16), kind=kOutput, calls=%fused_computation.94 | convolution fusion | flops 403439616 | bytes 3277312 | tf_op jit(solution)/shard_map/bcf,fg->bcg/dot_general | solution.py:40
  48.7 1.8 %fusion.53 = bf16[48,64,256]{2,1,0:T(8,128)(2,1)} fusion(bf16[4,256,256]{2,1,0:T(8,128)(2,1)S(1)} %copy-done.19, bf16[48,64,256]{2,1,0:T(8,128)(2,1)S(1)} %gather_fusion.5, pred[48]{0:T(512)(128)(4,1)S(1)} %get-tuple-element.16), kind=kOutput, calls=%fused_computation.84 | convolution fusion | flops 403439616 | bytes 3277312 | tf_op jit(solution)/shard_map/bcf,fg->bcg/dot_general | solution.py:40
  50.5 5.3 %fusion.5 = f32[48,256,64]{1,2,0:T(8,128)} fusion(bf16[48,64,256]{2,1,0:T(8,128)(2,1)} %fusion.81, bf16[48,64,256]{2,1,0:T(8,128)(2,1)} %fusion.71, bf16[48,64,256]{2,1,0:T(8,128)(2,1)} %fusion.61, pred[48]{0:T(512)(128)(4,1)S(1)} %get-tuple-element.40, pred[48]{0:T(512)(128)(4,1)S(1)} %get-tuple-element.39, pred[48]{0:T(512)(128)(4,1)S(1)} %get-tuple-element.51, ...), kind=kOutput, calls=%fused_computation.18 | convolution fusion | flops 506462208 | bytes 9586688 | tf_op jit(solution)/shard_map/dc,bcg->bdg/dot_general | solution.py:73
  55.8 5.4 %fusion.6 = f32[48,256,64]{1,2,0:T(8,128)} fusion(bf16[48,64,256]{2,1,0:T(8,128)(2,1)} %fusion.79, bf16[48,64,256]{2,1,0:T(8,128)(2,1)} %fusion.69, bf16[48,64,256]{2,1,0:T(8,128)(2,1)} %fusion.59, pred[48]{0:T(512)(128)(4,1)S(1)} %get-tuple-element.42, pred[48]{0:T(512)(128)(4,1)S(1)} %get-tuple-element.41, pred[48]{0:T(512)(128)(4,1)S(1)} %get-tuple-element.50, ...), kind=kOutput, calls=%fused_computation.19 | convolution fusion | flops 506462208 | bytes 9586688 | tf_op jit(solution)/shard_map/dc,bcg->bdg/dot_general | solution.py:73
  61.2 5.4 %fusion.7 = f32[48,256,64]{1,2,0:T(8,128)} fusion(bf16[48,64,256]{2,1,0:T(8,128)(2,1)} %fusion.77, bf16[48,64,256]{2,1,0:T(8,128)(2,1)} %fusion.67, bf16[48,64,256]{2,1,0:T(8,128)(2,1)} %fusion.57, pred[48]{0:T(512)(128)(4,1)S(1)} %get-tuple-element.44, pred[48]{0:T(512)(128)(4,1)S(1)} %get-tuple-element.43, pred[48]{0:T(512)(128)(4,1)S(1)} %get-tuple-element.49, ...), kind=kOutput, calls=%fused_computation.20 | convolution fusion | flops 506462208 | bytes 9586688 | tf_op jit(solution)/shard_map/dc,bcg->bdg/dot_general | solution.py:73
  66.6 5.3 %fusion.8 = f32[48,256,64]{1,2,0:T(8,128)} fusion(bf16[48,64,256]{2,1,0:T(8,128)(2,1)} %fusion.75, bf16[48,64,256]{2,1,0:T(8,128)(2,1)} %fusion.65, bf16[48,64,256]{2,1,0:T(8,128)(2,1)} %fusion.55, pred[48]{0:T(512)(128)(4,1)S(1)} %get-tuple-element.46, pred[48]{0:T(512)(128)(4,1)S(1)} %get-tuple-element.45, pred[48]{0:T(512)(128)(4,1)S(1)} %get-tuple-element.52, ...), kind=kOutput, calls=%fused_computation.21 | convolution fusion | flops 506462208 | bytes 9586688 | tf_op jit(solution)/shard_map/dc,bcg->bdg/dot_general | solution.py:73
  71.9 8.8 %fusion.4 = bf16[48,64,256]{2,1,0:T(8,128)(2,1)S(1)} fusion(f32[48,256,64]{1,2,0:T(8,128)} %fusion.8, f32[48,256,64]{1,2,0:T(8,128)} %fusion.7, f32[48,256,64]{1,2,0:T(8,128)} %fusion.5, f32[48,256,64]{1,2,0:T(8,128)} %fusion.6, bf16[48,64,256]{2,1,0:T(8,128)(2,1)} %fusion.73, bf16[48,64,256]{2,1,0:T(8,128)(2,1)} %fusion.63, ...), kind=kOutput, calls=%fused_computation.17 | convolution fusion | flops 515112960 | bytes 22169600 | tf_op jit(solution)/shard_map/dc,bcg->bdg/dot_general | solution.py:73
  82.8 14.9 %all_gather.3 = bf16[192,1024]{1,0:T(8,128)(2,1)S(1)} all-gather(bf16[48,1024]{1,0:T(8,128)(2,1)S(1)} %copy.20), channel_id=1, replica_groups=mesh['groups'=2,'tile'=4,'sect'=2,'chan'=2] {'tile'}, dimensions={0}, use_global_device_ids=true | all-gather | bytes 491520 | tf_op jit(solution)/shard_map/all_gather | solution.py:87
  99.5 2.1 %collective-permute-start.3 = (bf16[1,64,256]{2,1,0:T(8,128)(2,1)S(1)}, bf16[1,64,256]{2,1,0:T(8,128)(2,1)S(1)}, u32[]{:S(2)}, u32[]{:S(2)}) collective-permute-start(bf16[1,64,256]{2,1,0:T(8,128)(2,1)S(1)} %copy.28), channel_id=1, source_target_pairs={{4,0},{8,4},{12,8},{0,12},{5,1},{9,5},{13,9},{1,13},{6,2},{10,6},{... | collective-permute-start | bytes 98312 | tf_op jit(solution)/shard_map/ppermute | solution.py:24
  102.9 1.8 %collective-permute-start.4 = (bf16[3,64,256]{2,1,0:T(8,128)(2,1)S(1)}, bf16[3,64,256]{2,1,0:T(8,128)(2,1)S(1)}, u32[]{:S(2)}, u32[]{:S(2)}) collective-permute-start(bf16[3,64,256]{2,1,0:T(8,128)(2,1)S(1)} %copy.22), channel_id=1, source_target_pairs={{0,2},{2,0},{1,3},{3,1},{4,6},{6,4},{5,7},{7,5},{8,10},{10,8},{9,1... | collective-permute-start | bytes 294920 | tf_op jit(solution)/shard_map/ppermute | solution.py:34
  105.0 3.5 %collective-permute-done.2 = bf16[1,64,256]{2,1,0:T(8,128)(2,1)S(1)} collective-permute-done((bf16[1,64,256]{2,1,0:T(8,128)(2,1)S(1)}, bf16[1,64,256]{2,1,0:T(8,128)(2,1)S(1)}, u32[]{:S(2)}, u32[]{:S(2)}) %collective-permute-start.2) | collective-permute-done | bytes 32800 | tf_op jit(solution)/shard_map/ppermute | solution.py:22
  (97 shorter events, 22.1 us)
Async XLA Ops:
  0.6 80.1 %copy-start = (bf16[4,256,16]{1,2,0:T(8,128)(2,1)S(1)}, bf16[4,256,16]{1,2,0:T(8,128)(2,1)}, u32[]{:S(2)}) copy-start(bf16[4,256,16]{1,2,0:T(8,128)(2,1)} %param.18) | copy-start | bytes 98308
  1.5 11.4 %collective-permute-start = (bf16[2,64,256]{2,1,0:T(8,128)(2,1)S(1)}, bf16[2,64,256]{2,1,0:T(8,128)(2,1)S(1)}, u32[]{:S(2)}, u32[]{:S(2)}) collective-permute-start(bf16[2,64,256]{2,1,0:T(8,128)(2,1)S(1)} %get-tuple-element.26), channel_id=1, source_target_pairs={{0,4},{4,8},{8,12},{12,0},{1,5},{5,9},{9,13},{13,1},{2,6},{6,10},{... | collective-permute-start | bytes 196616 | tf_op jit(solution)/shard_map/ppermute | solution.py:22
  4.6 8.4 %collective-permute-start.1 = (bf16[2,64,256]{2,1,0:T(8,128)(2,1)S(1)}, bf16[2,64,256]{2,1,0:T(8,128)(2,1)S(1)}, u32[]{:S(2)}, u32[]{:S(2)}) collective-permute-start(bf16[2,64,256]{2,1,0:T(8,128)(2,1)S(1)} %get-tuple-element.27), channel_id=1, source_target_pairs={{4,0},{8,4},{12,8},{0,12},{5,1},{9,5},{13,9},{1,13},{6,2},{10,6},{... | collective-permute-start | bytes 196616 | tf_op jit(solution)/shard_map/ppermute | solution.py:24
  15.3 4.7 %copy-start.10 = (bf16[48,64,256]{2,1,0:T(8,128)(2,1)}, bf16[48,64,256]{2,1,0:T(8,128)(2,1)S(1)}, u32[]{:S(2)}) copy-start(bf16[48,64,256]{2,1,0:T(8,128)(2,1)S(1)} %gather_fusion.1) | copy-start | bytes 4718596
  15.3 2.9 %copy-start.15 = (bf16[4,256,256]{2,1,0:T(8,128)(2,1)S(1)}, bf16[4,256,256]{2,1,0:T(8,128)(2,1)}, u32[]{:S(2)}) copy-start(bf16[4,256,256]{2,1,0:T(8,128)(2,1)} %param.14) | copy-start | bytes 1572868
  22.4 4.8 %copy-start.8 = (bf16[48,64,256]{2,1,0:T(8,128)(2,1)}, bf16[48,64,256]{2,1,0:T(8,128)(2,1)S(1)}, u32[]{:S(2)}) copy-start(bf16[48,64,256]{2,1,0:T(8,128)(2,1)S(1)} %gather_fusion.2) | copy-start | bytes 4718596
  22.5 3.0 %copy-start.16 = (bf16[4,256,256]{2,1,0:T(8,128)(2,1)S(1)}, bf16[4,256,256]{2,1,0:T(8,128)(2,1)}, u32[]{:S(2)}) copy-start(bf16[4,256,256]{2,1,0:T(8,128)(2,1)} %param.14) | copy-start | bytes 1572868
  29.7 4.7 %copy-start.6 = (bf16[48,64,256]{2,1,0:T(8,128)(2,1)}, bf16[48,64,256]{2,1,0:T(8,128)(2,1)S(1)}, u32[]{:S(2)}) copy-start(bf16[48,64,256]{2,1,0:T(8,128)(2,1)S(1)} %gather_fusion.3) | copy-start | bytes 4718596
  29.7 2.9 %copy-start.17 = (bf16[4,256,256]{2,1,0:T(8,128)(2,1)S(1)}, bf16[4,256,256]{2,1,0:T(8,128)(2,1)}, u32[]{:S(2)}) copy-start(bf16[4,256,256]{2,1,0:T(8,128)(2,1)} %param.14) | copy-start | bytes 1572868
  36.9 4.7 %copy-start.4 = (bf16[48,64,256]{2,1,0:T(8,128)(2,1)}, bf16[48,64,256]{2,1,0:T(8,128)(2,1)S(1)}, u32[]{:S(2)}) copy-start(bf16[48,64,256]{2,1,0:T(8,128)(2,1)S(1)} %gather_fusion.4) | copy-start | bytes 4718596
  36.9 2.9 %copy-start.18 = (bf16[4,256,256]{2,1,0:T(8,128)(2,1)S(1)}, bf16[4,256,256]{2,1,0:T(8,128)(2,1)}, u32[]{:S(2)}) copy-start(bf16[4,256,256]{2,1,0:T(8,128)(2,1)} %param.14) | copy-start | bytes 1572868
  44.0 4.7 %copy-start.3 = (bf16[48,64,256]{2,1,0:T(8,128)(2,1)}, bf16[48,64,256]{2,1,0:T(8,128)(2,1)S(1)}, u32[]{:S(2)}) copy-start(bf16[48,64,256]{2,1,0:T(8,128)(2,1)S(1)} %gather_fusion.5) | copy-start | bytes 4718596
  44.0 2.9 %copy-start.19 = (bf16[4,256,256]{2,1,0:T(8,128)(2,1)S(1)}, bf16[4,256,256]{2,1,0:T(8,128)(2,1)}, u32[]{:S(2)}) copy-start(bf16[4,256,256]{2,1,0:T(8,128)(2,1)} %param.14) | copy-start | bytes 1572868
  48.7 1.8 %copy-start.20 = (bf16[5,64,64]{2,1,0:T(8,128)(2,1)S(1)}, bf16[5,64,64]{2,1,0:T(8,128)(2,1)}, u32[]{:S(2)}) copy-start(bf16[5,64,64]{2,1,0:T(8,128)(2,1)} %param.15) | copy-start | bytes 122884
  50.5 5.3 %copy-start.9 = (bf16[48,64,256]{2,1,0:T(8,128)(2,1)S(1)}, bf16[48,64,256]{2,1,0:T(8,128)(2,1)}, u32[]{:S(2)}) copy-start(bf16[48,64,256]{2,1,0:T(8,128)(2,1)} %copy-done.8) | copy-start | bytes 4718596
  55.8 5.4 %copy-start.7 = (bf16[48,64,256]{2,1,0:T(8,128)(2,1)S(1)}, bf16[48,64,256]{2,1,0:T(8,128)(2,1)}, u32[]{:S(2)}) copy-start(bf16[48,64,256]{2,1,0:T(8,128)(2,1)} %copy-done.6) | copy-start | bytes 4718596
  61.2 5.4 %copy-start.5 = (bf16[48,64,256]{2,1,0:T(8,128)(2,1)S(1)}, bf16[48,64,256]{2,1,0:T(8,128)(2,1)}, u32[]{:S(2)}) copy-start(bf16[48,64,256]{2,1,0:T(8,128)(2,1)} %copy-done.4) | copy-start | bytes 4718596
  66.6 5.3 %copy-start.1 = (bf16[1,1,48,64,256]{4,3,2,1,0:T(8,128)(2,1)S(1)}, bf16[1,1,48,64,256]{4,3,2,1,0:T(8,128)(2,1)}, u32[]{:S(2)}) copy-start(bf16[1,1,48,64,256]{4,3,2,1,0:T(8,128)(2,1)} %param.13) | copy-start | bytes 4718596
  99.0 2.6 %copy-start.14 = (s32[1,3,3]{2,0,1:T(1,128)S(1)}, s32[1,3,3]{2,0,1:T(1,128)}, u32[]{:S(2)}) copy-start(s32[1,3,3]{2,0,1:T(1,128)} %param.23) | copy-start | bytes 112
  99.2 5.6 %copy-start.12 = (bf16[4,256,256]{2,1,0:T(8,128)(2,1)S(1)}, bf16[4,256,256]{2,1,0:T(8,128)(2,1)}, u32[]{:S(2)}) copy-start(bf16[4,256,256]{2,1,0:T(8,128)(2,1)} %param.21) | copy-start | bytes 1572868
  99.5 5.3 %collective-permute-start.3 = (bf16[1,64,256]{2,1,0:T(8,128)(2,1)S(1)}, bf16[1,64,256]{2,1,0:T(8,128)(2,1)S(1)}, u32[]{:S(2)}, u32[]{:S(2)}) collective-permute-start(bf16[1,64,256]{2,1,0:T(8,128)(2,1)S(1)} %copy.28), channel_id=1, source_target_pairs={{4,0},{8,4},{12,8},{0,12},{5,1},{9,5},{13,9},{1,13},{6,2},{10,6},{... | collective-permute-start | bytes 98312 | tf_op jit(solution)/shard_map/ppermute | solution.py:24
  102.7 5.8 %collective-permute-start.2 = (bf16[1,64,256]{2,1,0:T(8,128)(2,1)S(1)}, bf16[1,64,256]{2,1,0:T(8,128)(2,1)S(1)}, u32[]{:S(2)}, u32[]{:S(2)}) collective-permute-start(bf16[1,64,256]{2,1,0:T(8,128)(2,1)S(1)} %copy.25), channel_id=1, source_target_pairs={{0,4},{4,8},{8,12},{12,0},{1,5},{5,9},{9,13},{13,1},{2,6},{6,10},{... | collective-permute-start | bytes 98312 | tf_op jit(solution)/shard_map/ppermute | solution.py:22
  102.9 6.5 %copy-start.13 = (bf16[4,64,64]{2,1,0:T(8,128)(2,1)S(1)}, bf16[4,64,64]{2,1,0:T(8,128)(2,1)}, u32[]{:S(2)}) copy-start(bf16[4,64,64]{2,1,0:T(8,128)(2,1)} %param.22) | copy-start | bytes 98308
  102.9 7.1 %collective-permute-start.4 = (bf16[3,64,256]{2,1,0:T(8,128)(2,1)S(1)}, bf16[3,64,256]{2,1,0:T(8,128)(2,1)S(1)}, u32[]{:S(2)}, u32[]{:S(2)}) collective-permute-start(bf16[3,64,256]{2,1,0:T(8,128)(2,1)S(1)} %copy.22), channel_id=1, source_target_pairs={{0,2},{2,0},{1,3},{3,1},{4,6},{6,4},{5,7},{7,5},{8,10},{10,8},{9,1... | collective-permute-start | bytes 294920 | tf_op jit(solution)/shard_map/ppermute | solution.py:34
  (2 other events, 3.2 us)
where the time goes:
time: 112 us
  matrix products  67.5 us (60%)
  blocking collectives  14.9 us (13%)
  starting transfers between devices  9.18 us (8%)
  other arithmetic  8.5 us (8%)
  local copies, waits for them, and re-layouts  7.19 us (6%)
  waiting for transfers between devices  3.54 us (3%)
    dot_general x24, matrix products, rotated_product(): jnp.einsum(form, rows, spatial_table[rotation], preferred_element_type=jn...  34 us
    dot_general x5, matrix products, per_device(): jnp.einsum('dc,bcg->bdg', conv_mix[term_index], term, preferred_element_t...  30.2 us
    all_gather x1, blocking collectives, per_device(): gathered = lax.all_gather(flat_piece, 'tile', axis=0, tiled=True)  14.9 us
    ppermute x2, starting transfers between devices, extended_2(): lax.ppermute(head, axis, [((i + 1) % count, i) for i in range(count)])  4.2 us
    sort x1, other arithmetic, per_device(): inverse = jnp.argsort(table)  3.84 us
    ppermute x2, waiting for transfers between devices, extended_2(): lax.ppermute(tail, axis, [(i, (i + 1) % count) for i in range(count)])  3.53 us
    gather x5, local copies, waits for them, and re-layouts, per_device(): rows = jnp.take(extended, local_rows[:, term_index], axis=0)  3.3 us
    ppermute x2, starting transfers between devices, extended_2(): lax.ppermute(tail, axis, [(i, (i + 1) % count) for i in range(count)])  3.13 us
  transfers between devices with their start and end apart: 5, of which 1 were waited for; matrix products, arithmetic and copies ran while one was open for 8% of the time, Pallas kernels for 0%

commit v1 on v0

v1 whole, which is shorter than its diff:
```python
import functools

import jax
import jax.numpy as jnp
from jax import lax
from jax.experimental import pallas as pl
from jax.experimental.pallas import tpu as pltpu
from jax.sharding import PartitionSpec as P

LANES = 128
RIM = 2
EDGE = 2 * RIM
CHUNK = 8
VMEM_BYTES = 48 * 1024 * 1024

SMEM = functools.partial(pl.BlockSpec, memory_space=pltpu.SMEM)
VMEM = functools.partial(pl.BlockSpec, memory_space=pltpu.VMEM)
ANY = functools.partial(pl.BlockSpec, memory_space=pl.ANY)
F32 = jnp.float32
BF16 = jnp.bfloat16


def dot(a, b):
    return jnp.dot(a, b, preferred_element_type=F32)


def silu(v):
    return v * (0.5 + 0.5 * jnp.tanh(0.5 * v))


def shifted(value, axis, steps):
    count = lax.axis_size(axis)
    return lax.ppermute(value, axis, [(i, (i + steps) % count) for i in range(count)])


def rotations_of(table_ref, rows, store):
    for rotation in range(table_ref.shape[0]):
        store(rotation, dot(rows, table_ref[rotation]).astype(BF16))


def joined_mix(mix_ref, terms):
    return jnp.concatenate([mix_ref[t] for t in range(terms)], axis=1)


def stacked_restrict(restrict_ref):
    parts = [restrict_ref[r].astype(F32) for r in range(restrict_ref.shape[0])]
    width = sum(p.shape[1] for p in parts)
    return jnp.concatenate(parts * (LANES // width), axis=1).astype(BF16)


def mixed_skip(y_ref, y_index, taps, mix_wide, mix_ref, own):
    terms = [y_ref[y_index(t)] for t in range(taps)]
    wide = mix_wide.shape[1] // mix_ref.shape[1]
    mixed = dot(mix_wide, jnp.concatenate(terms[:wide], axis=0))
    for t in range(wide, taps):
        mixed = mixed + dot(mix_ref[t], terms[t])
    return (own.astype(F32) + silu(mixed)).astype(BF16)


def place(acc_ref, at, product, code, rank, cq):
    per = LANES // cq
    slot = lax.rem(rank, per)
    amount = lax.rem((slot - code) * cq + LANES, LANES)
    turned = pltpu.roll(product, amount, axis=1)
    lane = lax.broadcasted_iota(jnp.int32, turned.shape, 1)
    at = at + lax.div(rank, per)
    acc_ref[at] = jnp.where(lax.div(lane, cq) == slot, turned, acc_ref[at])


def next_rank(counts_ref, dest):
    rank = counts_ref[dest]
    counts_ref[dest] = rank + 1
    return rank


def inner_kernel(
    nbr_ref, code_ref, rcode_ref, route_ref, x_ref, spatial_ref, mix_ref, restrict_ref,
    skip_ref, acc_ref, y_ref, counts_ref,
):
    count = x_ref.shape[0]
    channels, cells = x_ref.shape[1:]
    cq = restrict_ref.shape[2]
    taps = mix_ref.shape[0]
    tiles = route_ref.shape[1] // count
    halves = acc_ref.shape[0] // tiles
    me = lax.axis_index("tile")

    @pl.loop(0, count // CHUNK)
    def _(step):
        base = step * CHUNK
        rows = x_ref[pl.ds(base, CHUNK)].reshape(CHUNK * channels, cells)

        def store(rotation, value):
            y_ref[pl.ds(rotation * count + base, CHUNK)] = value.reshape(CHUNK, channels, cells)

        rotations_of(spatial_ref, rows, store)

    for d in range(tiles):
        counts_ref[d] = 0
    mix_wide = joined_mix(mix_ref, min(taps, cells // channels))
    stacked = stacked_restrict(restrict_ref)

    @pl.loop(0, count // CHUNK)
    def _(step):
        base = step * CHUNK
        for i in range(CHUNK):
            b = base + i

            def y_index(t):
                local = nbr_ref[b, t] - me * count
                local = jnp.clip(local, 0, count - 1)
                return code_ref[b, t] * count + local

            skip_ref[b] = mixed_skip(y_ref, y_index, taps, mix_wide, mix_ref, x_ref[b])
        rows = skip_ref[pl.ds(base, CHUNK)].reshape(CHUNK * channels, cells)
        products = dot(rows, stacked)
        for i in range(CHUNK):
            b = base + i
            dest = lax.div(route_ref[0, me * count + b], count)
            rank = next_rank(counts_ref, dest)
            hop = lax.rem(dest - me + tiles, tiles)
            place(
                acc_ref, hop * halves, products[i * channels:(i + 1) * channels],
                rcode_ref[0, b], rank, cq,
            )


def rim_kernel(
    nbr_ref, code_ref, rcode_ref, route_ref, before_ref, head_ref, tail_ref, after_ref,
    spatial_ref, mix_ref, restrict_ref, acc_in_ref, skip_in_ref,
    skip_ref, *refs,
):
    out_refs, (acc_ref, x_ref, y_ref, done_ref, counts_ref, sem) = refs[:-6], refs[-6:]
    del skip_in_ref
    count = rcode_ref.shape[1]
    channels, cells = head_ref.shape[1:]
    cq = restrict_ref.shape[2]
    taps = mix_ref.shape[0]
    blocks = route_ref.shape[1]
    tiles = blocks // count
    halves = acc_ref.shape[0] // tiles
    me = lax.axis_index("tile")
    side = EDGE + RIM

    x_ref[0:RIM] = before_ref[...]
    x_ref[RIM:side] = head_ref[...]
    x_ref[side:side + EDGE] = tail_ref[...]
    x_ref[side + EDGE:] = after_ref[...]
    rows = x_ref[...].reshape(2 * side * channels, cells)

    def store(rotation, value):
        y_ref[rotation * 2 * side:(rotation + 1) * 2 * side] = value.reshape(2 * side, channels, cells)

    rotations_of(spatial_ref, rows, store)
    acc_ref[...] = acc_in_ref[...]
    mix_wide = joined_mix(mix_ref, min(taps, cells // channels))
    stacked = stacked_restrict(restrict_ref)
    outer = [b for b in range(RIM)] + [count - RIM + b for b in range(RIM)]
    for i, b in enumerate(outer):
        first = 0 if i < RIM else count + 2 * RIM - side

        def y_index(t):
            local = nbr_ref[b, t] - me * count + RIM
            local = jnp.where(local < 0, local + blocks, local)
            local = jnp.where(local >= blocks, local - blocks, local)
            local = jnp.clip(local - first, 0, side - 1) + (0 if i < RIM else side)
            return code_ref[b, t] * (2 * side) + local

        own = x_ref[RIM + i if i < RIM else side + EDGE - 2 * RIM + i]
        done_ref[i] = mixed_skip(y_ref, y_index, taps, mix_wide, mix_ref, own)
    copies = [
        pltpu.make_async_copy(done_ref.at[pl.ds(0, RIM)], skip_ref.at[pl.ds(0, RIM)], sem.at[0]),
        pltpu.make_async_copy(done_ref.at[pl.ds(RIM, RIM)], skip_ref.at[pl.ds(count - RIM, RIM)], sem.at[1]),
    ]
    for copy in copies:
        copy.start()
    products = dot(done_ref[...].reshape(2 * RIM * channels, cells), stacked)
    for d in range(tiles):
        counts_ref[d] = 0
    for b in range(count):
        dest = lax.div(route_ref[0, me * count + b], count)
        rank = next_rank(counts_ref, dest)
        if b in outer:
            i = outer.index(b)
            hop = lax.rem(dest - me + tiles, tiles)
            place(
                acc_ref, hop * halves, products[i * channels:(i + 1) * channels],
                rcode_ref[0, b], rank, cq,
            )
    lane = lax.broadcasted_iota(jnp.int32, (channels // 2, LANES), 1)
    half = LANES // 2
    for hop in range(tiles):
        out = out_refs[hop]
        row = 0
        for h in range(halves):
            value = acc_ref[hop * halves + h]
            if out.shape[0] - row >= channels:
                out[row:row + channels] = value.astype(BF16)
                row += channels
            else:
                low = pltpu.roll(value[channels // 2:], half, axis=1)
                out[row:] = jnp.where(lane < half, value[:channels // 2], low).astype(BF16)
    for copy in copies:
        copy.wait()


def route_slots(route_ref, slots_ref, count):
    tiles = route_ref.shape[1] // count
    per = count // tiles
    me = lax.axis_index("tile")
    for hop in range(tiles):
        source = lax.rem(me - hop + tiles, tiles)
        at = hop * per
        for b in range(count):
            slot = route_ref[0, source * count + b] - me * count
            slots_ref[at] = slot
            at = at + jnp.where((slot >= 0) & (slot < count), 1, 0)


def prepare_kernel(count, route_ref, late_ref, slots_ref):
    del late_ref
    route_slots(route_ref, slots_ref, count)


def merge_kernel(cq, slots_ref, *refs):
    sent_refs, (coarse_ref, first_ref, last_ref, acc_ref) = refs[:-4], refs[-4:]
    tiles = len(sent_refs)
    blocks, channels, cells = coarse_ref.shape
    per_block = cells // cq
    per = blocks * per_block // tiles
    lanes = LANES // cq
    half = LANES // 2
    lane = lax.broadcasted_iota(jnp.int32, (channels, LANES), 1)
    group = lax.div(lane, cq)
    for hop, sent in enumerate(sent_refs):
        for rank in range(per):
            row = rank // lanes * channels
            if sent.shape[0] - row >= channels:
                piece = sent[row:row + channels].astype(F32)
            else:
                packed = sent[row:].astype(F32)
                piece = jnp.concatenate([packed, pltpu.roll(packed, half, axis=1)], axis=0)
            slot = slots_ref[hop * per + rank]
            target = lax.rem(slot, lanes)
            amount = lax.rem((target - rank % lanes) * cq + LANES, LANES)
            at = lax.div(slot, lanes)
            acc_ref[at] = jnp.where(group == target, pltpu.roll(piece, amount, axis=1), acc_ref[at])
    parts = cells // LANES
    for c in range(blocks):
        value = jnp.concatenate([acc_ref[c * parts + h] for h in range(parts)], axis=1).astype(BF16)
        coarse_ref[c] = value
        if c == 0:
            first_ref[...] = value
        if c == blocks - 1:
            last_ref[...] = value


def coarse_kernel(code_ref, coarse_ref, left_ref, right_ref, seam_ref, spatial_ref, mix_ref, out_ref):
    blocks = coarse_ref.shape[0]
    mix_wide = joined_mix(mix_ref, mix_ref.shape[0])
    for c in range(blocks):
        own = coarse_ref[c]
        beside = [
            left_ref[...] if c == 0 else coarse_ref[c - 1],
            right_ref[...] if c == blocks - 1 else coarse_ref[c + 1],
            seam_ref[c],
        ]
        edges = [dot(rows, spatial_ref[code_ref[c, e]]).astype(BF16) for e, rows in enumerate(beside)]
        total = dot(mix_wide, jnp.concatenate([own] + edges, axis=0))
        out_ref[c] = (own.astype(F32) + silu(total)).astype(BF16)


def params(**more):
    return pltpu.CompilerParams(vmem_limit_bytes=VMEM_BYTES, **more)


def per_device(
    fine, conv_spatial, conv_mix, neighbours, fine_codes, restrict, restrict_codes, route,
    coarse_spatial, coarse_mix, coarse_codes,
):
    x = fine[0, 0]
    count, channels, cells = x.shape
    rotations = conv_spatial.shape[0]
    cq = restrict.shape[2]
    tiles = route.shape[1] // count
    per = count // tiles
    halves = -(-per * cq // LANES)
    left_over = per * cq % LANES
    sent_rows = per * cq // LANES * channels
    if left_over:
        sent_rows += channels // 2 if left_over <= LANES // 2 else channels
    blocks = count * cq // cells
    nbr, codes = neighbours[0], fine_codes[0]

    before = shifted(x[count - RIM:], "tile", 1)
    after = shifted(x[:RIM], "tile", -1)
    skip, acc = pl.pallas_call(
        inner_kernel,
        out_shape=(
            jax.ShapeDtypeStruct(x.shape, BF16),
            jax.ShapeDtypeStruct((tiles * halves, channels, LANES), F32),
        ),
        in_specs=[SMEM()] * 4 + [VMEM()] * 4,
        out_specs=(VMEM(), VMEM()),
        scratch_shapes=[
            pltpu.VMEM((rotations * count, channels, cells), BF16),
            pltpu.SMEM((tiles,), jnp.int32),
        ],
        compiler_params=params(),
        cost_estimate=pl.CostEstimate(flops=4 * 10**9, bytes_accessed=4 * 10**6, transcendentals=10**6),
        name="inner",
    )(nbr, codes, restrict_codes, route, x, conv_spatial, conv_mix, restrict)

    side = EDGE + RIM
    whole = pl.BlockSpec((RIM, channels, cells), lambda i: (0, 0, 0))

    def full(a):
        return pl.BlockSpec(a.shape, lambda i: (0,) * a.ndim)

    sent_shape = jax.ShapeDtypeStruct((sent_rows, LANES), BF16)
    skip, *sent = pl.pallas_call(
        rim_kernel,
        grid=(1,),
        out_shape=(jax.ShapeDtypeStruct(x.shape, BF16),) + (sent_shape,) * tiles,
        in_specs=[SMEM()] * 4
        + [
            whole,
            pl.BlockSpec((EDGE, channels, cells), lambda i: (0, 0, 0)),
            pl.BlockSpec((EDGE, channels, cells), lambda i: (count // EDGE - 1, 0, 0)),
            whole,
            full(conv_spatial),
            full(conv_mix),
            full(restrict),
            full(acc),
            ANY(),
        ],
        out_specs=(ANY(),) + (pl.BlockSpec((sent_rows, LANES), lambda i: (0, 0)),) * tiles,
        scratch_shapes=[
            pltpu.VMEM(acc.shape, F32),
            pltpu.VMEM((2 * side, channels, cells), BF16),
            pltpu.VMEM((rotations * 2 * side, channels, cells), BF16),
            pltpu.VMEM((2 * RIM, channels, cells), BF16),
            pltpu.SMEM((tiles,), jnp.int32),
            pltpu.SemaphoreType.DMA((2,)),
        ],
        input_output_aliases={12: 0},
        compiler_params=params(),
        name="rim",
    )(nbr, codes, restrict_codes, route, before, x, x, after, conv_spatial, conv_mix, restrict, acc, skip)

    slots = pl.pallas_call(
        functools.partial(prepare_kernel, count),
        out_shape=jax.ShapeDtypeStruct((count + 1,), jnp.int32),
        in_specs=[SMEM(), ANY()],
        out_specs=SMEM(),
        name="slots",
    )(route, sent[0])
    arrived = [sent[0]] + [shifted(sent[hop], "tile", hop) for hop in range(1, tiles)]

    block_shape = jax.ShapeDtypeStruct((channels, cells), BF16)
    coarse, first, last = pl.pallas_call(
        functools.partial(merge_kernel, cq),
        out_shape=(jax.ShapeDtypeStruct((blocks, channels, cells), BF16), block_shape, block_shape),
        in_specs=[SMEM()] + [VMEM()] * tiles,
        out_specs=(VMEM(), VMEM(), VMEM()),
        scratch_shapes=[pltpu.VMEM((blocks * cells // LANES, channels, LANES), F32)],
        compiler_params=params(),
        name="merge",
    )(slots, *arrived)

    left = shifted(last, "tile", 1)
    right = shifted(first, "tile", -1)
    seam = shifted(coarse, "sect", 1)
    coarse_out = pl.pallas_call(
        coarse_kernel,
        out_shape=jax.ShapeDtypeStruct(coarse.shape, BF16),
        in_specs=[SMEM()] + [VMEM()] * 6,
        out_specs=VMEM(),
        compiler_params=params(),
        name="coarse",
    )(coarse_codes[0], coarse, left, right, seam, coarse_spatial, coarse_mix)
    return (skip[None, None], coarse_out[None, None])


def solution(mesh):
    data = P(("groups", "chan"), "sect", "tile", None, None)
    placed = (
        data,
        P(),
        P(),
        P("sect", "tile", None),
        P("sect", "tile", None),
        P(),
        P("sect", "tile"),
        P("sect", None),
        P(),
        P(),
        P("sect", "tile", None),
    )
    return jax.shard_map(
        per_device, mesh=mesh, in_specs=placed, out_specs=(data, data), check_vma=False
    )
```

time: 112 us -> 45.9 us (0.41)
  matrix products: 67.5 us -> 0 us
  Pallas kernels: 0 us -> 17.3 us
  blocking collectives: 14.9 us -> 0 us
  other arithmetic: 8.5 us -> 0 us
  starting transfers between devices: 9.18 us -> 14.4 us
  local copies, waits for them, and re-layouts: 7.19 us -> 10 us
    dot_general x35 -> x0, matrix products: 67.5 us -> none  [the longest x24 34 us: rotated_product(): jnp.einsum(form, rows, spatial_table[rotation], preferred_element_type=jn...]
    pallas_call x0 -> x5, Pallas kernels: none -> 17.3 us  [the longest x1 9.02 us: per_device(): pl.pallas_call(inner_kernel, out_shape=(jax.ShapeDtypeStruct(x.shape, BF1...]
    all_gather x1 -> x0, blocking collectives: 14.9 us -> none  [per_device(): gathered = lax.all_gather(flat_piece, 'tile', axis=0, tiled=True)]
    unnamed x42 -> x26, local copies, waits for them, and re-layouts: 0.11 us -> 9.13 us
    ppermute x5 -> x8, starting transfers between devices: 9.18 us -> 14.4 us  [shifted(): lax.ppermute(value, axis, [(i, (i + steps) % count) for i in range(count)])]
    gather x7 -> x0, local copies, waits for them, and re-layouts: 4.59 us -> none  [the longest x5 3.3 us: per_device(): rows = jnp.take(extended, local_rows[:, term_index], axis=0)]
    sort x1 -> x0, other arithmetic: 3.84 us -> none  [per_device(): inverse = jnp.argsort(table)]
    eq x3 -> x0, other arithmetic: 2.08 us -> none  [the longest x2 1.34 us: rotated_product(): codes == rotation]
  transfers between devices with their start and end apart: 5 -> 8, of which waited for: 1 -> 3; matrix products, arithmetic and copies ran while one was open for 8% -> 5% of each run, Pallas kernels for 0% -> 24%
where the time goes in v1:
time: 45.9 us; the launch traced here: 45.3 us
  Pallas kernels  17.3 us (38%)
  starting transfers between devices  14.4 us (31%)
  local copies, waits for them, and re-layouts  10 us (22%)
  waiting for transfers between devices  2.92 us (6%)
  between operations  0.71 us (2%)
    ppermute x8, starting transfers between devices, shifted(): lax.ppermute(value, axis, [(i, (i + steps) % count) for i in range(count)])  14.4 us
    unnamed x26, local copies, waits for them, and re-layouts  9.13 us
    pallas_call x1, Pallas kernels, per_device(): pl.pallas_call(inner_kernel, out_shape=(jax.ShapeDtypeStruct(x.shape, BF1...  9.02 us
    pallas_call x1, Pallas kernels, per_device(): pl.pallas_call(rim_kernel, grid=(1,), out_shape=(jax.ShapeDtypeStruct(x.s...  3.06 us
    ppermute x8, waiting for transfers between devices, shifted(): lax.ppermute(value, axis, [(i, (i + steps) % count) for i in range(count)])  2.92 us
    pallas_call x1, Pallas kernels, per_device(): pl.pallas_call(coarse_kernel, out_shape=jax.ShapeDtypeStruct(coarse.shape...  1.92 us
    pallas_call x1, Pallas kernels, per_device(): pl.pallas_call(functools.partial(prepare_kernel, count), out_shape=jax.Sh...  1.81 us
    pallas_call x1, Pallas kernels, per_device(): pl.pallas_call(functools.partial(merge_kernel, cq), out_shape=(jax.ShapeD...  1.47 us
  transfers between devices with their start and end apart: 8, of which 3 were waited for; matrix products, arithmetic and copies ran while one was open for 5% of the time, Pallas kernels for 24%

profile of v1, /device:TPU:0, one launch (start us, length us, event | category | flops | bytes accessed | tf_op | source)
XLA Modules:
  0.0 45.3 jit_solution(4234937563430471052)
XLA Ops:
  0.6 0.9 %slice_bitcast_fusion = (bf16[2,64,256]{2,1,0:T(8,128)(2,1)S(1)}, bf16[2,64,256]{2,1,0:T(8,128)(2,1)S(1)}) fusion(bf16[1,1,48,64,256]{4,3,2,1,0:T(8,128)(2,1)} %param.11), kind=kLoop, calls=%fused_computation | loop fusion | bytes 262144 | tf_op jit(solution)/shard_map/slice | solution.py:296
  1.5 3.1 %collective-permute-start = (bf16[2,64,256]{2,1,0:T(8,128)(2,1)S(1)}, bf16[2,64,256]{2,1,0:T(8,128)(2,1)S(1)}, u32[]{:S(2)}, u32[]{:S(2)}) collective-permute-start(bf16[2,64,256]{2,1,0:T(8,128)(2,1)S(1)} %get-tuple-element.23), channel_id=1, source_target_pairs={{0,4},{4,8},{8,12},{12,0},{1,5},{5,9},{9,13},{13,1},{2,6},{6,10},{... | collective-permute-start | bytes 196616 | tf_op jit(solution)/shard_map/ppermute | solution.py:33
  4.6 2.1 %collective-permute-start.1 = (bf16[2,64,256]{2,1,0:T(8,128)(2,1)S(1)}, bf16[2,64,256]{2,1,0:T(8,128)(2,1)S(1)}, u32[]{:S(2)}, u32[]{:S(2)}) collective-permute-start(bf16[2,64,256]{2,1,0:T(8,128)(2,1)S(1)} %get-tuple-element.22), channel_id=1, source_target_pairs={{0,12},{4,0},{8,4},{12,8},{1,13},{5,1},{9,5},{13,9},{2,14},{6,2},{... | collective-permute-start | bytes 196616 | tf_op jit(solution)/shard_map/ppermute | solution.py:33
  6.7 0.9 %copy.17.restrict_ref = bf16[4,256,16]{2,1,0:T(8,128)(2,1)S(1)} copy(bf16[4,256,16]{1,2,0:T(8,128)(2,1)} %param.16) | data formatting | bytes 65536 | tf_op args[5]
  7.6 0.8 %copy.14 = s32[1,48,5]{2,1,0:T(8,128)S(1)} copy(s32[1,48,5]{1,0,2:T(1,128)} %param.14) | data formatting | bytes 1920 | tf_op args[3]
  8.4 0.8 %copy.15 = s32[1,48,5]{2,1,0:T(8,128)S(1)} copy(s32[1,48,5]{1,0,2:T(1,128)} %param.15) | data formatting | bytes 1920 | tf_op args[4]
  9.2 1.4 %copy-done = bf16[1,1,48,64,256]{4,3,2,1,0:T(8,128)(2,1)S(1)} copy-done((bf16[1,1,48,64,256]{4,3,2,1,0:T(8,128)(2,1)S(1)}, bf16[1,1,48,64,256]{4,3,2,1,0:T(8,128)(2,1)}, u32[]{:S(2)}) %copy-start) | copy-done | bytes 1572888
  10.6 1.0 %copy-done.2 = bf16[4,256,256]{2,1,0:T(8,128)(2,1)S(1)} copy-done((bf16[4,256,256]{2,1,0:T(8,128)(2,1)S(1)}, bf16[4,256,256]{2,1,0:T(8,128)(2,1)}, u32[]{:S(2)}) %copy-start.2) | copy-done | bytes 524312
  11.6 0.9 %copy-done.5 = bf16[5,64,64]{2,1,0:T(8,128)(2,1)S(1)} copy-done((bf16[5,64,64]{2,1,0:T(8,128)(2,1)S(1)}, bf16[5,64,64]{2,1,0:T(8,128)(2,1)}, u32[]{:S(2)}) %copy-start.5) | copy-done | bytes 40984
  12.5 0.7 %copy-done.7 = s32[1,192]{1,0:T(1,128)S(1)} copy-done((s32[1,192]{1,0:T(1,128)S(1)}, s32[1,192]{1,0:T(1,128)}, u32[]{:S(2)}) %copy-start.7) | copy-done | bytes 792
  13.2 0.7 %copy-done.9 = s32[1,48]{1,0:T(1,128)S(1)} copy-done((s32[1,48]{1,0:T(1,128)S(1)}, s32[1,48]{1,0:T(1,128)}, u32[]{:S(2)}) %copy-start.9) | copy-done | bytes 216
  13.8 9.0 %inner.1 = (bf16[48,64,256]{2,1,0:T(8,128)(2,1)}, f32[8,64,128]{2,1,0:T(8,128)S(1)}) custom-call(s32[48,5]{1,0:T(8,128)S(1)} %bitcast.15, s32[48,5]{1,0:T(8,128)S(1)} %bitcast.17, s32[1,48]{1,0:T(1,128)S(1)} %copy-done.9, s32[1,192]{1,0:T(1,128)S(1)} %copy-done.7, bf16[48,64,256]{2,1,0:T(8,128)(2,1)S(1)} %bitcast.12, bf16[4,256,256]{2,1,0:T(8,128)(2,1)S(1)} %copy-done.2, ...), custom_call_target="tpu_custom_call" | custom-call | flops 4000000000 | bytes 4000000 | tf_op jit(solution)/shard_map/inner/pallas_call | solution.py:297
  22.9 3.1 %rim.1 = (bf16[48,64,256]{2,1,0:T(8,128)(2,1)}, bf16[96,128]{1,0:T(8,128)(2,1)S(1)}, bf16[96,128]{1,0:T(8,128)(2,1)S(1)}, bf16[96,128]{1,0:T(8,128)(2,1)S(1)}, bf16[96,128]{1,0:T(8,128)(2,1)S(1)}) custom-call(s32[48,5]{1,0:T(8,128)S(1)} %bitcast.16, s32[48,5]{1,0:T(8,128)S(1)} %bitcast.18, s32[1,48]{1,0:T(1,128)S(1)} %copy-done.9, ...), custom_call_target="tpu_custom_call", output_to_operand_aliasing={{0}: (12, {})} | custom-call | tf_op jit(solution)/shard_map/rim/pallas_call | solution.py:321
  26.6 2.5 %collective-permute-start.3 = (bf16[96,128]{1,0:T(8,128)(2,1)S(1)}, bf16[96,128]{1,0:T(8,128)(2,1)S(1)}, u32[]{:S(2)}, u32[]{:S(2)}) collective-permute-start(bf16[96,128]{1,0:T(8,128)(2,1)S(1)} %get-tuple-element.17), channel_id=1, source_target_pairs={{0,8},{4,12},{8,0},{12,4},{1,9},{5,13},{9,1},{13,5},{2,10},{6,14},... | collective-permute-start | bytes 73736 | tf_op jit(solution)/shard_map/ppermute | solution.py:33
  29.1 1.3 %collective-permute-start.4 = (bf16[96,128]{1,0:T(8,128)(2,1)S(1)}, bf16[96,128]{1,0:T(8,128)(2,1)S(1)}, u32[]{:S(2)}, u32[]{:S(2)}) collective-permute-start(bf16[96,128]{1,0:T(8,128)(2,1)S(1)} %get-tuple-element.18), channel_id=1, source_target_pairs={{0,12},{4,0},{8,4},{12,8},{1,13},{5,1},{9,5},{13,9},{2,14},{6,2},{... | collective-permute-start | bytes 73736 | tf_op jit(solution)/shard_map/ppermute | solution.py:33
  30.4 1.8 %slots.1.slots_ref = s32[49]{0:T(128)} custom-call(s32[1,192]{1,0:T(1,128)} %route_ref.5, bf16[96,128]{1,0:T(8,128)(2,1)} %copy-done.3), custom_call_target="tpu_custom_call" | custom-call | tf_op jit(solution)/shard_map/slots/pallas_call | solution.py:351
  32.9 0.7 %copy-done.4 = bf16[96,128]{1,0:T(8,128)(2,1)S(1)} copy-done((bf16[96,128]{1,0:T(8,128)(2,1)S(1)}, bf16[96,128]{1,0:T(8,128)(2,1)}, u32[]{:S(2)}) %copy-start.4) | copy-done | bytes 24600
  33.7 0.6 %copy-done.8 = s32[49]{0:T(128)S(1)} copy-done((s32[49]{0:T(128)S(1)}, s32[49]{0:T(128)}, u32[]{:S(2)}) %copy-start.8) | copy-done | bytes 220
  34.3 1.5 %merge.1 = (bf16[3,64,256]{2,1,0:T(8,128)(2,1)S(1)}, bf16[64,256]{1,0:T(8,128)(2,1)S(1)}, bf16[64,256]{1,0:T(8,128)(2,1)S(1)}) custom-call(s32[49]{0:T(128)S(1)} %copy-done.8, bf16[96,128]{1,0:T(8,128)(2,1)S(1)} %copy-done.4, bf16[96,128]{1,0:T(8,128)(2,1)S(1)} %collective-permute-done.2.refs_1_, bf16[96,128]{1,0:T(8,128)(2,1)S(1)} %collective-permute-done.3.refs_2_, ...), custom_call_target="tpu_custom_call" | custom-call | tf_op jit(solution)/shard_map/merge/pallas_call | solution.py:361
  35.8 1.6 %collective-permute-start.7 = (bf16[3,64,256]{2,1,0:T(8,128)(2,1)S(1)}, bf16[3,64,256]{2,1,0:T(8,128)(2,1)S(1)}, u32[]{:S(2)}, u32[]{:S(2)}) collective-permute-start(bf16[3,64,256]{2,1,0:T(8,128)(2,1)S(1)} %get-tuple-element.19.coarse_ref), channel_id=1, source_target_pairs={{0,2},{2,0},{1,3},{3,1},{4,6},{6,4},{5,7},{7,5},{8,10},{10,8},{9,1... | collective-permute-start | bytes 294920 | tf_op jit(solution)/shard_map/ppermute | solution.py:33
  37.3 2.0 %collective-permute-start.5 = (bf16[64,256]{1,0:T(8,128)(2,1)S(1)}, bf16[64,256]{1,0:T(8,128)(2,1)S(1)}, u32[]{:S(2)}, u32[]{:S(2)}) collective-permute-start(bf16[64,256]{1,0:T(8,128)(2,1)S(1)} %get-tuple-element.20), channel_id=1, source_target_pairs={{0,4},{4,8},{8,12},{12,0},{1,5},{5,9},{9,13},{13,1},{2,6},{6,10},{... | collective-permute-start | bytes 98312 | tf_op jit(solution)/shard_map/ppermute | solution.py:33
  39.4 1.8 %collective-permute-start.6 = (bf16[64,256]{1,0:T(8,128)(2,1)S(1)}, bf16[64,256]{1,0:T(8,128)(2,1)S(1)}, u32[]{:S(2)}, u32[]{:S(2)}) collective-permute-start(bf16[64,256]{1,0:T(8,128)(2,1)S(1)} %get-tuple-element.21), channel_id=1, source_target_pairs={{0,12},{4,0},{8,4},{12,8},{1,13},{5,1},{9,5},{13,9},{2,14},{6,2},{... | collective-permute-start | bytes 98312 | tf_op jit(solution)/shard_map/ppermute | solution.py:33
  41.2 2.0 %collective-permute-done.5.left_ref = bf16[64,256]{1,0:T(8,128)(2,1)S(1)} collective-permute-done((bf16[64,256]{1,0:T(8,128)(2,1)S(1)}, bf16[64,256]{1,0:T(8,128)(2,1)S(1)}, u32[]{:S(2)}, u32[]{:S(2)}) %collective-permute-start.5) | collective-permute-done | bytes 32800 | tf_op jit(solution)/shard_map/ppermute | solution.py:33
  43.4 1.9 %coarse.1 = bf16[3,64,256]{2,1,0:T(8,128)(2,1)} custom-call(s32[3,3]{1,0:T(4,128)S(1)} %bitcast.19, bf16[3,64,256]{2,1,0:T(8,128)(2,1)S(1)} %get-tuple-element.19.coarse_ref, bf16[64,256]{1,0:T(8,128)(2,1)S(1)} %collective-permute-done.5.left_ref, bf16[64,256]{1,0:T(8,128)(2,1)S(1)} %collective-permute-done.6.right_ref, ...), custom_call_target="tpu_custom_call" | custom-call | tf_op jit(solution)/shard_map/coarse/pallas_call | solution.py:374
  (24 shorter events, 1.5 us)
Async XLA Ops:
  1.5 21.3 %collective-permute-start = (bf16[2,64,256]{2,1,0:T(8,128)(2,1)S(1)}, bf16[2,64,256]{2,1,0:T(8,128)(2,1)S(1)}, u32[]{:S(2)}, u32[]{:S(2)}) collective-permute-start(bf16[2,64,256]{2,1,0:T(8,128)(2,1)S(1)} %get-tuple-element.23), channel_id=1, source_target_pairs={{0,4},{4,8},{8,12},{12,0},{1,5},{5,9},{9,13},{13,1},{2,6},{6,10},{... | collective-permute-start | bytes 196616 | tf_op jit(solution)/shard_map/ppermute | solution.py:33
  4.6 18.3 %collective-permute-start.1 = (bf16[2,64,256]{2,1,0:T(8,128)(2,1)S(1)}, bf16[2,64,256]{2,1,0:T(8,128)(2,1)S(1)}, u32[]{:S(2)}, u32[]{:S(2)}) collective-permute-start(bf16[2,64,256]{2,1,0:T(8,128)(2,1)S(1)} %get-tuple-element.22), channel_id=1, source_target_pairs={{0,12},{4,0},{8,4},{12,8},{1,13},{5,1},{9,5},{13,9},{2,14},{6,2},{... | collective-permute-start | bytes 196616 | tf_op jit(solution)/shard_map/ppermute | solution.py:33
  9.2 1.4 %copy-start = (bf16[1,1,48,64,256]{4,3,2,1,0:T(8,128)(2,1)S(1)}, bf16[1,1,48,64,256]{4,3,2,1,0:T(8,128)(2,1)}, u32[]{:S(2)}) copy-start(bf16[1,1,48,64,256]{4,3,2,1,0:T(8,128)(2,1)} %param.11) | copy-start | bytes 4718596
  10.6 1.0 %copy-start.2 = (bf16[4,256,256]{2,1,0:T(8,128)(2,1)S(1)}, bf16[4,256,256]{2,1,0:T(8,128)(2,1)}, u32[]{:S(2)}) copy-start(bf16[4,256,256]{2,1,0:T(8,128)(2,1)} %spatial_ref.4) | copy-start | bytes 1572868
  11.6 0.9 %copy-start.5 = (bf16[5,64,64]{2,1,0:T(8,128)(2,1)S(1)}, bf16[5,64,64]{2,1,0:T(8,128)(2,1)}, u32[]{:S(2)}) copy-start(bf16[5,64,64]{2,1,0:T(8,128)(2,1)} %mix_ref.4) | copy-start | bytes 122884
  12.5 0.7 %copy-start.7 = (s32[1,192]{1,0:T(1,128)S(1)}, s32[1,192]{1,0:T(1,128)}, u32[]{:S(2)}) copy-start(s32[1,192]{1,0:T(1,128)} %route_ref.5) | copy-start | bytes 2308
  13.2 0.7 %copy-start.9 = (s32[1,48]{1,0:T(1,128)S(1)}, s32[1,48]{1,0:T(1,128)}, u32[]{:S(2)}) copy-start(s32[1,48]{1,0:T(1,128)} %rcode_ref.3) | copy-start | bytes 580
  22.9 18.3 %copy-start.10 = (s32[1,3,3]{2,0,1:T(1,128)S(1)}, s32[1,3,3]{2,0,1:T(1,128)}, u32[]{:S(2)}) copy-start(s32[1,3,3]{2,0,1:T(1,128)} %param.21) | copy-start | bytes 112
  22.9 20.6 %copy-start.1 = (bf16[4,256,256]{2,1,0:T(8,128)(2,1)S(1)}, bf16[4,256,256]{2,1,0:T(8,128)(2,1)}, u32[]{:S(2)}) copy-start(bf16[4,256,256]{2,1,0:T(8,128)(2,1)} %spatial_ref.5) | copy-start | bytes 1572868
  22.9 20.5 %copy-start.6 = (bf16[4,64,64]{2,1,0:T(8,128)(2,1)S(1)}, bf16[4,64,64]{2,1,0:T(8,128)(2,1)}, u32[]{:S(2)}) copy-start(bf16[4,64,64]{2,1,0:T(8,128)(2,1)} %mix_ref.5) | copy-start | bytes 98308
  26.0 0.6 %copy-start.3 = (bf16[96,128]{1,0:T(8,128)(2,1)}, bf16[96,128]{1,0:T(8,128)(2,1)S(1)}, u32[]{:S(2)}) copy-start(bf16[96,128]{1,0:T(8,128)(2,1)S(1)} %get-tuple-element.15.late_ref.refs_0_) | copy-start | bytes 73732
  26.6 5.7 %collective-permute-start.2 = (bf16[96,128]{1,0:T(8,128)(2,1)S(1)}, bf16[96,128]{1,0:T(8,128)(2,1)S(1)}, u32[]{:S(2)}, u32[]{:S(2)}) collective-permute-start(bf16[96,128]{1,0:T(8,128)(2,1)S(1)} %get-tuple-element.16), channel_id=1, source_target_pairs={{0,4},{4,8},{8,12},{12,0},{1,5},{5,9},{9,13},{13,1},{2,6},{6,10},{... | collective-permute-start | bytes 73736 | tf_op jit(solution)/shard_map/ppermute | solution.py:33
  26.6 5.7 %collective-permute-start.3 = (bf16[96,128]{1,0:T(8,128)(2,1)S(1)}, bf16[96,128]{1,0:T(8,128)(2,1)S(1)}, u32[]{:S(2)}, u32[]{:S(2)}) collective-permute-start(bf16[96,128]{1,0:T(8,128)(2,1)S(1)} %get-tuple-element.17), channel_id=1, source_target_pairs={{0,8},{4,12},{8,0},{12,4},{1,9},{5,13},{9,1},{13,5},{2,10},{6,14},... | collective-permute-start | bytes 73736 | tf_op jit(solution)/shard_map/ppermute | solution.py:33
  29.1 3.8 %collective-permute-start.4 = (bf16[96,128]{1,0:T(8,128)(2,1)S(1)}, bf16[96,128]{1,0:T(8,128)(2,1)S(1)}, u32[]{:S(2)}, u32[]{:S(2)}) collective-permute-start(bf16[96,128]{1,0:T(8,128)(2,1)S(1)} %get-tuple-element.18), channel_id=1, source_target_pairs={{0,12},{4,0},{8,4},{12,8},{1,13},{5,1},{9,5},{13,9},{2,14},{6,2},{... | collective-permute-start | bytes 73736 | tf_op jit(solution)/shard_map/ppermute | solution.py:33
  32.9 0.7 %copy-start.4 = (bf16[96,128]{1,0:T(8,128)(2,1)S(1)}, bf16[96,128]{1,0:T(8,128)(2,1)}, u32[]{:S(2)}) copy-start(bf16[96,128]{1,0:T(8,128)(2,1)} %copy-done.3) | copy-start | bytes 73732
  33.7 0.6 %copy-start.8 = (s32[49]{0:T(128)S(1)}, s32[49]{0:T(128)}, u32[]{:S(2)}) copy-start(s32[49]{0:T(128)} %slots.1.slots_ref) | copy-start | bytes 592
  35.8 7.6 %collective-permute-start.7 = (bf16[3,64,256]{2,1,0:T(8,128)(2,1)S(1)}, bf16[3,64,256]{2,1,0:T(8,128)(2,1)S(1)}, u32[]{:S(2)}, u32[]{:S(2)}) collective-permute-start(bf16[3,64,256]{2,1,0:T(8,128)(2,1)S(1)} %get-tuple-element.19.coarse_ref), channel_id=1, source_target_pairs={{0,2},{2,0},{1,3},{3,1},{4,6},{6,4},{5,7},{7,5},{8,10},{10,8},{9,1... | collective-permute-start | bytes 294920 | tf_op jit(solution)/shard_map/ppermute | solution.py:33
  37.3 5.8 %collective-permute-start.5 = (bf16[64,256]{1,0:T(8,128)(2,1)S(1)}, bf16[64,256]{1,0:T(8,128)(2,1)S(1)}, u32[]{:S(2)}, u32[]{:S(2)}) collective-permute-start(bf16[64,256]{1,0:T(8,128)(2,1)S(1)} %get-tuple-element.20), channel_id=1, source_target_pairs={{0,4},{4,8},{8,12},{12,0},{1,5},{5,9},{9,13},{13,1},{2,6},{6,10},{... | collective-permute-start | bytes 98312 | tf_op jit(solution)/shard_map/ppermute | solution.py:33
  39.4 4.1 %collective-permute-start.6 = (bf16[64,256]{1,0:T(8,128)(2,1)S(1)}, bf16[64,256]{1,0:T(8,128)(2,1)S(1)}, u32[]{:S(2)}, u32[]{:S(2)}) collective-permute-start(bf16[64,256]{1,0:T(8,128)(2,1)S(1)} %get-tuple-element.21), channel_id=1, source_target_pairs={{0,12},{4,0},{8,4},{12,8},{1,13},{5,1},{9,5},{13,9},{2,14},{6,2},{... | collective-permute-start | bytes 98312 | tf_op jit(solution)/shard_map/ppermute | solution.py:33

commit v2 on v0

v2 whole, which is shorter than its diff:
```python
import functools

import jax
import jax.numpy as jnp
from jax import lax
from jax.experimental import pallas as pl
from jax.experimental.pallas import tpu as pltpu
from jax.sharding import PartitionSpec as P

LANES = 128
RIM = 2
CHUNK = 8
VMEM_MIB = 40

SMEM = functools.partial(pl.BlockSpec, memory_space=pltpu.SMEM)
VMEM = functools.partial(pl.BlockSpec, memory_space=pltpu.VMEM)
ANY = functools.partial(pl.BlockSpec, memory_space=pl.ANY)
F32 = jnp.float32
BF16 = jnp.bfloat16


def dot(a, b):
    return jnp.dot(a, b, preferred_element_type=F32)


def silu(v):
    return v * (0.5 + 0.5 * jnp.tanh(0.5 * v))


def shifted(value, axis, steps):
    count = lax.axis_size(axis)
    return lax.ppermute(value, axis, [(i, (i + steps) % count) for i in range(count)])


def joined_mix(mix_ref, terms):
    return jnp.concatenate([mix_ref[t] for t in range(terms)], axis=1)


def dot_t(a, b):
    return lax.dot_general(a, b, (((1,), (1,)), ((), ())), preferred_element_type=F32)


def swapped(even, value, axis):
    count = lax.axis_size(axis)
    first = 0 if even else 1
    pairs = []
    for i in range(first, count + first, 2):
        here, there = i % count, (i + 1) % count
        pairs += [(here, there), (there, here)]
    return lax.ppermute(value, axis, pairs)


def faces_right():
    return lax.rem(lax.axis_index("tile"), 2) == 0


def mixed_skip(y_ref, y_index, taps, mix_wide, mix_ref, own):
    terms = [y_ref[y_index(t)] for t in range(taps)]
    wide = mix_wide.shape[1] // mix_ref.shape[1]
    mixed = dot(mix_wide, jnp.concatenate(terms[:wide], axis=0))
    for t in range(wide, taps):
        mixed = mixed + dot(mix_ref[t], terms[t])
    return (own.astype(F32) + silu(mixed)).astype(BF16)


def place(acc_ref, at, product, code, rank, cq):
    per = LANES // cq
    slot = lax.rem(rank, per)
    amount = lax.rem((slot - code) * cq + LANES, LANES)
    turned = pltpu.roll(product, amount, axis=1)
    lane = lax.broadcasted_iota(jnp.int32, turned.shape, 1)
    at = at + lax.div(rank, per)
    acc_ref[at] = jnp.where(lax.div(lane, cq) == slot, turned, acc_ref[at])


class Packing:
    def __init__(self, per, cq, channels):
        self.cq, self.channels = cq, channels
        self.lanes = LANES // cq
        self.full, left = divmod(per, self.lanes)
        self.half = 0 < left * 2 <= self.lanes
        if left and not self.half:
            self.full += 1
        self.parts = self.full + self.half
        self.rows = self.full * channels + (channels // 2 if self.half else 0)

    def width(self, tiles):
        return (tiles * self.full + (-(-tiles // 2) if self.half else 0)) * LANES

    def column(self, tiles, hop, rank):
        whole = (hop * self.full * self.lanes + rank) * self.cq
        if not self.half:
            return whole
        split = (
            (tiles * self.full + hop // 2) * LANES
            + hop % 2 * (LANES // 2)
            + (rank - self.full * self.lanes) * self.cq
        )
        return jnp.where(rank < self.full * self.lanes, whole, split)


def cut_kernel(x_ref, first_ref, second_ref, sems):
    count = x_ref.shape[0]
    right = faces_right()
    last = count - RIM
    copies = [
        pltpu.make_async_copy(x_ref.at[pl.ds(jnp.where(right, last, 0), RIM)], first_ref, sems.at[0]),
        pltpu.make_async_copy(x_ref.at[pl.ds(jnp.where(right, 0, last), RIM)], second_ref, sems.at[1]),
    ]
    for copy in copies:
        copy.start()
    for copy in copies:
        copy.wait()


def products_kernel(x_ref, spatial_ref, y_ref, rows_ref, table_ref, x_sems, table_sems):
    count, channels, cells = x_ref.shape
    rotations = spatial_ref.shape[0]
    extended = count + 2 * RIM
    steps = count // CHUNK
    tables = [
        pltpu.make_async_copy(spatial_ref.at[r], table_ref.at[r], table_sems.at[r]) for r in range(rotations)
    ]

    def fetch(step):
        part = pl.ds(step * CHUNK, CHUNK)
        return pltpu.make_async_copy(x_ref.at[part], rows_ref.at[part], x_sems.at[step])

    fetch(0).start()
    for table in tables:
        table.start()
    for step in range(1, steps):
        fetch(step).start()
    for table in tables:
        table.wait()

    @pl.loop(0, steps)
    def _(step):
        fetch(step).wait()
        rows = rows_ref[pl.ds(step * CHUNK, CHUNK)].reshape(CHUNK * channels, cells)
        for r in range(rotations):
            product = dot(rows, table_ref[r]).astype(BF16)
            y_ref[pl.ds(r * extended + RIM + step * CHUNK, CHUNK)] = product.reshape(CHUNK, channels, cells)


def fine_kernel(
    nbr_in, code_in, rcode_in, route_in, first_ref, second_ref, x_ref, spatial_ref, mix_ref, restrict_ref, y_in_ref,
    skip_ref, y_ref, *refs,
):
    sent_refs, refs = refs[:-14], refs[-14:]
    nbr_ref, code_ref, rcode_ref, route_ref, table_sems = refs[:5]
    acc_ref, x_own, table_ref, mix_own, restrict_own, done_ref, counts_ref, in_sems, out_sems = refs[5:]
    del y_in_ref
    count, channels, cells = x_ref.shape
    rotations, cq = restrict_ref.shape[:2]
    taps = mix_ref.shape[0]
    blocks = route_ref.shape[1]
    tiles = blocks // count
    extended = count + 2 * RIM
    parts = acc_ref.shape[0] // tiles
    packing = Packing(count // tiles, cq, channels)
    me = lax.axis_index("tile")
    fetches = [
        pltpu.make_async_copy(spatial_ref, table_ref, in_sems.at[0]),
        pltpu.make_async_copy(mix_ref, mix_own, in_sems.at[1]),
        pltpu.make_async_copy(restrict_ref, restrict_own, in_sems.at[2]),
        pltpu.make_async_copy(x_ref, x_own, in_sems.at[3]),
    ]
    tables = [
        pltpu.make_async_copy(source, target, table_sems.at[i])
        for i, (source, target) in enumerate(
            [(nbr_in, nbr_ref), (code_in, code_ref), (rcode_in, rcode_ref), (route_in, route_ref)]
        )
    ]
    for fetch in fetches + tables:
        fetch.start()
    acc_ref[...] = jnp.zeros(acc_ref.shape, F32)
    for d in range(tiles):
        counts_ref[d] = 0
    right = faces_right()
    received = [first_ref[...], second_ref[...]]
    before = jnp.where(right, received[1], received[0])
    after = jnp.where(right, received[0], received[1])
    halo = jnp.concatenate([before, after], axis=0).reshape(2 * RIM * channels, cells)
    fetches[0].wait()
    for r in range(rotations):
        product = dot(halo, table_ref[r]).astype(BF16).reshape(2 * RIM, channels, cells)
        y_ref[r * extended:r * extended + RIM] = product[:RIM]
        y_ref[r * extended + RIM + count:(r + 1) * extended] = product[RIM:]
    for fetch in fetches[1:] + tables:
        fetch.wait()
    mix_wide = joined_mix(mix_own, min(taps, cells // channels))
    restricts = restrict_own[...].reshape(rotations * cq, cells)
    stacked = jnp.concatenate([restricts] * (LANES // (rotations * cq)), axis=0)

    def put(step):
        part = pl.ds(step * CHUNK, CHUNK)
        return pltpu.make_async_copy(done_ref.at[part], skip_ref.at[part], out_sems.at[step])

    @pl.loop(0, count // CHUNK)
    def _(step):
        base = step * CHUNK
        for i in range(CHUNK):
            b = base + i

            def y_index(t):
                local = nbr_ref[t, 0, b] - me * count + RIM
                local = jnp.where(local < 0, local + blocks, local)
                local = jnp.where(local >= blocks, local - blocks, local)
                return code_ref[t, 0, b] * extended + local

            done_ref[b] = mixed_skip(y_ref, y_index, taps, mix_wide, mix_own, x_own[b])
        put(step).start()
        rows = done_ref[pl.ds(base, CHUNK)].reshape(CHUNK * channels, cells)
        products = dot_t(rows, stacked)
        for i in range(CHUNK):
            b = base + i
            dest = lax.div(route_ref[0, me * count + b], count)
            rank = counts_ref[dest]
            counts_ref[dest] = rank + 1
            hop = lax.rem(dest - me + tiles, tiles)
            place(
                acc_ref, hop * parts, products[i * channels:(i + 1) * channels],
                rcode_ref[0, b], rank, cq,
            )

    half = LANES // 2
    lane = lax.broadcasted_iota(jnp.int32, (channels // 2, LANES), 1)
    for hop in range(tiles):
        out = sent_refs[hop]
        for p in range(packing.full):
            out[p * channels:(p + 1) * channels] = acc_ref[hop * parts + p].astype(BF16)
        if packing.half:
            value = acc_ref[hop * parts + packing.full]
            lower = pltpu.roll(value[channels // 2:], half, axis=1)
            joined = jnp.where(lane < half, value[:channels // 2], lower)
            out[packing.full * channels:] = joined.astype(BF16)

    @pl.loop(0, count // CHUNK)
    def _(step):
        put(step).wait()


def order_kernel(count, cq, channels, route_ref, late_ref, order_ref):
    del late_ref
    blocks = route_ref.shape[1]
    tiles = blocks // count
    packing = Packing(count // tiles, cq, channels)
    me = lax.axis_index("tile")
    base = me * count
    route = route_ref[...]
    mine = jnp.where((route >= base) & (route < base + count), 1.0, 0.0)
    shape = (blocks, blocks)
    of, at = (lax.broadcasted_iota(jnp.int32, shape, d) for d in (0, 1))
    earlier = jnp.where((of < at) & (lax.div(of, count) == lax.div(at, count)), 1.0, 0.0)
    rank = dot(jnp.broadcast_to(mine, (8, blocks)).astype(BF16), earlier.astype(BF16))[:1].astype(jnp.int32)
    source = lax.div(lax.broadcasted_iota(jnp.int32, (1, blocks), 1), count)
    hop = lax.rem(me - source + tiles, tiles)
    column = packing.column(tiles, hop, rank).astype(F32)
    cells = count * cq
    cell = lax.broadcasted_iota(jnp.int32, (cells, blocks), 0)
    found = jnp.where(route == base + lax.div(cell, cq), column, 0.0)
    wanted = jnp.sum(found, axis=1, keepdims=True)
    wanted = wanted + lax.rem(lax.broadcasted_iota(jnp.int32, (cells, 1), 0), cq).astype(F32)
    across = jnp.transpose(jnp.broadcast_to(wanted, (cells, LANES)))[:1].astype(jnp.int32)
    step = LANES
    for row in range(0, order_ref.shape[0], step):
        index = row + lax.broadcasted_iota(jnp.int32, (step, cells), 0)
        order_ref[row:row + step] = jnp.where(index == across, 1.0, 0.0).astype(BF16)


def merge_kernel(per, cq, order_ref, *refs):
    arrived, (coarse_ref, first_ref, second_ref) = refs[:-3], refs[-3:]
    blocks, channels, cells = coarse_ref.shape
    tiles = len(arrived)
    packing = Packing(per, cq, channels)
    columns = [ref[p * channels:(p + 1) * channels] for ref in arrived for p in range(packing.full)]
    if packing.half:
        half = LANES // 2
        lane = lax.broadcasted_iota(jnp.int32, (channels // 2, LANES), 1)
        halves = [ref[packing.full * channels:].astype(F32) for ref in arrived]
        halves += [jnp.zeros_like(halves[0])] * (tiles % 2)
        for one, other in zip(halves[::2], halves[1::2]):
            upper = jnp.where(lane < half, one, pltpu.roll(other, half, axis=1))
            lower = jnp.where(lane < half, pltpu.roll(one, half, axis=1), other)
            columns.append(jnp.concatenate([upper, lower], axis=0).astype(BF16))
    joined = jnp.concatenate(columns, axis=1)
    values = [
        dot(joined, order_ref[:, c * cells:(c + 1) * cells]).astype(BF16) for c in range(blocks)
    ]
    for c in range(blocks):
        coarse_ref[c] = values[c]
    right = faces_right()
    first_ref[...] = jnp.where(right, values[-1], values[0])
    second_ref[...] = jnp.where(right, values[0], values[-1])


def coarse_kernel(code_ref, coarse_ref, first_ref, second_ref, seam_ref, spatial_ref, mix_ref, out_ref):
    blocks = coarse_ref.shape[0]
    right = faces_right()
    left_rows = jnp.where(right, second_ref[...], first_ref[...])
    right_rows = jnp.where(right, first_ref[...], second_ref[...])
    mix_wide = joined_mix(mix_ref, mix_ref.shape[0])
    for c in range(blocks):
        own = coarse_ref[c]
        beside = [
            left_rows if c == 0 else coarse_ref[c - 1],
            right_rows if c == blocks - 1 else coarse_ref[c + 1],
            seam_ref[c],
        ]
        edges = [dot(rows, spatial_ref[code_ref[c, 0, e]]).astype(BF16) for e, rows in enumerate(beside)]
        total = dot(mix_wide, jnp.concatenate([own] + edges, axis=0))
        out_ref[c] = (own.astype(F32) + silu(total)).astype(BF16)


def params(mib=VMEM_MIB):
    return pltpu.CompilerParams(vmem_limit_bytes=mib * 1024 * 1024)


def per_device(
    fine, conv_spatial, conv_mix, neighbours, fine_codes, restrict, restrict_codes, route,
    coarse_spatial, coarse_mix, coarse_codes,
):
    x = fine[0, 0]
    count, channels, cells = x.shape
    rotations = conv_spatial.shape[0]
    cq = restrict.shape[2]
    tiles = route.shape[1] // count
    per = count // tiles
    blocks = count * cq // cells
    packing = Packing(per, cq, channels)
    nbr, codes = neighbours.transpose(2, 0, 1), fine_codes.transpose(2, 0, 1)
    narrow = restrict.transpose(0, 2, 1)

    rim_shape = jax.ShapeDtypeStruct((RIM, channels, cells), BF16)
    first, second = pl.pallas_call(
        cut_kernel,
        out_shape=(rim_shape, rim_shape),
        in_specs=[ANY()],
        out_specs=(VMEM(), VMEM()),
        scratch_shapes=[pltpu.SemaphoreType.DMA((2,))],
        name="cut",
    )(x)
    first = swapped(True, first, "tile")
    second = swapped(False, second, "tile")

    y_shape = (rotations * (count + 2 * RIM), channels, cells)
    steps = count // CHUNK
    y = pl.pallas_call(
        products_kernel,
        out_shape=jax.ShapeDtypeStruct(y_shape, BF16),
        in_specs=[ANY(), ANY()],
        out_specs=VMEM(),
        scratch_shapes=[
            pltpu.VMEM(x.shape, BF16),
            pltpu.VMEM(conv_spatial.shape, BF16),
            pltpu.SemaphoreType.DMA((steps,)),
            pltpu.SemaphoreType.DMA((rotations,)),
        ],
        compiler_params=params(),
        cost_estimate=pl.CostEstimate(flops=4 * 10**9, bytes_accessed=4 * 10**6, transcendentals=10**6),
        name="products",
    )(x, conv_spatial)

    sent_shape = jax.ShapeDtypeStruct((packing.rows, LANES), BF16)
    skip, _, *sent = pl.pallas_call(
        fine_kernel,
        out_shape=(jax.ShapeDtypeStruct(x.shape, BF16), jax.ShapeDtypeStruct(y_shape, BF16)) + (sent_shape,) * tiles,
        in_specs=[ANY()] * 4 + [VMEM()] * 2 + [ANY()] * 4 + [VMEM()],
        out_specs=(ANY(), VMEM()) + (VMEM(),) * tiles,
        scratch_shapes=[pltpu.SMEM(a.shape, jnp.int32) for a in (nbr, codes, restrict_codes, route)]
        + [
            pltpu.SemaphoreType.DMA((4,)),
            pltpu.VMEM((tiles * packing.parts, channels, LANES), F32),
            pltpu.VMEM(x.shape, BF16),
            pltpu.VMEM(conv_spatial.shape, BF16),
            pltpu.VMEM(conv_mix.shape, BF16),
            pltpu.VMEM(narrow.shape, BF16),
            pltpu.VMEM(x.shape, BF16),
            pltpu.SMEM((tiles,), jnp.int32),
            pltpu.SemaphoreType.DMA((4,)),
            pltpu.SemaphoreType.DMA((steps,)),
        ],
        input_output_aliases={10: 1},
        compiler_params=params(),
        name="fine",
    )(nbr, codes, restrict_codes, route, first, second, x, conv_spatial, conv_mix, narrow, y)

    order = pl.pallas_call(
        functools.partial(order_kernel, count, cq, channels),
        out_shape=jax.ShapeDtypeStruct((packing.width(tiles), count * cq), BF16),
        in_specs=[VMEM(), VMEM()],
        out_specs=VMEM(),
        compiler_params=params(),
        name="order",
    )(route, sent[0])
    arrived = [sent[0]] + [shifted(sent[hop], "tile", hop) for hop in range(1, tiles)]

    block_shape = jax.ShapeDtypeStruct((channels, cells), BF16)
    coarse, first, second = pl.pallas_call(
        functools.partial(merge_kernel, per, cq),
        out_shape=(jax.ShapeDtypeStruct((blocks, channels, cells), BF16), block_shape, block_shape),
        in_specs=[VMEM()] * (1 + tiles),
        out_specs=(VMEM(), VMEM(), VMEM()),
        compiler_params=params(),
        name="merge",
    )(order, *arrived)

    first = swapped(True, first, "tile")
    second = swapped(False, second, "tile")
    seam = shifted(coarse, "sect", 1)
    coarse_out = pl.pallas_call(
        coarse_kernel,
        out_shape=jax.ShapeDtypeStruct(coarse.shape, BF16),
        in_specs=[SMEM()] + [VMEM()] * 6,
        out_specs=VMEM(),
        compiler_params=params(),
        name="coarse",
    )(coarse_codes.transpose(1, 0, 2), coarse, first, second, seam, coarse_spatial, coarse_mix)
    return (skip[None, None], coarse_out[None, None])


def solution(mesh):
    data = P(("groups", "chan"), "sect", "tile", None, None)
    placed = (
        data,
        P(),
        P(),
        P("sect", "tile", None),
        P("sect", "tile", None),
        P(),
        P("sect", "tile"),
        P("sect", None),
        P(),
        P(),
        P("sect", "tile", None),
    )
    return jax.shard_map(
        per_device, mesh=mesh, in_specs=placed, out_specs=(data, data), check_vma=False
    )
```

time: 112 us -> 36.2 us (0.32)
  matrix products: 67.5 us -> 0 us
  blocking collectives: 14.9 us -> 0 us
  Pallas kernels: 0 us -> 13.6 us
  other arithmetic: 8.5 us -> 0 us
  local copies, waits for them, and re-layouts: 7.19 us -> 1.09 us
  starting transfers between devices: 9.18 us -> 14.2 us
  waiting for transfers between devices: 3.54 us -> 6.34 us
    dot_general x35 -> x0, matrix products: 67.5 us -> none  [the longest x24 34 us: rotated_product(): jnp.einsum(form, rows, spatial_table[rotation], preferred_element_type=jn...]
    all_gather x1 -> x0, blocking collectives: 14.9 us -> none  [per_device(): gathered = lax.all_gather(flat_piece, 'tile', axis=0, tiled=True)]
    pallas_call x0 -> x6, Pallas kernels: none -> 13.6 us  [the longest x1 5.59 us: per_device(): pl.pallas_call(fine_kernel, out_shape=(jax.ShapeDtypeStruct(x.shape, BF16...]
    ppermute x5 -> x8, starting transfers between devices: 9.18 us -> 14.2 us  [the longest x4 8.73 us: swapped(): return lax.ppermute(value, axis, pairs)]
    gather x7 -> x0, local copies, waits for them, and re-layouts: 4.59 us -> none  [the longest x5 3.3 us: per_device(): rows = jnp.take(extended, local_rows[:, term_index], axis=0)]
    sort x1 -> x0, other arithmetic: 3.84 us -> none  [per_device(): inverse = jnp.argsort(table)]
    ppermute x5 -> x8, waiting for transfers between devices: 3.54 us -> 6.34 us  [the longest x4 4.48 us: swapped(): return lax.ppermute(value, axis, pairs)]
    eq x3 -> x0, other arithmetic: 2.08 us -> none  [the longest x2 1.34 us: rotated_product(): codes == rotation]
  transfers between devices with their start and end apart: 5 -> 8, of which waited for: 1 -> 5; matrix products, arithmetic and copies ran while one was open for 8% -> 0% of each run, Pallas kernels for 0% -> 11%
where the time goes in v2:
time: 36.2 us; the launch traced here: 36 us
  starting transfers between devices  14.2 us (39%)
  Pallas kernels  13.6 us (38%)
  waiting for transfers between devices  6.34 us (18%)
  local copies, waits for them, and re-layouts  1.09 us (3%)
  between operations  0.8 us (2%)
    ppermute x4, starting transfers between devices, swapped(): return lax.ppermute(value, axis, pairs)  8.73 us
    pallas_call x1, Pallas kernels, per_device(): pl.pallas_call(fine_kernel, out_shape=(jax.ShapeDtypeStruct(x.shape, BF16...  5.59 us
    ppermute x4, starting transfers between devices, shifted(): lax.ppermute(value, axis, [(i, (i + steps) % count) for i in range(count)])  5.44 us
    ppermute x4, waiting for transfers between devices, swapped(): return lax.ppermute(value, axis, pairs)  4.48 us
    pallas_call x1, Pallas kernels, per_device(): pl.pallas_call(products_kernel, out_shape=jax.ShapeDtypeStruct(y_shape, B...  3.53 us
    pallas_call x1, Pallas kernels, per_device(): pl.pallas_call(coarse_kernel, out_shape=jax.ShapeDtypeStruct(coarse.shape...  1.91 us
    ppermute x4, waiting for transfers between devices, shifted(): lax.ppermute(value, axis, [(i, (i + steps) % count) for i in range(count)])  1.86 us
    pallas_call x1, Pallas kernels, per_device(): pl.pallas_call(cut_kernel, out_shape=(rim_shape, rim_shape), in_specs=[AN...  1.67 us
  transfers between devices with their start and end apart: 8, of which 5 were waited for; matrix products, arithmetic and copies ran while one was open for 0% of the time, Pallas kernels for 11%

profile of v2, /device:TPU:0, one launch (start us, length us, event | category | flops | bytes accessed | tf_op | source)
XLA Modules:
  0.0 36.0 jit_solution(794772934079319885)
XLA Ops:
  0.6 1.7 %cut.1 = (bf16[2,64,256]{2,1,0:T(8,128)(2,1)}, bf16[2,64,256]{2,1,0:T(8,128)(2,1)}) custom-call(bf16[48,64,256]{2,1,0:T(8,128)(2,1)} %bitcast.7), custom_call_target="tpu_custom_call" | custom-call | tf_op jit(solution)/shard_map/cut/pallas_call | solution.py:336
  2.3 3.1 %collective-permute-start = (bf16[2,64,256]{2,1,0:T(8,128)(2,1)}, bf16[2,64,256]{2,1,0:T(8,128)(2,1)S(1)}, u32[]{:S(2)}, u32[]{:S(2)}) collective-permute-start(bf16[2,64,256]{2,1,0:T(8,128)(2,1)} %get-tuple-element.12), channel_id=1, source_target_pairs={{0,4},{4,0},{8,12},{12,8},{1,5},{5,1},{9,13},{13,9},{2,6},{6,2},{1... | collective-permute-start | bytes 196616 | tf_op jit(solution)/shard_map/ppermute | solution.py:50
  5.4 2.5 %collective-permute-start.1 = (bf16[2,64,256]{2,1,0:T(8,128)(2,1)}, bf16[2,64,256]{2,1,0:T(8,128)(2,1)S(1)}, u32[]{:S(2)}, u32[]{:S(2)}) collective-permute-start(bf16[2,64,256]{2,1,0:T(8,128)(2,1)} %get-tuple-element.13), channel_id=1, source_target_pairs={{4,8},{8,4},{12,0},{0,12},{5,9},{9,5},{13,1},{1,13},{6,10},{10,6},... | collective-permute-start | bytes 196616 | tf_op jit(solution)/shard_map/ppermute | solution.py:50
  7.9 1.0 %copy-done.1 = bf16[4,256,256]{2,1,0:T(8,128)(2,1)S(1)} copy-done((bf16[4,256,256]{2,1,0:T(8,128)(2,1)S(1)}, bf16[4,256,256]{2,1,0:T(8,128)(2,1)}, u32[]{:S(2)}) %copy-start.1) | copy-done | bytes 524312
  8.9 0.0 copy-start.8
  8.9 0.0 copy-start.10
  9.0 3.5 %products.1.y_in_ref = bf16[208,64,256]{2,1,0:T(8,128)(2,1)S(1)} custom-call(bf16[48,64,256]{2,1,0:T(8,128)(2,1)S(1)} %bitcast.8, bf16[4,256,256]{2,1,0:T(8,128)(2,1)S(1)} %copy-done.1), custom_call_target="tpu_custom_call" | custom-call | flops 4000000000 | bytes 4000000 | tf_op jit(solution)/shard_map/products/pallas_call | solution.py:349
  12.6 5.6 %fine.1 = (bf16[48,64,256]{2,1,0:T(8,128)(2,1)}, bf16[208,64,256]{2,1,0:T(8,128)(2,1)S(1)}, bf16[96,128]{1,0:T(8,128)(2,1)S(1)}, bf16[96,128]{1,0:T(8,128)(2,1)S...) custom-call(s32[5,1,48]{2,1,0:T(1,128)S(1)} %bitcast.11, ...), custom_call_target="tpu_custom_call", output_to_operand_aliasing={{1}: (10, {})} | custom-call | tf_op jit(solution)/shard_map/fine/pallas_call | solution.py:366
  18.2 0.0 copy-start.2
  18.2 0.0 copy-start.4
  18.2 0.7 %collective-permute-start.2 = (bf16[96,128]{1,0:T(8,128)(2,1)S(1)}, bf16[96,128]{1,0:T(8,128)(2,1)S(1)}, u32[]{:S(2)}, u32[]{:S(2)}) collective-permute-start(bf16[96,128]{1,0:T(8,128)(2,1)S(1)} %get-tuple-element.16), channel_id=1, source_target_pairs={{0,4},{4,8},{8,12},{12,0},{1,5},{5,9},{9,13},{13,1},{2,6},{6,10},{... | collective-permute-start | bytes 73736 | tf_op jit(solution)/shard_map/ppermute | solution.py:32
  18.9 1.5 %collective-permute-start.3 = (bf16[96,128]{1,0:T(8,128)(2,1)S(1)}, bf16[96,128]{1,0:T(8,128)(2,1)S(1)}, u32[]{:S(2)}, u32[]{:S(2)}) collective-permute-start(bf16[96,128]{1,0:T(8,128)(2,1)S(1)} %get-tuple-element.17), channel_id=1, source_target_pairs={{0,8},{4,12},{8,0},{12,4},{1,9},{5,13},{9,1},{13,5},{2,10},{6,14},... | collective-permute-start | bytes 73736 | tf_op jit(solution)/shard_map/ppermute | solution.py:32
  20.4 1.7 %collective-permute-start.4 = (bf16[96,128]{1,0:T(8,128)(2,1)S(1)}, bf16[96,128]{1,0:T(8,128)(2,1)S(1)}, u32[]{:S(2)}, u32[]{:S(2)}) collective-permute-start(bf16[96,128]{1,0:T(8,128)(2,1)S(1)} %get-tuple-element.18), channel_id=1, source_target_pairs={{0,12},{4,0},{8,4},{12,8},{1,13},{5,1},{9,5},{13,9},{2,14},{6,2},{... | collective-permute-start | bytes 73736 | tf_op jit(solution)/shard_map/ppermute | solution.py:32
  22.1 0.6 %order.1.order_ref = bf16[768,768]{1,0:T(8,128)(2,1)S(1)} custom-call(s32[1,192]{1,0:T(1,128)S(1)} %copy-done.6, bf16[96,128]{1,0:T(8,128)(2,1)S(1)} %get-tuple-element.15.late_ref.refs_0_), custom_call_target="tpu_custom_call" | custom-call | tf_op jit(solution)/shard_map/order/pallas_call | solution.py:389
  22.7 1.3 %collective-permute-done.2.refs_1_ = bf16[96,128]{1,0:T(8,128)(2,1)S(1)} collective-permute-done((bf16[96,128]{1,0:T(8,128)(2,1)S(1)}, bf16[96,128]{1,0:T(8,128)(2,1)S(1)}, u32[]{:S(2)}, u32[]{:S(2)}) %collective-permute-start.2) | collective-permute-done | bytes 24608 | tf_op jit(solution)/shard_map/ppermute | solution.py:32
  24.0 0.5 %collective-permute-done.3.refs_2_ = bf16[96,128]{1,0:T(8,128)(2,1)S(1)} collective-permute-done((bf16[96,128]{1,0:T(8,128)(2,1)S(1)}, bf16[96,128]{1,0:T(8,128)(2,1)S(1)}, u32[]{:S(2)}, u32[]{:S(2)}) %collective-permute-start.3) | collective-permute-done | bytes 24608 | tf_op jit(solution)/shard_map/ppermute | solution.py:32
  24.5 0.1 collective-permute-done.4.refs_3_
  24.6 0.3 merge.1
  24.9 1.6 %collective-permute-start.7 = (bf16[3,64,256]{2,1,0:T(8,128)(2,1)S(1)}, bf16[3,64,256]{2,1,0:T(8,128)(2,1)S(1)}, u32[]{:S(2)}, u32[]{:S(2)}) collective-permute-start(bf16[3,64,256]{2,1,0:T(8,128)(2,1)S(1)} %get-tuple-element.19.coarse_ref), channel_id=1, source_target_pairs={{0,2},{2,0},{1,3},{3,1},{4,6},{6,4},{5,7},{7,5},{8,10},{10,8},{9,1... | collective-permute-start | bytes 294920 | tf_op jit(solution)/shard_map/ppermute | solution.py:32
  26.5 1.9 %collective-permute-start.5 = (bf16[64,256]{1,0:T(8,128)(2,1)S(1)}, bf16[64,256]{1,0:T(8,128)(2,1)S(1)}, u32[]{:S(2)}, u32[]{:S(2)}) collective-permute-start(bf16[64,256]{1,0:T(8,128)(2,1)S(1)} %get-tuple-element.20), channel_id=1, source_target_pairs={{0,4},{4,0},{8,12},{12,8},{1,5},{5,1},{9,13},{13,9},{2,6},{6,2},{1... | collective-permute-start | bytes 98312 | tf_op jit(solution)/shard_map/ppermute | solution.py:50
  28.4 1.2 %collective-permute-start.6 = (bf16[64,256]{1,0:T(8,128)(2,1)S(1)}, bf16[64,256]{1,0:T(8,128)(2,1)S(1)}, u32[]{:S(2)}, u32[]{:S(2)}) collective-permute-start(bf16[64,256]{1,0:T(8,128)(2,1)S(1)} %get-tuple-element.21), channel_id=1, source_target_pairs={{4,8},{8,4},{12,0},{0,12},{5,9},{9,5},{13,1},{1,13},{6,10},{10,6},... | collective-permute-start | bytes 98312 | tf_op jit(solution)/shard_map/ppermute | solution.py:50
  29.6 0.8 %collective-permute-done.5.first_ref = bf16[64,256]{1,0:T(8,128)(2,1)S(1)} collective-permute-done((bf16[64,256]{1,0:T(8,128)(2,1)S(1)}, bf16[64,256]{1,0:T(8,128)(2,1)S(1)}, u32[]{:S(2)}, u32[]{:S(2)}) %collective-permute-start.5) | collective-permute-done | bytes 32800 | tf_op jit(solution)/shard_map/ppermute | solution.py:50
  30.4 3.7 %collective-permute-done.6.second_ref = bf16[64,256]{1,0:T(8,128)(2,1)S(1)} collective-permute-done((bf16[64,256]{1,0:T(8,128)(2,1)S(1)}, bf16[64,256]{1,0:T(8,128)(2,1)S(1)}, u32[]{:S(2)}, u32[]{:S(2)}) %collective-permute-start.6) | collective-permute-done | bytes 32800 | tf_op jit(solution)/shard_map/ppermute | solution.py:50
  34.1 1.9 %coarse.1 = bf16[3,64,256]{2,1,0:T(8,128)(2,1)} custom-call(s32[3,1,3]{2,1,0:T(1,128)S(1)} %bitcast.13, bf16[3,64,256]{2,1,0:T(8,128)(2,1)S(1)} %get-tuple-element.19.coarse_ref, bf16[64,256]{1,0:T(8,128)(2,1)S(1)} %collective-permute-done.5.first_ref, bf16[64,256]{1,0:T(8,128)(2,1)S(1)} %collective-permute-done.6.second_ref, ...), custom_call_target="tpu_custom_call" | custom-call | tf_op jit(solution)/shard_map/coarse/pallas_call | solution.py:412
  (20 shorter events, 0.0 us)
Async XLA Ops:
  0.6 7.3 %copy-start = (bf16[1,1,48,64,256]{4,3,2,1,0:T(8,128)(2,1)S(1)}, bf16[1,1,48,64,256]{4,3,2,1,0:T(8,128)(2,1)}, u32[]{:S(2)}) copy-start(bf16[1,1,48,64,256]{4,3,2,1,0:T(8,128)(2,1)} %param.11) | copy-start | bytes 4718596
  2.3 10.2 %collective-permute-start = (bf16[2,64,256]{2,1,0:T(8,128)(2,1)}, bf16[2,64,256]{2,1,0:T(8,128)(2,1)S(1)}, u32[]{:S(2)}, u32[]{:S(2)}) collective-permute-start(bf16[2,64,256]{2,1,0:T(8,128)(2,1)} %get-tuple-element.12), channel_id=1, source_target_pairs={{0,4},{4,0},{8,12},{12,8},{1,5},{5,1},{9,13},{13,9},{2,6},{6,2},{1... | collective-permute-start | bytes 196616 | tf_op jit(solution)/shard_map/ppermute | solution.py:50
  5.4 7.1 %collective-permute-start.1 = (bf16[2,64,256]{2,1,0:T(8,128)(2,1)}, bf16[2,64,256]{2,1,0:T(8,128)(2,1)S(1)}, u32[]{:S(2)}, u32[]{:S(2)}) collective-permute-start(bf16[2,64,256]{2,1,0:T(8,128)(2,1)} %get-tuple-element.13), channel_id=1, source_target_pairs={{4,8},{8,4},{12,0},{0,12},{5,9},{9,5},{13,1},{1,13},{6,10},{10,6},... | collective-permute-start | bytes 196616 | tf_op jit(solution)/shard_map/ppermute | solution.py:50
  7.9 1.0 %copy-start.1 = (bf16[4,256,256]{2,1,0:T(8,128)(2,1)S(1)}, bf16[4,256,256]{2,1,0:T(8,128)(2,1)}, u32[]{:S(2)}) copy-start(bf16[4,256,256]{2,1,0:T(8,128)(2,1)} %spatial_ref.4) | copy-start | bytes 1572868
  8.9 3.6 %copy-start.3 = (bf16[5,64,64]{2,1,0:T(8,128)(2,1)S(1)}, bf16[5,64,64]{2,1,0:T(8,128)(2,1)}, u32[]{:S(2)}) copy-start(bf16[5,64,64]{2,1,0:T(8,128)(2,1)} %mix_ref.2) | copy-start | bytes 122884
  8.9 3.6 %copy-start.5 = (bf16[4,256,16]{1,2,0:T(8,128)(2,1)S(1)}, bf16[4,256,16]{1,2,0:T(8,128)(2,1)}, u32[]{:S(2)}) copy-start(bf16[4,256,16]{1,2,0:T(8,128)(2,1)} %param.16) | copy-start | bytes 98308
  8.9 3.6 %copy-start.6 = (s32[1,192]{1,0:T(1,128)S(1)}, s32[1,192]{1,0:T(1,128)}, u32[]{:S(2)}) copy-start(s32[1,192]{1,0:T(1,128)} %route_ref.1) | copy-start | bytes 2308
  8.9 3.6 %copy-start.7 = (s32[1,48,5]{1,0,2:T(1,128)S(1)}, s32[1,48,5]{1,0,2:T(1,128)}, u32[]{:S(2)}) copy-start(s32[1,48,5]{1,0,2:T(1,128)} %param.14) | copy-start | bytes 2884
  8.9 3.6 %copy-start.8 = (s32[1,48,5]{1,0,2:T(1,128)S(1)}, s32[1,48,5]{1,0,2:T(1,128)}, u32[]{:S(2)}) copy-start(s32[1,48,5]{1,0,2:T(1,128)} %param.15) | copy-start | bytes 2884
  8.9 3.6 %copy-start.10 = (s32[1,48]{1,0:T(1,128)S(1)}, s32[1,48]{1,0:T(1,128)}, u32[]{:S(2)}) copy-start(s32[1,48]{1,0:T(1,128)} %rcode_in.1) | copy-start | bytes 580
  18.2 15.9 %copy-start.2 = (bf16[4,256,256]{2,1,0:T(8,128)(2,1)S(1)}, bf16[4,256,256]{2,1,0:T(8,128)(2,1)}, u32[]{:S(2)}) copy-start(bf16[4,256,256]{2,1,0:T(8,128)(2,1)} %spatial_ref.5) | copy-start | bytes 1572868
  18.2 15.9 %copy-start.4 = (bf16[4,64,64]{2,1,0:T(8,128)(2,1)S(1)}, bf16[4,64,64]{2,1,0:T(8,128)(2,1)}, u32[]{:S(2)}) copy-start(bf16[4,64,64]{2,1,0:T(8,128)(2,1)} %mix_ref.3) | copy-start | bytes 98308
  18.2 15.9 %copy-start.9 = (s32[1,3,3]{2,0,1:T(1,128)S(1)}, s32[1,3,3]{2,0,1:T(1,128)}, u32[]{:S(2)}) copy-start(s32[1,3,3]{2,0,1:T(1,128)} %param.21) | copy-start | bytes 112
  18.2 5.8 %collective-permute-start.2 = (bf16[96,128]{1,0:T(8,128)(2,1)S(1)}, bf16[96,128]{1,0:T(8,128)(2,1)S(1)}, u32[]{:S(2)}, u32[]{:S(2)}) collective-permute-start(bf16[96,128]{1,0:T(8,128)(2,1)S(1)} %get-tuple-element.16), channel_id=1, source_target_pairs={{0,4},{4,8},{8,12},{12,0},{1,5},{5,9},{9,13},{13,1},{2,6},{6,10},{... | collective-permute-start | bytes 73736 | tf_op jit(solution)/shard_map/ppermute | solution.py:32
  18.9 5.5 %collective-permute-start.3 = (bf16[96,128]{1,0:T(8,128)(2,1)S(1)}, bf16[96,128]{1,0:T(8,128)(2,1)S(1)}, u32[]{:S(2)}, u32[]{:S(2)}) collective-permute-start(bf16[96,128]{1,0:T(8,128)(2,1)S(1)} %get-tuple-element.17), channel_id=1, source_target_pairs={{0,8},{4,12},{8,0},{12,4},{1,9},{5,13},{9,1},{13,5},{2,10},{6,14},... | collective-permute-start | bytes 73736 | tf_op jit(solution)/shard_map/ppermute | solution.py:32
  20.4 4.1 %collective-permute-start.4 = (bf16[96,128]{1,0:T(8,128)(2,1)S(1)}, bf16[96,128]{1,0:T(8,128)(2,1)S(1)}, u32[]{:S(2)}, u32[]{:S(2)}) collective-permute-start(bf16[96,128]{1,0:T(8,128)(2,1)S(1)} %get-tuple-element.18), channel_id=1, source_target_pairs={{0,12},{4,0},{8,4},{12,8},{1,13},{5,1},{9,5},{13,9},{2,14},{6,2},{... | collective-permute-start | bytes 73736 | tf_op jit(solution)/shard_map/ppermute | solution.py:32
  24.9 9.2 %collective-permute-start.7 = (bf16[3,64,256]{2,1,0:T(8,128)(2,1)S(1)}, bf16[3,64,256]{2,1,0:T(8,128)(2,1)S(1)}, u32[]{:S(2)}, u32[]{:S(2)}) collective-permute-start(bf16[3,64,256]{2,1,0:T(8,128)(2,1)S(1)} %get-tuple-element.19.coarse_ref), channel_id=1, source_target_pairs={{0,2},{2,0},{1,3},{3,1},{4,6},{6,4},{5,7},{7,5},{8,10},{10,8},{9,1... | collective-permute-start | bytes 294920 | tf_op jit(solution)/shard_map/ppermute | solution.py:32
  26.5 3.9 %collective-permute-start.5 = (bf16[64,256]{1,0:T(8,128)(2,1)S(1)}, bf16[64,256]{1,0:T(8,128)(2,1)S(1)}, u32[]{:S(2)}, u32[]{:S(2)}) collective-permute-start(bf16[64,256]{1,0:T(8,128)(2,1)S(1)} %get-tuple-element.20), channel_id=1, source_target_pairs={{0,4},{4,0},{8,12},{12,8},{1,5},{5,1},{9,13},{13,9},{2,6},{6,2},{1... | collective-permute-start | bytes 98312 | tf_op jit(solution)/shard_map/ppermute | solution.py:50
  28.4 5.7 %collective-permute-start.6 = (bf16[64,256]{1,0:T(8,128)(2,1)S(1)}, bf16[64,256]{1,0:T(8,128)(2,1)S(1)}, u32[]{:S(2)}, u32[]{:S(2)}) collective-permute-start(bf16[64,256]{1,0:T(8,128)(2,1)S(1)} %get-tuple-element.21), channel_id=1, source_target_pairs={{4,8},{8,4},{12,0},{0,12},{5,9},{9,5},{13,1},{1,13},{6,10},{10,6},... | collective-permute-start | bytes 98312 | tf_op jit(solution)/shard_map/ppermute | solution.py:50

commit v3 on v2

v3 whole, which is shorter than its diff:
```python
import functools

import jax
import jax.numpy as jnp
from jax import lax
from jax.experimental import pallas as pl
from jax.experimental.pallas import tpu as pltpu
from jax.sharding import PartitionSpec as P

LANES = 128
RIM = 2
CHUNK = 8
EARLY = 3
VMEM_MIB = 40

SMEM = functools.partial(pl.BlockSpec, memory_space=pltpu.SMEM)
VMEM = functools.partial(pl.BlockSpec, memory_space=pltpu.VMEM)
ANY = functools.partial(pl.BlockSpec, memory_space=pl.ANY)
HBM = functools.partial(pl.BlockSpec, memory_space=pltpu.HBM)
F32 = jnp.float32
BF16 = jnp.bfloat16


def dot(a, b):
    return jnp.dot(a, b, preferred_element_type=F32)


def silu(v):
    return v * (0.5 + 0.5 * jnp.tanh(0.5 * v))


def shifted(value, axis, steps):
    count = lax.axis_size(axis)
    return lax.ppermute(value, axis, [(i, (i + steps) % count) for i in range(count)])


def joined_mix(mix_ref, terms):
    return jnp.concatenate([mix_ref[t] for t in range(terms)], axis=1)


def dot_t(a, b):
    return lax.dot_general(a, b, (((1,), (1,)), ((), ())), preferred_element_type=F32)


def swapped(even, value, axis):
    count = lax.axis_size(axis)
    first = 0 if even else 1
    pairs = []
    for i in range(first, count + first, 2):
        here, there = i % count, (i + 1) % count
        pairs += [(here, there), (there, here)]
    return lax.ppermute(value, axis, pairs)


def faces_right():
    return lax.rem(lax.axis_index("tile"), 2) == 0


def mixed_skip(y_ref, y_index, taps, mix_wide, mix_ref, own):
    terms = [y_ref[y_index(t)] for t in range(taps)]
    wide = mix_wide.shape[1] // mix_ref.shape[1]
    mixed = dot(mix_wide, jnp.concatenate(terms[:wide], axis=0))
    for t in range(wide, taps):
        mixed = mixed + dot(mix_ref[t], terms[t])
    return (own.astype(F32) + silu(mixed)).astype(BF16)


def place(acc_ref, at, product, code, rank, cq):
    per = LANES // cq
    slot = lax.rem(rank, per)
    amount = lax.rem((slot - code) * cq + LANES, LANES)
    turned = pltpu.roll(product, amount, axis=1)
    lane = lax.broadcasted_iota(jnp.int32, turned.shape, 1)
    at = at + lax.div(rank, per)
    acc_ref[at] = jnp.where(lax.div(lane, cq) == slot, turned, acc_ref[at])


class Packing:
    def __init__(self, per, cq, channels):
        self.cq, self.channels = cq, channels
        self.lanes = LANES // cq
        self.full, left = divmod(per, self.lanes)
        self.half = 0 < left * 2 <= self.lanes
        if left and not self.half:
            self.full += 1
        self.parts = self.full + self.half
        self.rows = self.full * channels + (channels // 2 if self.half else 0)

    def width(self, tiles):
        return (tiles * self.full + (-(-tiles // 2) if self.half else 0)) * LANES

    def column(self, tiles, hop, rank):
        whole = (hop * self.full * self.lanes + rank) * self.cq
        if not self.half:
            return whole
        split = (
            (tiles * self.full + hop // 2) * LANES
            + hop % 2 * (LANES // 2)
            + (rank - self.full * self.lanes) * self.cq
        )
        return jnp.where(rank < self.full * self.lanes, whole, split)


def cut_kernel(x_ref, first_ref, second_ref, sems):
    right = faces_right()
    last = x_ref.shape[0] - RIM
    copies = [
        pltpu.make_async_copy(x_ref.at[pl.ds(jnp.where(right, last, 0), RIM)], first_ref, sems.at[0]),
        pltpu.make_async_copy(x_ref.at[pl.ds(jnp.where(right, 0, last), RIM)], second_ref, sems.at[1]),
    ]
    for copy in copies:
        copy.start()
    for copy in copies:
        copy.wait()


class Level:
    def __init__(self, tables, y_ref, x_ref, mix_ref, restrict_ref, done_ref, acc_ref, counts_ref):
        self.nbr, self.code, self.rcode, self.route = tables
        self.y, self.x, self.mix, self.done, self.acc, self.counts = y_ref, x_ref, mix_ref, done_ref, acc_ref, counts_ref
        self.count, self.channels, self.cells = x_ref.shape
        self.rotations, self.cq = restrict_ref.shape[:2]
        self.taps = mix_ref.shape[0]
        self.blocks = self.route.shape[1]
        self.tiles = self.blocks // self.count
        self.extended = self.count + 2 * RIM
        self.me = lax.axis_index("tile")
        self.mix_wide = joined_mix(mix_ref, min(self.taps, self.cells // self.channels))
        restricts = restrict_ref[...].reshape(self.rotations * self.cq, self.cells)
        self.stacked = jnp.concatenate([restricts] * (LANES // (self.rotations * self.cq)), axis=0)
        for d in range(self.tiles):
            counts_ref[d] = 0

    def y_index(self, b, t):
        local = self.nbr[t, 0, b] - self.me * self.count + RIM
        local = jnp.where(local < 0, local + self.blocks, local)
        local = jnp.where(local >= self.blocks, local - self.blocks, local)
        return self.code[t, 0, b] * self.extended + local

    def pass_over(self, base, store=None):
        for i in range(CHUNK):
            b = base + i
            dest = lax.div(self.route[0, self.me * self.count + b], self.count)
            rank = self.counts[dest]
            self.counts[dest] = rank + 1
            if store is not None:
                store(i, b, dest, rank)

    def run(self, base):
        for i in range(CHUNK):
            b = base + i
            self.done[b] = mixed_skip(
                self.y, functools.partial(self.y_index, b), self.taps, self.mix_wide, self.mix, self.x[b]
            )

    def pack(self, base):
        rows = self.done[base:base + CHUNK].reshape(CHUNK * self.channels, self.cells)
        products = dot_t(rows, self.stacked)
        parts = self.acc.shape[0] // self.tiles

        def store(i, b, dest, rank):
            hop = lax.rem(dest - self.me + self.tiles, self.tiles)
            product = products[i * self.channels:(i + 1) * self.channels]
            place(self.acc, hop * parts, product, self.rcode[0, b], rank, self.cq)

        self.pass_over(base, store)


def fetched(sources, targets, sems):
    copies = [
        pltpu.make_async_copy(source, target, sems.at[i])
        for i, (source, target) in enumerate(zip(sources, targets))
    ]
    for copy in copies:
        copy.start()
    return copies


def chunks_of(count):
    return range(0, count, CHUNK)


def is_early(base, count):
    return CHUNK <= base < min((1 + EARLY) * CHUNK, count - CHUNK)


def put_of(done_ref, skip_ref, sems):
    def put(base):
        part = pl.ds(base, CHUNK)
        return pltpu.make_async_copy(done_ref.at[part], skip_ref.at[part], sems.at[base // CHUNK])

    return put


def early_kernel(
    x_ref, table_ref, nbr_ref, code_ref, rcode_ref, route_ref, mix_ref, restrict_ref,
    y_ref, skip_ref, acc_ref,
    nbr, code, rcode, route, mix, restrict, done_ref, counts_ref, in_sems, out_sems,
):
    count, channels, cells = x_ref.shape
    rotations = table_ref.shape[0]
    extended = count + 2 * RIM
    copies = fetched(
        (nbr_ref, code_ref, rcode_ref, route_ref, mix_ref, restrict_ref),
        (nbr, code, rcode, route, mix, restrict), in_sems,
    )
    acc_ref[...] = jnp.zeros(acc_ref.shape, F32)
    for base in chunks_of(count):
        rows = x_ref[base:base + CHUNK].reshape(CHUNK * channels, cells)
        for r in range(rotations):
            product = dot(rows, table_ref[r]).astype(BF16)
            y_ref[pl.ds(r * extended + RIM + base, CHUNK)] = product.reshape(CHUNK, channels, cells)
    for copy in copies:
        copy.wait()
    level = Level((nbr, code, rcode, route), y_ref, x_ref, mix, restrict, done_ref, acc_ref, counts_ref)
    put = put_of(done_ref, skip_ref, out_sems)
    for base in chunks_of(count):
        if is_early(base, count):
            level.run(base)
            put(base).start()
            level.pack(base)
        else:
            level.pass_over(base)
    for base in chunks_of(count):
        if is_early(base, count):
            put(base).wait()


def late_kernel(
    x_ref, table_ref, nbr_ref, code_ref, rcode_ref, route_ref, mix_ref, restrict_ref,
    first_ref, second_ref, y_in_ref, skip_in_ref, acc_in_ref, y_ref, skip_ref, acc_ref, *refs,
):
    sent_refs, refs = refs[:-10], refs[-10:]
    nbr, code, rcode, route, mix, restrict, done_ref, counts_ref, in_sems, out_sems = refs
    del y_in_ref, skip_in_ref, acc_in_ref
    count, channels, cells = x_ref.shape
    rotations = table_ref.shape[0]
    extended = count + 2 * RIM
    copies = fetched(
        (nbr_ref, code_ref, rcode_ref, route_ref, mix_ref, restrict_ref),
        (nbr, code, rcode, route, mix, restrict), in_sems,
    )
    right = faces_right()
    received = [first_ref[...], second_ref[...]]
    before = jnp.where(right, received[1], received[0])
    after = jnp.where(right, received[0], received[1])
    halo = jnp.concatenate([before, after], axis=0).reshape(2 * RIM * channels, cells)
    for r in range(rotations):
        product = dot(halo, table_ref[r]).astype(BF16).reshape(2 * RIM, channels, cells)
        y_ref[r * extended:r * extended + RIM] = product[:RIM]
        y_ref[r * extended + RIM + count:(r + 1) * extended] = product[RIM:]
    for copy in copies:
        copy.wait()
    level = Level((nbr, code, rcode, route), y_ref, x_ref, mix, restrict, done_ref, acc_ref, counts_ref)
    put = put_of(done_ref, skip_ref, out_sems)
    for base in chunks_of(count):
        if is_early(base, count):
            level.pass_over(base)
        else:
            level.run(base)
            put(base).start()
            level.pack(base)
    packing = Packing(count // level.tiles, level.cq, channels)
    half = LANES // 2
    lane = lax.broadcasted_iota(jnp.int32, (channels // 2, LANES), 1)
    for hop in range(level.tiles):
        out = sent_refs[hop]
        at = hop * packing.parts
        for p in range(packing.full):
            out[p * channels:(p + 1) * channels] = acc_ref[at + p].astype(BF16)
        if packing.half:
            value = acc_ref[at + packing.full]
            lower = pltpu.roll(value[channels // 2:], half, axis=1)
            joined = jnp.where(lane < half, value[:channels // 2], lower)
            out[packing.full * channels:] = joined.astype(BF16)
    for base in chunks_of(count):
        if not is_early(base, count):
            put(base).wait()


def order_kernel(count, cq, channels, route_ref, late_ref, order_ref):
    del late_ref
    blocks = route_ref.shape[1]
    tiles = blocks // count
    packing = Packing(count // tiles, cq, channels)
    me = lax.axis_index("tile")
    base = me * count
    route = route_ref[...]
    mine = jnp.where((route >= base) & (route < base + count), 1.0, 0.0)
    shape = (blocks, blocks)
    of, at = (lax.broadcasted_iota(jnp.int32, shape, d) for d in (0, 1))
    earlier = jnp.where((of < at) & (lax.div(of, count) == lax.div(at, count)), 1.0, 0.0)
    rank = dot(jnp.broadcast_to(mine, (8, blocks)).astype(BF16), earlier.astype(BF16))[:1].astype(jnp.int32)
    source = lax.div(lax.broadcasted_iota(jnp.int32, (1, blocks), 1), count)
    hop = lax.rem(me - source + tiles, tiles)
    column = packing.column(tiles, hop, rank).astype(F32)
    cells = count * cq
    cell = lax.broadcasted_iota(jnp.int32, (cells, blocks), 0)
    found = jnp.where(route == base + lax.div(cell, cq), column, 0.0)
    wanted = jnp.sum(found, axis=1, keepdims=True)
    wanted = wanted + lax.rem(lax.broadcasted_iota(jnp.int32, (cells, 1), 0), cq).astype(F32)
    across = jnp.transpose(jnp.broadcast_to(wanted, (cells, LANES)))[:1].astype(jnp.int32)
    step = LANES
    for row in range(0, order_ref.shape[0], step):
        index = row + lax.broadcasted_iota(jnp.int32, (step, cells), 0)
        order_ref[row:row + step] = jnp.where(index == across, 1.0, 0.0).astype(BF16)


def merge_kernel(per, cq, order_ref, *refs):
    arrived, (coarse_ref, first_ref, second_ref) = refs[:-3], refs[-3:]
    arrived = arrived[:1] + arrived[:0:-1]
    blocks, channels, cells = coarse_ref.shape
    tiles = len(arrived)
    packing = Packing(per, cq, channels)
    columns = [ref[p * channels:(p + 1) * channels] for ref in arrived for p in range(packing.full)]
    if packing.half:
        half = LANES // 2
        lane = lax.broadcasted_iota(jnp.int32, (channels // 2, LANES), 1)
        halves = [ref[packing.full * channels:].astype(F32) for ref in arrived]
        halves += [jnp.zeros_like(halves[0])] * (tiles % 2)
        for one, other in zip(halves[::2], halves[1::2]):
            upper = jnp.where(lane < half, one, pltpu.roll(other, half, axis=1))
            lower = jnp.where(lane < half, pltpu.roll(one, half, axis=1), other)
            columns.append(jnp.concatenate([upper, lower], axis=0).astype(BF16))
    joined = jnp.concatenate(columns, axis=1)
    values = [
        dot(joined, order_ref[:, c * cells:(c + 1) * cells]).astype(BF16) for c in range(blocks)
    ]
    for c in range(blocks):
        coarse_ref[c] = values[c]
    right = faces_right()
    first_ref[...] = jnp.where(right, values[-1], values[0])
    second_ref[...] = jnp.where(right, values[0], values[-1])


def inside_kernel(code_ref, coarse_ref, spatial_ref, mix_ref, total_ref, table_ref):
    blocks = coarse_ref.shape[0]
    values = [coarse_ref[c] for c in range(blocks)]
    for c in range(blocks):
        total = dot(mix_ref[0], values[c])
        for e, other in enumerate((c - 1, c + 1)):
            if 0 <= other < blocks:
                edge = dot(values[other], spatial_ref[code_ref[c, 0, e]]).astype(BF16)
                total = total + dot(mix_ref[e + 1], edge)
        total_ref[c] = total
        table_ref[2 + c] = spatial_ref[code_ref[c, 0, 2]]
    table_ref[0] = spatial_ref[code_ref[0, 0, 0]]
    table_ref[1] = spatial_ref[code_ref[blocks - 1, 0, 1]]


def coarse_kernel(seam_ref, first_ref, second_ref, coarse_ref, total_ref, table_ref, mix_ref, out_ref):
    blocks = coarse_ref.shape[0]
    right = faces_right()
    left_rows = jnp.where(right, second_ref[...], first_ref[...])
    right_rows = jnp.where(right, first_ref[...], second_ref[...])
    left_edge = dot(left_rows, table_ref[0]).astype(BF16)
    right_edge = dot(right_rows, table_ref[1]).astype(BF16)
    for c in range(blocks):
        total = total_ref[c] + dot(mix_ref[3], dot(seam_ref[c], table_ref[2 + c]).astype(BF16))
        if c == 0:
            total = total + dot(mix_ref[1], left_edge)
        if c == blocks - 1:
            total = total + dot(mix_ref[2], right_edge)
        out_ref[c] = (coarse_ref[c].astype(F32) + silu(total)).astype(BF16)


def params(mib=VMEM_MIB):
    return pltpu.CompilerParams(vmem_limit_bytes=mib * 1024 * 1024)


def per_device(
    fine, conv_spatial, conv_mix, neighbours, fine_codes, restrict, restrict_codes, route,
    coarse_spatial, coarse_mix, coarse_codes,
):
    x = fine[0, 0]
    count, channels, cells = x.shape
    rotations = conv_spatial.shape[0]
    cq = restrict.shape[2]
    tiles = route.shape[1] // count
    per = count // tiles
    blocks = count * cq // cells
    packing = Packing(per, cq, channels)
    nbr, codes = neighbours.transpose(2, 0, 1), fine_codes.transpose(2, 0, 1)
    narrow = restrict.transpose(0, 2, 1)

    rim_shape = jax.ShapeDtypeStruct((RIM, channels, cells), BF16)
    first, second = pl.pallas_call(
        cut_kernel,
        out_shape=(rim_shape, rim_shape),
        in_specs=[HBM()],
        out_specs=(VMEM(),) * 2,
        scratch_shapes=[pltpu.SemaphoreType.DMA((2,))],
        compiler_params=params(),
        cost_estimate=pl.CostEstimate(flops=4 * 10**9, bytes_accessed=10**6, transcendentals=0),
        name="cut",
    )(x)
    second = swapped(False, second, "tile")
    first = swapped(True, first, "tile")

    y_shape = (rotations * (count + 2 * RIM), channels, cells)
    steps = count // CHUNK
    tables = (nbr, codes, restrict_codes, route)
    shared = [pltpu.SMEM(a.shape, jnp.int32) for a in tables] + [
        pltpu.VMEM(conv_mix.shape, BF16),
        pltpu.VMEM(narrow.shape, BF16),
        pltpu.VMEM(x.shape, BF16),
        pltpu.SMEM((tiles,), jnp.int32),
        pltpu.SemaphoreType.DMA((6,)),
        pltpu.SemaphoreType.DMA((steps,)),
    ]
    made = (
        jax.ShapeDtypeStruct(y_shape, BF16),
        jax.ShapeDtypeStruct(x.shape, BF16),
        jax.ShapeDtypeStruct((tiles * packing.parts, channels, LANES), F32),
    )
    given = (x, conv_spatial) + tables + (conv_mix, narrow)
    given_specs = [VMEM()] * 2 + [ANY()] * 6
    y, skip, acc = pl.pallas_call(
        early_kernel,
        out_shape=made,
        in_specs=given_specs,
        out_specs=(VMEM(), ANY(), VMEM()),
        scratch_shapes=shared,
        compiler_params=params(),
        cost_estimate=pl.CostEstimate(flops=4 * 10**9, bytes_accessed=4 * 10**6, transcendentals=10**6),
        name="early",
    )(*given)

    sent_shape = jax.ShapeDtypeStruct((packing.rows, LANES), BF16)
    _, skip, _, *sent = pl.pallas_call(
        late_kernel,
        out_shape=made + (sent_shape,) * tiles,
        in_specs=given_specs + [VMEM()] * 3 + [ANY(), VMEM()],
        out_specs=(VMEM(), ANY(), VMEM()) + (VMEM(),) * tiles,
        scratch_shapes=shared,
        input_output_aliases={10: 0, 11: 1, 12: 2},
        compiler_params=params(),
        name="late",
    )(*given, first, second, y, skip, acc)

    order = pl.pallas_call(
        functools.partial(order_kernel, count, cq, channels),
        out_shape=jax.ShapeDtypeStruct((packing.width(tiles), count * cq), BF16),
        in_specs=[VMEM(), VMEM()],
        out_specs=VMEM(),
        compiler_params=params(),
        name="order",
    )(route, sent[0])
    arrived = [sent[0]] + [shifted(sent[hop], "tile", hop) for hop in range(1, tiles)]

    block_shape = jax.ShapeDtypeStruct((channels, cells), BF16)
    coarse, first, second = pl.pallas_call(
        functools.partial(merge_kernel, per, cq),
        out_shape=(jax.ShapeDtypeStruct((blocks, channels, cells), BF16), block_shape, block_shape),
        in_specs=[VMEM()] * (1 + tiles),
        out_specs=(VMEM(), VMEM(), VMEM()),
        compiler_params=params(),
        name="merge",
    )(order, arrived[0], *arrived[:0:-1])

    second = swapped(False, second, "tile")
    first = swapped(True, first, "tile")
    seam = shifted(coarse, "sect", 1)
    total, tables = pl.pallas_call(
        inside_kernel,
        out_shape=(
            jax.ShapeDtypeStruct(coarse.shape, F32),
            jax.ShapeDtypeStruct((2 + blocks,) + coarse_spatial.shape[1:], BF16),
        ),
        in_specs=[SMEM()] + [VMEM()] * 3,
        out_specs=(VMEM(), VMEM()),
        compiler_params=params(),
        name="inside",
    )(coarse_codes.transpose(1, 0, 2), coarse, coarse_spatial, coarse_mix)
    coarse_out = pl.pallas_call(
        coarse_kernel,
        out_shape=jax.ShapeDtypeStruct(coarse.shape, BF16),
        in_specs=[VMEM()] * 7,
        out_specs=VMEM(),
        compiler_params=params(),
        name="coarse",
    )(seam, first, second, coarse, total, tables, coarse_mix)
    return (skip[None, None], coarse_out[None, None])


def solution(mesh):
    data = P(("groups", "chan"), "sect", "tile", None, None)
    placed = (
        data,
        P(),
        P(),
        P("sect", "tile", None),
        P("sect", "tile", None),
        P(),
        P("sect", "tile"),
        P("sect", None),
        P(),
        P(),
        P("sect", "tile", None),
    )
    return jax.shard_map(
        per_device, mesh=mesh, in_specs=placed, out_specs=(data, data), check_vma=False
    )
```

time: 36.2 us -> 31.9 us (0.88)
  Pallas kernels: 13.6 us -> 10.7 us
  starting transfers between devices: 14.2 us -> 11.7 us
  waiting for transfers between devices: 6.34 us -> 7.12 us
    ppermute x4, waiting for transfers between devices: 1.86 us -> 4.82 us  [shifted(): lax.ppermute(value, axis, [(i, (i + steps) % count) for i in range(count)])]
    pallas_call x3 -> x4, Pallas kernels: 10.8 us -> 8.56 us  [the longest x1 4.26 us: per_device(): pl.pallas_call(early_kernel, out_shape=made, in_specs=given_specs, out_sp...]
    ppermute x4, waiting for transfers between devices: 4.48 us -> 2.3 us  [swapped(): return lax.ppermute(value, axis, pairs)]
    ppermute x4, starting transfers between devices: 5.44 us -> 3.96 us  [shifted(): lax.ppermute(value, axis, [(i, (i + steps) % count) for i in range(count)])]
    ppermute x4, starting transfers between devices: 8.73 us -> 7.73 us  [swapped(): return lax.ppermute(value, axis, pairs)]
    pallas_call x1, Pallas kernels: 1.91 us -> 1.21 us  [per_device(): pl.pallas_call(coarse_kernel, out_shape=jax.ShapeDtypeStruct(coarse.shape...]
  transfers between devices with their start and end apart: 8 -> 8, of which waited for: 5 -> 5; matrix products, arithmetic and copies ran while one was open for 0% -> 0% of each run, Pallas kernels for 11% -> 19%
where the time goes in v3:
time: 31.9 us; the launch traced here: 31.7 us
  starting transfers between devices  11.7 us (37%)
  Pallas kernels  10.7 us (34%)
  waiting for transfers between devices  7.12 us (22%)
  local copies, waits for them, and re-layouts  1.45 us (5%)
  between operations  0.79 us (2%)
    ppermute x4, starting transfers between devices, swapped(): return lax.ppermute(value, axis, pairs)  7.73 us
    ppermute x4, waiting for transfers between devices, shifted(): lax.ppermute(value, axis, [(i, (i + steps) % count) for i in range(count)])  4.82 us
    pallas_call x1, Pallas kernels, per_device(): pl.pallas_call(early_kernel, out_shape=made, in_specs=given_specs, out_sp...  4.26 us
    ppermute x4, starting transfers between devices, shifted(): lax.ppermute(value, axis, [(i, (i + steps) % count) for i in range(count)])  3.96 us
    pallas_call x1, Pallas kernels, per_device(): pl.pallas_call(late_kernel, out_shape=made + (sent_shape,) * tiles, in_sp...  2.85 us
    ppermute x4, waiting for transfers between devices, swapped(): return lax.ppermute(value, axis, pairs)  2.3 us
    unnamed x22, local copies, waits for them, and re-layouts  1.45 us
    pallas_call x1, Pallas kernels, per_device(): pl.pallas_call(inside_kernel, out_shape=(jax.ShapeDtypeStruct(coarse.shap...  1.25 us
  transfers between devices with their start and end apart: 8, of which 5 were waited for; matrix products, arithmetic and copies ran while one was open for 0% of the time, Pallas kernels for 19%

profile of v3, /device:TPU:0, one launch (start us, length us, event | category | flops | bytes accessed | tf_op | source)
XLA Modules:
  0.0 31.7 jit_solution(11628803032683578155)
XLA Ops:
  0.6 1.4 %copy-done = bf16[1,1,48,64,256]{4,3,2,1,0:T(8,128)(2,1)S(1)} copy-done((bf16[1,1,48,64,256]{4,3,2,1,0:T(8,128)(2,1)S(1)}, bf16[1,1,48,64,256]{4,3,2,1,0:T(8,128)(2,1)}, u32[]{:S(2)}) %copy-start) | copy-done | bytes 1572888
  2.1 0.2 cut.1
  2.3 3.1 %collective-permute-start = (bf16[2,64,256]{2,1,0:T(8,128)(2,1)S(1)}, bf16[2,64,256]{2,1,0:T(8,128)(2,1)S(1)}, u32[]{:S(2)}, u32[]{:S(2)}) collective-permute-start(bf16[2,64,256]{2,1,0:T(8,128)(2,1)S(1)} %get-tuple-element.17), channel_id=1, source_target_pairs={{0,4},{4,0},{8,12},{12,8},{1,5},{5,1},{9,13},{13,9},{2,6},{6,2},{1... | collective-permute-start | bytes 196616 | tf_op jit(solution)/shard_map/ppermute | solution.py:52
  5.4 2.5 %collective-permute-start.1 = (bf16[2,64,256]{2,1,0:T(8,128)(2,1)S(1)}, bf16[2,64,256]{2,1,0:T(8,128)(2,1)S(1)}, u32[]{:S(2)}, u32[]{:S(2)}) collective-permute-start(bf16[2,64,256]{2,1,0:T(8,128)(2,1)S(1)} %get-tuple-element.18), channel_id=1, source_target_pairs={{4,8},{8,4},{12,0},{0,12},{5,9},{9,5},{13,1},{1,13},{6,10},{10,6},... | collective-permute-start | bytes 196616 | tf_op jit(solution)/shard_map/ppermute | solution.py:52
  7.9 4.3 %early.1 = (bf16[208,64,256]{2,1,0:T(8,128)(2,1)S(1)}, bf16[48,64,256]{2,1,0:T(8,128)(2,1)}, f32[8,64,128]{2,1,0:T(8,128)S(1)}) custom-call(bf16[48,64,256]{2,1,0:T(8,128)(2,1)S(1)} %bitcast.8, bf16[4,256,256]{2,1,0:T(8,128)(2,1)S(1)} %copy-done.1, s32[5,1,48]{2,1,0:T(1,128)S(1)} %bitcast.12, s32[5,1,48]{2,1,0:T(1,128)S(1)} %bitcast.14, ...), custom_call_target="tpu_custom_call" | custom-call | flops 4000000000 | bytes 4000000 | tf_op jit(solution)/shard_map/early/pallas_call | solution.py:418
  12.2 0.0 collective-permute-done.first_ref
  12.2 2.8 %late.1 = (bf16[208,64,256]{2,1,0:T(8,128)(2,1)S(1)}, bf16[48,64,256]{2,1,0:T(8,128)(2,1)}, f32[8,64,128]{2,1,0:T(8,128)S(1)}, bf16[96,128]{1,0:T(8,128)(2,1)S(1...) custom-call(bf16[48,64,256]{2,1,0:T(8,128)(2,1)S(1)} %bitcast.9, ...), custom_call_target="tpu_custom_call", output_to_operand_aliasing={{0}: (10, {}), {1}: (11, {}), {2}: (12, {})} | custom-call | tf_op jit(solution)/shard_map/late/pallas_call | solution.py:430
  15.0 0.0 copy-start.2
  15.1 0.0 copy-start.3
  15.1 0.0 copy-start.9
  15.1 1.8 %collective-permute-start.2 = (bf16[96,128]{1,0:T(8,128)(2,1)S(1)}, bf16[96,128]{1,0:T(8,128)(2,1)S(1)}, u32[]{:S(2)}, u32[]{:S(2)}) collective-permute-start(bf16[96,128]{1,0:T(8,128)(2,1)S(1)} %get-tuple-element.24), channel_id=1, source_target_pairs={{0,12},{4,0},{8,4},{12,8},{1,13},{5,1},{9,5},{13,9},{2,14},{6,2},{... | collective-permute-start | bytes 73736 | tf_op jit(solution)/shard_map/ppermute | solution.py:34
  16.8 0.4 %collective-permute-start.3 = (bf16[96,128]{1,0:T(8,128)(2,1)S(1)}, bf16[96,128]{1,0:T(8,128)(2,1)S(1)}, u32[]{:S(2)}, u32[]{:S(2)}) collective-permute-start(bf16[96,128]{1,0:T(8,128)(2,1)S(1)} %get-tuple-element.25), channel_id=1, source_target_pairs={{0,8},{4,12},{8,0},{12,4},{1,9},{5,13},{9,1},{13,5},{2,10},{6,14},... | collective-permute-start | bytes 73736 | tf_op jit(solution)/shard_map/ppermute | solution.py:34
  17.3 0.2 collective-permute-start.4
  17.5 0.6 %order.1.order_ref = bf16[768,768]{1,0:T(8,128)(2,1)S(1)} custom-call(s32[1,192]{1,0:T(1,128)S(1)} %copy-done.6, bf16[96,128]{1,0:T(8,128)(2,1)S(1)} %get-tuple-element.23.late_ref.refs_0_), custom_call_target="tpu_custom_call" | custom-call | tf_op jit(solution)/shard_map/order/pallas_call | solution.py:441
  18.1 0.9 %collective-permute-done.2.refs_1_ = bf16[96,128]{1,0:T(8,128)(2,1)S(1)} collective-permute-done((bf16[96,128]{1,0:T(8,128)(2,1)S(1)}, bf16[96,128]{1,0:T(8,128)(2,1)S(1)}, u32[]{:S(2)}, u32[]{:S(2)}) %collective-permute-start.2) | collective-permute-done | bytes 24608 | tf_op jit(solution)/shard_map/ppermute | solution.py:34
  19.0 2.6 %collective-permute-done.3.refs_2_ = bf16[96,128]{1,0:T(8,128)(2,1)S(1)} collective-permute-done((bf16[96,128]{1,0:T(8,128)(2,1)S(1)}, bf16[96,128]{1,0:T(8,128)(2,1)S(1)}, u32[]{:S(2)}, u32[]{:S(2)}) %collective-permute-start.3) | collective-permute-done | bytes 24608 | tf_op jit(solution)/shard_map/ppermute | solution.py:34
  21.6 1.3 %collective-permute-done.4.refs_3_ = bf16[96,128]{1,0:T(8,128)(2,1)S(1)} collective-permute-done((bf16[96,128]{1,0:T(8,128)(2,1)S(1)}, bf16[96,128]{1,0:T(8,128)(2,1)S(1)}, u32[]{:S(2)}, u32[]{:S(2)}) %collective-permute-start.4) | collective-permute-done | bytes 24608 | tf_op jit(solution)/shard_map/ppermute | solution.py:34
  22.9 0.3 %merge.1 = (bf16[3,64,256]{2,1,0:T(8,128)(2,1)S(1)}, bf16[64,256]{1,0:T(8,128)(2,1)S(1)}, bf16[64,256]{1,0:T(8,128)(2,1)S(1)}) custom-call(bf16[768,768]{1,0:T(8,128)(2,1)S(1)} %order.1.order_ref, bf16[96,128]{1,0:T(8,128)(2,1)S(1)} %get-tuple-element.23.late_ref.refs_0_, bf16[96,128]{1,0:T(8,128)(2,1)S(1)} %collective-permute-done.2.refs_1_, ...), custom_call_target="tpu_custom_call" | custom-call | tf_op jit(solution)/shard_map/merge/pallas_call | solution.py:452
  23.2 1.6 %collective-permute-start.5 = (bf16[3,64,256]{2,1,0:T(8,128)(2,1)S(1)}, bf16[3,64,256]{2,1,0:T(8,128)(2,1)S(1)}, u32[]{:S(2)}, u32[]{:S(2)}) collective-permute-start(bf16[3,64,256]{2,1,0:T(8,128)(2,1)S(1)} %get-tuple-element.27.coarse_ref), channel_id=1, source_target_pairs={{0,2},{2,0},{1,3},{3,1},{4,6},{6,4},{5,7},{7,5},{8,10},{10,8},{9,1... | collective-permute-start | bytes 294920 | tf_op jit(solution)/shard_map/ppermute | solution.py:34
  24.8 2.2 %collective-permute-start.7 = (bf16[64,256]{1,0:T(8,128)(2,1)S(1)}, bf16[64,256]{1,0:T(8,128)(2,1)S(1)}, u32[]{:S(2)}, u32[]{:S(2)}) collective-permute-start(bf16[64,256]{1,0:T(8,128)(2,1)S(1)} %get-tuple-element.29), channel_id=1, source_target_pairs={{4,8},{8,4},{12,0},{0,12},{5,9},{9,5},{13,1},{1,13},{6,10},{10,6},... | collective-permute-start | bytes 98312 | tf_op jit(solution)/shard_map/ppermute | solution.py:52
  27.0 1.2 %inside.1 = (f32[3,64,256]{2,1,0:T(8,128)S(1)}, bf16[5,256,256]{2,1,0:T(8,128)(2,1)S(1)}) custom-call(s32[3,1,3]{2,1,0:T(1,128)S(1)} %bitcast.16, bf16[3,64,256]{2,1,0:T(8,128)(2,1)S(1)} %get-tuple-element.27.coarse_ref, bf16[4,256,256]{2,1,0:T(8,128)(2,1)S(1)} %copy-done.2, bf16[4,64,64]{2,1,0:T(8,128)(2,1)S(1)} %copy-done.3), custom_call_target="tpu_custom_call" | custom-call | tf_op jit(solution)/shard_map/inside/pallas_call | solution.py:464
  28.2 0.5 %collective-permute-done.6.first_ref = bf16[64,256]{1,0:T(8,128)(2,1)S(1)} collective-permute-done((bf16[64,256]{1,0:T(8,128)(2,1)S(1)}, bf16[64,256]{1,0:T(8,128)(2,1)S(1)}, u32[]{:S(2)}, u32[]{:S(2)}) %collective-permute-start.6) | collective-permute-done | bytes 32800 | tf_op jit(solution)/shard_map/ppermute | solution.py:52
  28.7 1.8 %collective-permute-done.7.second_ref = bf16[64,256]{1,0:T(8,128)(2,1)S(1)} collective-permute-done((bf16[64,256]{1,0:T(8,128)(2,1)S(1)}, bf16[64,256]{1,0:T(8,128)(2,1)S(1)}, u32[]{:S(2)}, u32[]{:S(2)}) %collective-permute-start.7) | collective-permute-done | bytes 32800 | tf_op jit(solution)/shard_map/ppermute | solution.py:52
  30.5 1.2 %coarse.1 = bf16[3,64,256]{2,1,0:T(8,128)(2,1)} custom-call(bf16[3,64,256]{2,1,0:T(8,128)(2,1)S(1)} %collective-permute-done.5.seam_ref, bf16[64,256]{1,0:T(8,128)(2,1)S(1)} %collective-permute-done.6.first_ref, bf16[64,256]{1,0:T(8,128)(2,1)S(1)} %collective-permute-done.7.second_ref, bf16[3,64,256]{2,1,0:T(8,128)(2,1)S(1)} %get-tuple-element.27.coarse_ref, ...), custom_call_target="tpu_custom_call" | custom-call | tf_op jit(solution)/shard_map/coarse/pallas_call | solution.py:475
  (21 shorter events, 0.0 us)
Async XLA Ops:
  0.6 1.4 %copy-start = (bf16[1,1,48,64,256]{4,3,2,1,0:T(8,128)(2,1)S(1)}, bf16[1,1,48,64,256]{4,3,2,1,0:T(8,128)(2,1)}, u32[]{:S(2)}) copy-start(bf16[1,1,48,64,256]{4,3,2,1,0:T(8,128)(2,1)} %param.11) | copy-start | bytes 4718596
  2.0 5.8 %copy-start.1 = (bf16[4,256,256]{2,1,0:T(8,128)(2,1)S(1)}, bf16[4,256,256]{2,1,0:T(8,128)(2,1)}, u32[]{:S(2)}) copy-start(bf16[4,256,256]{2,1,0:T(8,128)(2,1)} %table_ref.3) | copy-start | bytes 1572868
  2.0 5.8 %copy-start.4 = (bf16[5,64,64]{2,1,0:T(8,128)(2,1)S(1)}, bf16[5,64,64]{2,1,0:T(8,128)(2,1)}, u32[]{:S(2)}) copy-start(bf16[5,64,64]{2,1,0:T(8,128)(2,1)} %mix_ref.5) | copy-start | bytes 122884
  2.0 5.8 %copy-start.5 = (bf16[4,256,16]{1,2,0:T(8,128)(2,1)S(1)}, bf16[4,256,16]{1,2,0:T(8,128)(2,1)}, u32[]{:S(2)}) copy-start(bf16[4,256,16]{1,2,0:T(8,128)(2,1)} %param.16) | copy-start | bytes 98308
  2.0 5.8 %copy-start.6 = (s32[1,192]{1,0:T(1,128)S(1)}, s32[1,192]{1,0:T(1,128)}, u32[]{:S(2)}) copy-start(s32[1,192]{1,0:T(1,128)} %route_ref.5) | copy-start | bytes 2308
  2.1 5.8 %copy-start.7 = (s32[1,48,5]{1,0,2:T(1,128)S(1)}, s32[1,48,5]{1,0,2:T(1,128)}, u32[]{:S(2)}) copy-start(s32[1,48,5]{1,0,2:T(1,128)} %param.14) | copy-start | bytes 2884
  2.1 5.8 %copy-start.8 = (s32[1,48,5]{1,0,2:T(1,128)S(1)}, s32[1,48,5]{1,0,2:T(1,128)}, u32[]{:S(2)}) copy-start(s32[1,48,5]{1,0,2:T(1,128)} %param.15) | copy-start | bytes 2884
  2.1 5.8 %copy-start.10 = (s32[1,48]{1,0:T(1,128)S(1)}, s32[1,48]{1,0:T(1,128)}, u32[]{:S(2)}) copy-start(s32[1,48]{1,0:T(1,128)} %rcode_ref.3) | copy-start | bytes 580
  2.3 9.9 %collective-permute-start = (bf16[2,64,256]{2,1,0:T(8,128)(2,1)S(1)}, bf16[2,64,256]{2,1,0:T(8,128)(2,1)S(1)}, u32[]{:S(2)}, u32[]{:S(2)}) collective-permute-start(bf16[2,64,256]{2,1,0:T(8,128)(2,1)S(1)} %get-tuple-element.17), channel_id=1, source_target_pairs={{0,4},{4,0},{8,12},{12,8},{1,5},{5,1},{9,13},{13,9},{2,6},{6,2},{1... | collective-permute-start | bytes 196616 | tf_op jit(solution)/shard_map/ppermute | solution.py:52
  5.4 6.8 %collective-permute-start.1 = (bf16[2,64,256]{2,1,0:T(8,128)(2,1)S(1)}, bf16[2,64,256]{2,1,0:T(8,128)(2,1)S(1)}, u32[]{:S(2)}, u32[]{:S(2)}) collective-permute-start(bf16[2,64,256]{2,1,0:T(8,128)(2,1)S(1)} %get-tuple-element.18), channel_id=1, source_target_pairs={{4,8},{8,4},{12,0},{0,12},{5,9},{9,5},{13,1},{1,13},{6,10},{10,6},... | collective-permute-start | bytes 196616 | tf_op jit(solution)/shard_map/ppermute | solution.py:52
  15.0 11.9 %copy-start.2 = (bf16[4,256,256]{2,1,0:T(8,128)(2,1)S(1)}, bf16[4,256,256]{2,1,0:T(8,128)(2,1)}, u32[]{:S(2)}) copy-start(bf16[4,256,256]{2,1,0:T(8,128)(2,1)} %spatial_ref.1) | copy-start | bytes 1572868
  15.1 11.9 %copy-start.3 = (bf16[4,64,64]{2,1,0:T(8,128)(2,1)S(1)}, bf16[4,64,64]{2,1,0:T(8,128)(2,1)}, u32[]{:S(2)}) copy-start(bf16[4,64,64]{2,1,0:T(8,128)(2,1)} %mix_ref.7) | copy-start | bytes 98308
  15.1 11.9 %copy-start.9 = (s32[1,3,3]{2,0,1:T(1,128)S(1)}, s32[1,3,3]{2,0,1:T(1,128)}, u32[]{:S(2)}) copy-start(s32[1,3,3]{2,0,1:T(1,128)} %param.21) | copy-start | bytes 112
  15.1 3.9 %collective-permute-start.2 = (bf16[96,128]{1,0:T(8,128)(2,1)S(1)}, bf16[96,128]{1,0:T(8,128)(2,1)S(1)}, u32[]{:S(2)}, u32[]{:S(2)}) collective-permute-start(bf16[96,128]{1,0:T(8,128)(2,1)S(1)} %get-tuple-element.24), channel_id=1, source_target_pairs={{0,12},{4,0},{8,4},{12,8},{1,13},{5,1},{9,5},{13,9},{2,14},{6,2},{... | collective-permute-start | bytes 73736 | tf_op jit(solution)/shard_map/ppermute | solution.py:34
  16.8 4.7 %collective-permute-start.3 = (bf16[96,128]{1,0:T(8,128)(2,1)S(1)}, bf16[96,128]{1,0:T(8,128)(2,1)S(1)}, u32[]{:S(2)}, u32[]{:S(2)}) collective-permute-start(bf16[96,128]{1,0:T(8,128)(2,1)S(1)} %get-tuple-element.25), channel_id=1, source_target_pairs={{0,8},{4,12},{8,0},{12,4},{1,9},{5,13},{9,1},{13,5},{2,10},{6,14},... | collective-permute-start | bytes 73736 | tf_op jit(solution)/shard_map/ppermute | solution.py:34
  17.3 5.6 %collective-permute-start.4 = (bf16[96,128]{1,0:T(8,128)(2,1)S(1)}, bf16[96,128]{1,0:T(8,128)(2,1)S(1)}, u32[]{:S(2)}, u32[]{:S(2)}) collective-permute-start(bf16[96,128]{1,0:T(8,128)(2,1)S(1)} %get-tuple-element.26), channel_id=1, source_target_pairs={{0,4},{4,8},{8,12},{12,0},{1,5},{5,9},{9,13},{13,1},{2,6},{6,10},{... | collective-permute-start | bytes 73736 | tf_op jit(solution)/shard_map/ppermute | solution.py:34
  23.2 7.3 %collective-permute-start.5 = (bf16[3,64,256]{2,1,0:T(8,128)(2,1)S(1)}, bf16[3,64,256]{2,1,0:T(8,128)(2,1)S(1)}, u32[]{:S(2)}, u32[]{:S(2)}) collective-permute-start(bf16[3,64,256]{2,1,0:T(8,128)(2,1)S(1)} %get-tuple-element.27.coarse_ref), channel_id=1, source_target_pairs={{0,2},{2,0},{1,3},{3,1},{4,6},{6,4},{5,7},{7,5},{8,10},{10,8},{9,1... | collective-permute-start | bytes 294920 | tf_op jit(solution)/shard_map/ppermute | solution.py:34
  24.8 3.9 %collective-permute-start.6 = (bf16[64,256]{1,0:T(8,128)(2,1)S(1)}, bf16[64,256]{1,0:T(8,128)(2,1)S(1)}, u32[]{:S(2)}, u32[]{:S(2)}) collective-permute-start(bf16[64,256]{1,0:T(8,128)(2,1)S(1)} %get-tuple-element.28), channel_id=1, source_target_pairs={{0,4},{4,0},{8,12},{12,8},{1,5},{5,1},{9,13},{13,9},{2,6},{6,2},{1... | collective-permute-start | bytes 98312 | tf_op jit(solution)/shard_map/ppermute | solution.py:52
  24.8 5.7 %collective-permute-start.7 = (bf16[64,256]{1,0:T(8,128)(2,1)S(1)}, bf16[64,256]{1,0:T(8,128)(2,1)S(1)}, u32[]{:S(2)}, u32[]{:S(2)}) collective-permute-start(bf16[64,256]{1,0:T(8,128)(2,1)S(1)} %get-tuple-element.29), channel_id=1, source_target_pairs={{4,8},{8,4},{12,0},{0,12},{5,9},{9,5},{13,1},{1,13},{6,10},{10,6},... | collective-permute-start | bytes 98312 | tf_op jit(solution)/shard_map/ppermute | solution.py:52

commit v4 on v3

--- a/solution.py
+++ b/solution.py
@@ -50,6 +50,26 @@
         here, there = i % count, (i + 1) % count
         pairs += [(here, there), (there, here)]
     return lax.ppermute(value, axis, pairs)
+
+
+def paired(tiles):
+    return tiles & (tiles - 1) == 0
+
+
+def hop_between(dest, source, tiles):
+    if paired(tiles):
+        return lax.bitwise_xor(dest, source)
+    return lax.rem(dest - source + tiles, tiles)
+
+
+def exchanged(value, axis, hop):
+    count = lax.axis_size(axis)
+    pairs = [(i, i ^ hop if paired(count) else (i + hop) % count) for i in range(count)]
+    return lax.ppermute(value, axis, pairs)
+
+
+def hop_order(tiles):
+    return list(range(tiles // 2, tiles)) + list(range(1, tiles // 2))
 
 
 def faces_right():
@@ -159,7 +179,7 @@
         parts = self.acc.shape[0] // self.tiles
 
         def store(i, b, dest, rank):
-            hop = lax.rem(dest - self.me + self.tiles, self.tiles)
+            hop = hop_between(dest, self.me, self.tiles)
             product = products[i * self.channels:(i + 1) * self.channels]
             place(self.acc, hop * parts, product, self.rcode[0, b], rank, self.cq)
 
@@ -292,7 +312,7 @@
     earlier = jnp.where((of < at) & (lax.div(of, count) == lax.div(at, count)), 1.0, 0.0)
     rank = dot(jnp.broadcast_to(mine, (8, blocks)).astype(BF16), earlier.astype(BF16))[:1].astype(jnp.int32)
     source = lax.div(lax.broadcasted_iota(jnp.int32, (1, blocks), 1), count)
-    hop = lax.rem(me - source + tiles, tiles)
+    hop = hop_between(me, source, tiles)
     column = packing.column(tiles, hop, rank).astype(F32)
     cells = count * cq
     cell = lax.broadcasted_iota(jnp.int32, (cells, blocks), 0)
@@ -308,7 +328,8 @@
 
 def merge_kernel(per, cq, order_ref, *refs):
     arrived, (coarse_ref, first_ref, second_ref) = refs[:-3], refs[-3:]
-    arrived = arrived[:1] + arrived[:0:-1]
+    order = hop_order(len(arrived))
+    arrived = [arrived[0]] + [arrived[1 + order.index(hop)] for hop in range(1, len(arrived))]
     blocks, channels, cells = coarse_ref.shape
     tiles = len(arrived)
     packing = Packing(per, cq, channels)
@@ -446,7 +467,7 @@
         compiler_params=params(),
         name="order",
     )(route, sent[0])
-    arrived = [sent[0]] + [shifted(sent[hop], "tile", hop) for hop in range(1, tiles)]
+    arrived = [sent[0]] + [exchanged(sent[hop], "tile", hop) for hop in range(1, tiles)]
 
     block_shape = jax.ShapeDtypeStruct((channels, cells), BF16)
     coarse, first, second = pl.pallas_call(
@@ -456,7 +477,7 @@
         out_specs=(VMEM(), VMEM(), VMEM()),
         compiler_params=params(),
         name="merge",
-    )(order, arrived[0], *arrived[:0:-1])
+    )(order, arrived[0], *[arrived[hop] for hop in hop_order(tiles)])
 
     second = swapped(False, second, "tile")
     first = swapped(True, first, "tile")

time: 31.9 us -> 31.4 us (0.984)
  waiting for transfers between devices: 7.12 us -> 5.48 us
  starting transfers between devices: 11.7 us -> 12.9 us
    ppermute x4 -> x1, waiting for transfers between devices: 4.82 us -> 0.01 us  [shifted(): lax.ppermute(value, axis, [(i, (i + steps) % count) for i in range(count)])]
    ppermute x0 -> x3, starting transfers between devices: none -> 3.55 us  [exchanged(): return lax.ppermute(value, axis, pairs)]
    ppermute x0 -> x3, waiting for transfers between devices: none -> 2.78 us  [exchanged(): return lax.ppermute(value, axis, pairs)]
    ppermute x4 -> x1, starting transfers between devices: 3.96 us -> 1.55 us  [shifted(): lax.ppermute(value, axis, [(i, (i + steps) % count) for i in range(count)])]
    ppermute x4, waiting for transfers between devices: 2.3 us -> 2.7 us  [swapped(): return lax.ppermute(value, axis, pairs)]
where the time goes in v4:
time: 31.4 us; the launch traced here: 31.2 us
  starting transfers between devices  12.9 us (41%)
  Pallas kernels  10.6 us (34%)
  waiting for transfers between devices  5.48 us (17%)
  local copies, waits for them, and re-layouts  1.45 us (5%)
  between operations  0.79 us (3%)
    ppermute x4, starting transfers between devices, swapped(): return lax.ppermute(value, axis, pairs)  7.76 us
    pallas_call x1, Pallas kernels, per_device(): pl.pallas_call(early_kernel, out_shape=made, in_specs=given_specs, out_sp...  4.22 us
    ppermute x3, starting transfers between devices, exchanged(): return lax.ppermute(value, axis, pairs)  3.55 us
    pallas_call x1, Pallas kernels, per_device(): pl.pallas_call(late_kernel, out_shape=made + (sent_shape,) * tiles, in_sp...  2.82 us
    ppermute x3, waiting for transfers between devices, exchanged(): return lax.ppermute(value, axis, pairs)  2.78 us
    ppermute x4, waiting for transfers between devices, swapped(): return lax.ppermute(value, axis, pairs)  2.7 us
    ppermute x1, starting transfers between devices, shifted(): lax.ppermute(value, axis, [(i, (i + steps) % count) for i in range(count)])  1.55 us
    unnamed x22, local copies, waits for them, and re-layouts  1.45 us
  transfers between devices with their start and end apart: 8, of which 5 were waited for; matrix products, arithmetic and copies ran while one was open for 0% of the time, Pallas kernels for 19%

profile of v4, /device:TPU:0, one launch (start us, length us, event | category | flops | bytes accessed | tf_op | source)
XLA Modules:
  0.0 31.2 jit_solution(3584627436495915418)
XLA Ops:
  0.6 1.4 %copy-done = bf16[1,1,48,64,256]{4,3,2,1,0:T(8,128)(2,1)S(1)} copy-done((bf16[1,1,48,64,256]{4,3,2,1,0:T(8,128)(2,1)S(1)}, bf16[1,1,48,64,256]{4,3,2,1,0:T(8,128)(2,1)}, u32[]{:S(2)}) %copy-start) | copy-done | bytes 1572888
  2.1 0.2 cut.1
  2.3 3.1 %collective-permute-start = (bf16[2,64,256]{2,1,0:T(8,128)(2,1)S(1)}, bf16[2,64,256]{2,1,0:T(8,128)(2,1)S(1)}, u32[]{:S(2)}, u32[]{:S(2)}) collective-permute-start(bf16[2,64,256]{2,1,0:T(8,128)(2,1)S(1)} %get-tuple-element.17), channel_id=1, source_target_pairs={{0,4},{4,0},{8,12},{12,8},{1,5},{5,1},{9,13},{13,9},{2,6},{6,2},{1... | collective-permute-start | bytes 196616 | tf_op jit(solution)/shard_map/ppermute | solution.py:52
  5.4 2.5 %collective-permute-start.1 = (bf16[2,64,256]{2,1,0:T(8,128)(2,1)S(1)}, bf16[2,64,256]{2,1,0:T(8,128)(2,1)S(1)}, u32[]{:S(2)}, u32[]{:S(2)}) collective-permute-start(bf16[2,64,256]{2,1,0:T(8,128)(2,1)S(1)} %get-tuple-element.18), channel_id=1, source_target_pairs={{4,8},{8,4},{12,0},{0,12},{5,9},{9,5},{13,1},{1,13},{6,10},{10,6},... | collective-permute-start | bytes 196616 | tf_op jit(solution)/shard_map/ppermute | solution.py:52
  7.9 4.2 %early.1 = (bf16[208,64,256]{2,1,0:T(8,128)(2,1)S(1)}, bf16[48,64,256]{2,1,0:T(8,128)(2,1)}, f32[8,64,128]{2,1,0:T(8,128)S(1)}) custom-call(bf16[48,64,256]{2,1,0:T(8,128)(2,1)S(1)} %bitcast.8, bf16[4,256,256]{2,1,0:T(8,128)(2,1)S(1)} %copy-done.1, s32[5,1,48]{2,1,0:T(1,128)S(1)} %bitcast.12, s32[5,1,48]{2,1,0:T(1,128)S(1)} %bitcast.14, ...), custom_call_target="tpu_custom_call" | custom-call | flops 4000000000 | bytes 4000000 | tf_op jit(solution)/shard_map/early/pallas_call | solution.py:439
  12.2 2.8 %late.1 = (bf16[208,64,256]{2,1,0:T(8,128)(2,1)S(1)}, bf16[48,64,256]{2,1,0:T(8,128)(2,1)}, f32[8,64,128]{2,1,0:T(8,128)S(1)}, bf16[96,128]{1,0:T(8,128)(2,1)S(1...) custom-call(bf16[48,64,256]{2,1,0:T(8,128)(2,1)S(1)} %bitcast.9, ...), custom_call_target="tpu_custom_call", output_to_operand_aliasing={{0}: (10, {}), {1}: (11, {}), {2}: (12, {})} | custom-call | tf_op jit(solution)/shard_map/late/pallas_call | solution.py:451
  15.0 0.0 copy-start.2
  15.0 0.0 copy-start.3
  15.0 0.0 copy-start.9
  15.0 0.2 collective-permute-start.2
  15.2 2.9 %collective-permute-start.3 = (bf16[96,128]{1,0:T(8,128)(2,1)S(1)}, bf16[96,128]{1,0:T(8,128)(2,1)S(1)}, u32[]{:S(2)}, u32[]{:S(2)}) collective-permute-start(bf16[96,128]{1,0:T(8,128)(2,1)S(1)} %get-tuple-element.25), channel_id=1, source_target_pairs={{0,12},{4,8},{8,4},{12,0},{1,13},{5,9},{9,5},{13,1},{2,14},{6,10},... | collective-permute-start | bytes 73736 | tf_op jit(solution)/shard_map/ppermute | solution.py:68
  18.1 0.5 %collective-permute-start.4 = (bf16[96,128]{1,0:T(8,128)(2,1)S(1)}, bf16[96,128]{1,0:T(8,128)(2,1)S(1)}, u32[]{:S(2)}, u32[]{:S(2)}) collective-permute-start(bf16[96,128]{1,0:T(8,128)(2,1)S(1)} %get-tuple-element.26), channel_id=1, source_target_pairs={{0,4},{4,0},{8,12},{12,8},{1,5},{5,1},{9,13},{13,9},{2,6},{6,2},{1... | collective-permute-start | bytes 73736 | tf_op jit(solution)/shard_map/ppermute | solution.py:68
  18.6 0.6 %order.1.order_ref = bf16[768,768]{1,0:T(8,128)(2,1)S(1)} custom-call(s32[1,192]{1,0:T(1,128)S(1)} %copy-done.6, bf16[96,128]{1,0:T(8,128)(2,1)S(1)} %get-tuple-element.23.late_ref.refs_0_), custom_call_target="tpu_custom_call" | custom-call | tf_op jit(solution)/shard_map/order/pallas_call | solution.py:462
  19.2 0.9 %collective-permute-done.2.refs_1_ = bf16[96,128]{1,0:T(8,128)(2,1)S(1)} collective-permute-done((bf16[96,128]{1,0:T(8,128)(2,1)S(1)}, bf16[96,128]{1,0:T(8,128)(2,1)S(1)}, u32[]{:S(2)}, u32[]{:S(2)}) %collective-permute-start.2) | collective-permute-done | bytes 24608 | tf_op jit(solution)/shard_map/ppermute | solution.py:68
  20.1 0.8 %collective-permute-done.3.refs_2_ = bf16[96,128]{1,0:T(8,128)(2,1)S(1)} collective-permute-done((bf16[96,128]{1,0:T(8,128)(2,1)S(1)}, bf16[96,128]{1,0:T(8,128)(2,1)S(1)}, u32[]{:S(2)}, u32[]{:S(2)}) %collective-permute-start.3) | collective-permute-done | bytes 24608 | tf_op jit(solution)/shard_map/ppermute | solution.py:68
  20.9 1.0 %collective-permute-done.4.refs_3_ = bf16[96,128]{1,0:T(8,128)(2,1)S(1)} collective-permute-done((bf16[96,128]{1,0:T(8,128)(2,1)S(1)}, bf16[96,128]{1,0:T(8,128)(2,1)S(1)}, u32[]{:S(2)}, u32[]{:S(2)}) %collective-permute-start.4) | collective-permute-done | bytes 24608 | tf_op jit(solution)/shard_map/ppermute | solution.py:68
  22.0 0.3 %merge.1 = (bf16[3,64,256]{2,1,0:T(8,128)(2,1)S(1)}, bf16[64,256]{1,0:T(8,128)(2,1)S(1)}, bf16[64,256]{1,0:T(8,128)(2,1)S(1)}) custom-call(bf16[768,768]{1,0:T(8,128)(2,1)S(1)} %order.1.order_ref, bf16[96,128]{1,0:T(8,128)(2,1)S(1)} %get-tuple-element.23.late_ref.refs_0_, bf16[96,128]{1,0:T(8,128)(2,1)S(1)} %collective-permute-done.2.refs_1_, ...), custom_call_target="tpu_custom_call" | custom-call | tf_op jit(solution)/shard_map/merge/pallas_call | solution.py:473
  22.3 1.6 %collective-permute-start.5 = (bf16[3,64,256]{2,1,0:T(8,128)(2,1)S(1)}, bf16[3,64,256]{2,1,0:T(8,128)(2,1)S(1)}, u32[]{:S(2)}, u32[]{:S(2)}) collective-permute-start(bf16[3,64,256]{2,1,0:T(8,128)(2,1)S(1)} %get-tuple-element.27.coarse_ref), channel_id=1, source_target_pairs={{0,2},{2,0},{1,3},{3,1},{4,6},{6,4},{5,7},{7,5},{8,10},{10,8},{9,1... | collective-permute-start | bytes 294920 | tf_op jit(solution)/shard_map/ppermute | solution.py:34
  23.9 0.5 %collective-permute-start.6 = (bf16[64,256]{1,0:T(8,128)(2,1)S(1)}, bf16[64,256]{1,0:T(8,128)(2,1)S(1)}, u32[]{:S(2)}, u32[]{:S(2)}) collective-permute-start(bf16[64,256]{1,0:T(8,128)(2,1)S(1)} %get-tuple-element.28), channel_id=1, source_target_pairs={{0,4},{4,0},{8,12},{12,8},{1,5},{5,1},{9,13},{13,9},{2,6},{6,2},{1... | collective-permute-start | bytes 98312 | tf_op jit(solution)/shard_map/ppermute | solution.py:52
  24.3 1.7 %collective-permute-start.7 = (bf16[64,256]{1,0:T(8,128)(2,1)S(1)}, bf16[64,256]{1,0:T(8,128)(2,1)S(1)}, u32[]{:S(2)}, u32[]{:S(2)}) collective-permute-start(bf16[64,256]{1,0:T(8,128)(2,1)S(1)} %get-tuple-element.29), channel_id=1, source_target_pairs={{4,8},{8,4},{12,0},{0,12},{5,9},{9,5},{13,1},{1,13},{6,10},{10,6},... | collective-permute-start | bytes 98312 | tf_op jit(solution)/shard_map/ppermute | solution.py:52
  26.1 1.2 %inside.1 = (f32[3,64,256]{2,1,0:T(8,128)S(1)}, bf16[5,256,256]{2,1,0:T(8,128)(2,1)S(1)}) custom-call(s32[3,1,3]{2,1,0:T(1,128)S(1)} %bitcast.16, bf16[3,64,256]{2,1,0:T(8,128)(2,1)S(1)} %get-tuple-element.27.coarse_ref, bf16[4,256,256]{2,1,0:T(8,128)(2,1)S(1)} %copy-done.2, bf16[4,64,64]{2,1,0:T(8,128)(2,1)S(1)} %copy-done.3), custom_call_target="tpu_custom_call" | custom-call | tf_op jit(solution)/shard_map/inside/pallas_call | solution.py:485
  27.3 0.4 %collective-permute-done.6.first_ref = bf16[64,256]{1,0:T(8,128)(2,1)S(1)} collective-permute-done((bf16[64,256]{1,0:T(8,128)(2,1)S(1)}, bf16[64,256]{1,0:T(8,128)(2,1)S(1)}, u32[]{:S(2)}, u32[]{:S(2)}) %collective-permute-start.6) | collective-permute-done | bytes 32800 | tf_op jit(solution)/shard_map/ppermute | solution.py:52
  27.8 2.2 %collective-permute-done.7.second_ref = bf16[64,256]{1,0:T(8,128)(2,1)S(1)} collective-permute-done((bf16[64,256]{1,0:T(8,128)(2,1)S(1)}, bf16[64,256]{1,0:T(8,128)(2,1)S(1)}, u32[]{:S(2)}, u32[]{:S(2)}) %collective-permute-start.7) | collective-permute-done | bytes 32800 | tf_op jit(solution)/shard_map/ppermute | solution.py:52
  30.0 1.2 %coarse.1 = bf16[3,64,256]{2,1,0:T(8,128)(2,1)} custom-call(bf16[3,64,256]{2,1,0:T(8,128)(2,1)S(1)} %collective-permute-done.5.seam_ref, bf16[64,256]{1,0:T(8,128)(2,1)S(1)} %collective-permute-done.6.first_ref, bf16[64,256]{1,0:T(8,128)(2,1)S(1)} %collective-permute-done.7.second_ref, bf16[3,64,256]{2,1,0:T(8,128)(2,1)S(1)} %get-tuple-element.27.coarse_ref, ...), custom_call_target="tpu_custom_call" | custom-call | tf_op jit(solution)/shard_map/coarse/pallas_call | solution.py:496
  (21 shorter events, 0.0 us)
Async XLA Ops:
  0.6 1.4 %copy-start = (bf16[1,1,48,64,256]{4,3,2,1,0:T(8,128)(2,1)S(1)}, bf16[1,1,48,64,256]{4,3,2,1,0:T(8,128)(2,1)}, u32[]{:S(2)}) copy-start(bf16[1,1,48,64,256]{4,3,2,1,0:T(8,128)(2,1)} %param.11) | copy-start | bytes 4718596
  2.0 5.8 %copy-start.1 = (bf16[4,256,256]{2,1,0:T(8,128)(2,1)S(1)}, bf16[4,256,256]{2,1,0:T(8,128)(2,1)}, u32[]{:S(2)}) copy-start(bf16[4,256,256]{2,1,0:T(8,128)(2,1)} %table_ref.3) | copy-start | bytes 1572868
  2.0 5.8 %copy-start.4 = (bf16[5,64,64]{2,1,0:T(8,128)(2,1)S(1)}, bf16[5,64,64]{2,1,0:T(8,128)(2,1)}, u32[]{:S(2)}) copy-start(bf16[5,64,64]{2,1,0:T(8,128)(2,1)} %mix_ref.5) | copy-start | bytes 122884
  2.0 5.8 %copy-start.5 = (bf16[4,256,16]{1,2,0:T(8,128)(2,1)S(1)}, bf16[4,256,16]{1,2,0:T(8,128)(2,1)}, u32[]{:S(2)}) copy-start(bf16[4,256,16]{1,2,0:T(8,128)(2,1)} %param.16) | copy-start | bytes 98308
  2.0 5.8 %copy-start.6 = (s32[1,192]{1,0:T(1,128)S(1)}, s32[1,192]{1,0:T(1,128)}, u32[]{:S(2)}) copy-start(s32[1,192]{1,0:T(1,128)} %route_ref.5) | copy-start | bytes 2308
  2.1 5.8 %copy-start.7 = (s32[1,48,5]{1,0,2:T(1,128)S(1)}, s32[1,48,5]{1,0,2:T(1,128)}, u32[]{:S(2)}) copy-start(s32[1,48,5]{1,0,2:T(1,128)} %param.14) | copy-start | bytes 2884
  2.1 5.8 %copy-start.8 = (s32[1,48,5]{1,0,2:T(1,128)S(1)}, s32[1,48,5]{1,0,2:T(1,128)}, u32[]{:S(2)}) copy-start(s32[1,48,5]{1,0,2:T(1,128)} %param.15) | copy-start | bytes 2884
  2.1 5.8 %copy-start.10 = (s32[1,48]{1,0:T(1,128)S(1)}, s32[1,48]{1,0:T(1,128)}, u32[]{:S(2)}) copy-start(s32[1,48]{1,0:T(1,128)} %rcode_ref.3) | copy-start | bytes 580
  2.3 9.8 %collective-permute-start = (bf16[2,64,256]{2,1,0:T(8,128)(2,1)S(1)}, bf16[2,64,256]{2,1,0:T(8,128)(2,1)S(1)}, u32[]{:S(2)}, u32[]{:S(2)}) collective-permute-start(bf16[2,64,256]{2,1,0:T(8,128)(2,1)S(1)} %get-tuple-element.17), channel_id=1, source_target_pairs={{0,4},{4,0},{8,12},{12,8},{1,5},{5,1},{9,13},{13,9},{2,6},{6,2},{1... | collective-permute-start | bytes 196616 | tf_op jit(solution)/shard_map/ppermute | solution.py:52
  5.4 6.8 %collective-permute-start.1 = (bf16[2,64,256]{2,1,0:T(8,128)(2,1)S(1)}, bf16[2,64,256]{2,1,0:T(8,128)(2,1)S(1)}, u32[]{:S(2)}, u32[]{:S(2)}) collective-permute-start(bf16[2,64,256]{2,1,0:T(8,128)(2,1)S(1)} %get-tuple-element.18), channel_id=1, source_target_pairs={{4,8},{8,4},{12,0},{0,12},{5,9},{9,5},{13,1},{1,13},{6,10},{10,6},... | collective-permute-start | bytes 196616 | tf_op jit(solution)/shard_map/ppermute | solution.py:52
  15.0 11.1 %copy-start.2 = (bf16[4,256,256]{2,1,0:T(8,128)(2,1)S(1)}, bf16[4,256,256]{2,1,0:T(8,128)(2,1)}, u32[]{:S(2)}) copy-start(bf16[4,256,256]{2,1,0:T(8,128)(2,1)} %spatial_ref.1) | copy-start | bytes 1572868
  15.0 11.1 %copy-start.3 = (bf16[4,64,64]{2,1,0:T(8,128)(2,1)S(1)}, bf16[4,64,64]{2,1,0:T(8,128)(2,1)}, u32[]{:S(2)}) copy-start(bf16[4,64,64]{2,1,0:T(8,128)(2,1)} %mix_ref.7) | copy-start | bytes 98308
  15.0 11.0 %copy-start.9 = (s32[1,3,3]{2,0,1:T(1,128)S(1)}, s32[1,3,3]{2,0,1:T(1,128)}, u32[]{:S(2)}) copy-start(s32[1,3,3]{2,0,1:T(1,128)} %param.21) | copy-start | bytes 112
  15.0 5.1 %collective-permute-start.2 = (bf16[96,128]{1,0:T(8,128)(2,1)S(1)}, bf16[96,128]{1,0:T(8,128)(2,1)S(1)}, u32[]{:S(2)}, u32[]{:S(2)}) collective-permute-start(bf16[96,128]{1,0:T(8,128)(2,1)S(1)} %get-tuple-element.24), channel_id=1, source_target_pairs={{0,8},{4,12},{8,0},{12,4},{1,9},{5,13},{9,1},{13,5},{2,10},{6,14},... | collective-permute-start | bytes 73736 | tf_op jit(solution)/shard_map/ppermute | solution.py:68
  15.2 5.7 %collective-permute-start.3 = (bf16[96,128]{1,0:T(8,128)(2,1)S(1)}, bf16[96,128]{1,0:T(8,128)(2,1)S(1)}, u32[]{:S(2)}, u32[]{:S(2)}) collective-permute-start(bf16[96,128]{1,0:T(8,128)(2,1)S(1)} %get-tuple-element.25), channel_id=1, source_target_pairs={{0,12},{4,8},{8,4},{12,0},{1,13},{5,9},{9,5},{13,1},{2,14},{6,10},... | collective-permute-start | bytes 73736 | tf_op jit(solution)/shard_map/ppermute | solution.py:68
  18.1 3.8 %collective-permute-start.4 = (bf16[96,128]{1,0:T(8,128)(2,1)S(1)}, bf16[96,128]{1,0:T(8,128)(2,1)S(1)}, u32[]{:S(2)}, u32[]{:S(2)}) collective-permute-start(bf16[96,128]{1,0:T(8,128)(2,1)S(1)} %get-tuple-element.26), channel_id=1, source_target_pairs={{0,4},{4,0},{8,12},{12,8},{1,5},{5,1},{9,13},{13,9},{2,6},{6,2},{1... | collective-permute-start | bytes 73736 | tf_op jit(solution)/shard_map/ppermute | solution.py:68
  22.3 7.7 %collective-permute-start.5 = (bf16[3,64,256]{2,1,0:T(8,128)(2,1)S(1)}, bf16[3,64,256]{2,1,0:T(8,128)(2,1)S(1)}, u32[]{:S(2)}, u32[]{:S(2)}) collective-permute-start(bf16[3,64,256]{2,1,0:T(8,128)(2,1)S(1)} %get-tuple-element.27.coarse_ref), channel_id=1, source_target_pairs={{0,2},{2,0},{1,3},{3,1},{4,6},{6,4},{5,7},{7,5},{8,10},{10,8},{9,1... | collective-permute-start | bytes 294920 | tf_op jit(solution)/shard_map/ppermute | solution.py:34
  23.9 3.9 %collective-permute-start.6 = (bf16[64,256]{1,0:T(8,128)(2,1)S(1)}, bf16[64,256]{1,0:T(8,128)(2,1)S(1)}, u32[]{:S(2)}, u32[]{:S(2)}) collective-permute-start(bf16[64,256]{1,0:T(8,128)(2,1)S(1)} %get-tuple-element.28), channel_id=1, source_target_pairs={{0,4},{4,0},{8,12},{12,8},{1,5},{5,1},{9,13},{13,9},{2,6},{6,2},{1... | collective-permute-start | bytes 98312 | tf_op jit(solution)/shard_map/ppermute | solution.py:52
  24.3 5.7 %collective-permute-start.7 = (bf16[64,256]{1,0:T(8,128)(2,1)S(1)}, bf16[64,256]{1,0:T(8,128)(2,1)S(1)}, u32[]{:S(2)}, u32[]{:S(2)}) collective-permute-start(bf16[64,256]{1,0:T(8,128)(2,1)S(1)} %get-tuple-element.29), channel_id=1, source_target_pairs={{4,8},{8,4},{12,0},{0,12},{5,9},{9,5},{13,1},{1,13},{6,10},{10,6},... | collective-permute-start | bytes 98312 | tf_op jit(solution)/shard_map/ppermute | solution.py:52

commit v5 on v4

--- a/solution.py
+++ b/solution.py
@@ -10,7 +10,7 @@
 LANES = 128
 RIM = 2
 CHUNK = 8
-EARLY = 3
+EARLY = 4
 VMEM_MIB = 40
 
 SMEM = functools.partial(pl.BlockSpec, memory_space=pltpu.SMEM)
@@ -121,17 +121,11 @@
         return jnp.where(rank < self.full * self.lanes, whole, split)
 
 
-def cut_kernel(x_ref, first_ref, second_ref, sems):
+def cut_kernel(head_ref, tail_ref, first_ref, second_ref):
     right = faces_right()
-    last = x_ref.shape[0] - RIM
-    copies = [
-        pltpu.make_async_copy(x_ref.at[pl.ds(jnp.where(right, last, 0), RIM)], first_ref, sems.at[0]),
-        pltpu.make_async_copy(x_ref.at[pl.ds(jnp.where(right, 0, last), RIM)], second_ref, sems.at[1]),
-    ]
-    for copy in copies:
-        copy.start()
-    for copy in copies:
-        copy.wait()
+    head, tail = head_ref[...], tail_ref[...]
+    first_ref[...] = jnp.where(right, tail, head)
+    second_ref[...] = jnp.where(right, head, tail)
 
 
 class Level:
@@ -408,13 +402,12 @@
     first, second = pl.pallas_call(
         cut_kernel,
         out_shape=(rim_shape, rim_shape),
-        in_specs=[HBM()],
+        in_specs=[VMEM()] * 2,
         out_specs=(VMEM(),) * 2,
-        scratch_shapes=[pltpu.SemaphoreType.DMA((2,))],
         compiler_params=params(),
         cost_estimate=pl.CostEstimate(flops=4 * 10**9, bytes_accessed=10**6, transcendentals=0),
         name="cut",
-    )(x)
+    )(x[:RIM], x[count - RIM:])
     second = swapped(False, second, "tile")
     first = swapped(True, first, "tile")
 

time: 31.4 us -> 30.6 us (0.975)
  local copies, waits for them, and re-layouts: 1.45 us -> 0.95 us
    unnamed x22, local copies, waits for them, and re-layouts: 1.45 us -> 0.07 us
    slice x0 -> x1, local copies, waits for them, and re-layouts: none -> 0.88 us  [per_device(): x[count - RIM:]]
    pallas_call x1, Pallas kernels: 2.82 us -> 2.41 us  [per_device(): pl.pallas_call(late_kernel, out_shape=made + (sent_shape,) * tiles, in_sp...]
  transfers between devices with their start and end apart: 8 -> 8, of which waited for: 5 -> 5; matrix products, arithmetic and copies ran while one was open for 0% -> 0% of each run, Pallas kernels for 19% -> 21%
where the time goes in v5:
time: 30.6 us; the launch traced here: 30.5 us
  starting transfers between devices  12.6 us (41%)
  Pallas kernels  10.3 us (34%)
  waiting for transfers between devices  5.79 us (19%)
  local copies, waits for them, and re-layouts  0.95 us (3%)
  between operations  0.83 us (3%)
    ppermute x4, starting transfers between devices, swapped(): return lax.ppermute(value, axis, pairs)  7.45 us
    pallas_call x1, Pallas kernels, per_device(): pl.pallas_call(early_kernel, out_shape=made, in_specs=given_specs, out_sp...  4.52 us
    ppermute x3, starting transfers between devices, exchanged(): return lax.ppermute(value, axis, pairs)  3.55 us
    ppermute x4, waiting for transfers between devices, swapped(): return lax.ppermute(value, axis, pairs)  3.01 us
    ppermute x3, waiting for transfers between devices, exchanged(): return lax.ppermute(value, axis, pairs)  2.78 us
    pallas_call x1, Pallas kernels, per_device(): pl.pallas_call(late_kernel, out_shape=made + (sent_shape,) * tiles, in_sp...  2.41 us
    ppermute x1, starting transfers between devices, shifted(): lax.ppermute(value, axis, [(i, (i + steps) % count) for i in range(count)])  1.56 us
    pallas_call x1, Pallas kernels, per_device(): pl.pallas_call(inside_kernel, out_shape=(jax.ShapeDtypeStruct(coarse.shap...  1.25 us
  transfers between devices with their start and end apart: 8, of which 5 were waited for; matrix products, arithmetic and copies ran while one was open for 0% of the time, Pallas kernels for 21%

profile of v5, /device:TPU:0, one launch (start us, length us, event | category | flops | bytes accessed | tf_op | source)
XLA Modules:
  0.0 30.5 jit_solution(8743113201177743451)
XLA Ops:
  0.6 0.9 %slice_bitcast_fusion = (bf16[2,64,256]{2,1,0:T(8,128)(2,1)S(1)}, bf16[2,64,256]{2,1,0:T(8,128)(2,1)S(1)}) fusion(bf16[1,1,48,64,256]{4,3,2,1,0:T(8,128)(2,1)} %param.11), kind=kLoop, calls=%fused_computation | loop fusion | bytes 262144 | tf_op jit(solution)/shard_map/slice | solution.py:410
  1.5 0.0 copy-start
  1.5 0.0 copy-start.1
  1.6 0.0 copy-start.6
  1.6 0.0 copy-start.7
  1.6 3.1 %collective-permute-start = (bf16[2,64,256]{2,1,0:T(8,128)(2,1)S(1)}, bf16[2,64,256]{2,1,0:T(8,128)(2,1)S(1)}, u32[]{:S(2)}, u32[]{:S(2)}) collective-permute-start(bf16[2,64,256]{2,1,0:T(8,128)(2,1)S(1)} %get-tuple-element.17), channel_id=1, source_target_pairs={{0,4},{4,0},{8,12},{12,8},{1,5},{5,1},{9,13},{13,9},{2,6},{6,2},{1... | collective-permute-start | bytes 196616 | tf_op jit(solution)/shard_map/ppermute | solution.py:52
  4.7 2.5 %collective-permute-start.1 = (bf16[2,64,256]{2,1,0:T(8,128)(2,1)S(1)}, bf16[2,64,256]{2,1,0:T(8,128)(2,1)S(1)}, u32[]{:S(2)}, u32[]{:S(2)}) collective-permute-start(bf16[2,64,256]{2,1,0:T(8,128)(2,1)S(1)} %get-tuple-element.18), channel_id=1, source_target_pairs={{4,8},{8,4},{12,0},{0,12},{5,9},{9,5},{13,1},{1,13},{6,10},{10,6},... | collective-permute-start | bytes 196616 | tf_op jit(solution)/shard_map/ppermute | solution.py:52
  7.3 4.5 %early.1 = (bf16[208,64,256]{2,1,0:T(8,128)(2,1)S(1)}, bf16[48,64,256]{2,1,0:T(8,128)(2,1)}, f32[8,64,128]{2,1,0:T(8,128)S(1)}) custom-call(bf16[48,64,256]{2,1,0:T(8,128)(2,1)S(1)} %bitcast.11, bf16[4,256,256]{2,1,0:T(8,128)(2,1)S(1)} %copy-done.1, s32[5,1,48]{2,1,0:T(1,128)S(1)} %bitcast.15, s32[5,1,48]{2,1,0:T(1,128)S(1)} %bitcast.17, ...), custom_call_target="tpu_custom_call" | custom-call | flops 4000000000 | bytes 4000000 | tf_op jit(solution)/shard_map/early/pallas_call | solution.py:432
  11.8 2.4 %late.1 = (bf16[208,64,256]{2,1,0:T(8,128)(2,1)S(1)}, bf16[48,64,256]{2,1,0:T(8,128)(2,1)}, f32[8,64,128]{2,1,0:T(8,128)S(1)}, bf16[96,128]{1,0:T(8,128)(2,1)S(1...) custom-call(bf16[48,64,256]{2,1,0:T(8,128)(2,1)S(1)} %bitcast.12, ...), custom_call_target="tpu_custom_call", output_to_operand_aliasing={{0}: (10, {}), {1}: (11, {}), {2}: (12, {})} | custom-call | tf_op jit(solution)/shard_map/late/pallas_call | solution.py:444
  14.3 0.2 collective-permute-start.2
  14.5 2.9 %collective-permute-start.3 = (bf16[96,128]{1,0:T(8,128)(2,1)S(1)}, bf16[96,128]{1,0:T(8,128)(2,1)S(1)}, u32[]{:S(2)}, u32[]{:S(2)}) collective-permute-start(bf16[96,128]{1,0:T(8,128)(2,1)S(1)} %get-tuple-element.25), channel_id=1, source_target_pairs={{0,12},{4,8},{8,4},{12,0},{1,13},{5,9},{9,5},{13,1},{2,14},{6,10},... | collective-permute-start | bytes 73736 | tf_op jit(solution)/shard_map/ppermute | solution.py:68
  17.4 0.5 %collective-permute-start.4 = (bf16[96,128]{1,0:T(8,128)(2,1)S(1)}, bf16[96,128]{1,0:T(8,128)(2,1)S(1)}, u32[]{:S(2)}, u32[]{:S(2)}) collective-permute-start(bf16[96,128]{1,0:T(8,128)(2,1)S(1)} %get-tuple-element.26), channel_id=1, source_target_pairs={{0,4},{4,0},{8,12},{12,8},{1,5},{5,1},{9,13},{13,9},{2,6},{6,2},{1... | collective-permute-start | bytes 73736 | tf_op jit(solution)/shard_map/ppermute | solution.py:68
  17.8 0.6 %order.1.order_ref = bf16[768,768]{1,0:T(8,128)(2,1)S(1)} custom-call(s32[1,192]{1,0:T(1,128)S(1)} %copy-done.6, bf16[96,128]{1,0:T(8,128)(2,1)S(1)} %get-tuple-element.23.late_ref.refs_0_), custom_call_target="tpu_custom_call" | custom-call | tf_op jit(solution)/shard_map/order/pallas_call | solution.py:455
  18.4 0.9 %collective-permute-done.2.refs_1_ = bf16[96,128]{1,0:T(8,128)(2,1)S(1)} collective-permute-done((bf16[96,128]{1,0:T(8,128)(2,1)S(1)}, bf16[96,128]{1,0:T(8,128)(2,1)S(1)}, u32[]{:S(2)}, u32[]{:S(2)}) %collective-permute-start.2) | collective-permute-done | bytes 24608 | tf_op jit(solution)/shard_map/ppermute | solution.py:68
  19.3 0.8 %collective-permute-done.3.refs_2_ = bf16[96,128]{1,0:T(8,128)(2,1)S(1)} collective-permute-done((bf16[96,128]{1,0:T(8,128)(2,1)S(1)}, bf16[96,128]{1,0:T(8,128)(2,1)S(1)}, u32[]{:S(2)}, u32[]{:S(2)}) %collective-permute-start.3) | collective-permute-done | bytes 24608 | tf_op jit(solution)/shard_map/ppermute | solution.py:68
  20.1 1.1 %collective-permute-done.4.refs_3_ = bf16[96,128]{1,0:T(8,128)(2,1)S(1)} collective-permute-done((bf16[96,128]{1,0:T(8,128)(2,1)S(1)}, bf16[96,128]{1,0:T(8,128)(2,1)S(1)}, u32[]{:S(2)}, u32[]{:S(2)}) %collective-permute-start.4) | collective-permute-done | bytes 24608 | tf_op jit(solution)/shard_map/ppermute | solution.py:68
  21.2 0.3 %merge.1 = (bf16[3,64,256]{2,1,0:T(8,128)(2,1)S(1)}, bf16[64,256]{1,0:T(8,128)(2,1)S(1)}, bf16[64,256]{1,0:T(8,128)(2,1)S(1)}) custom-call(bf16[768,768]{1,0:T(8,128)(2,1)S(1)} %order.1.order_ref, bf16[96,128]{1,0:T(8,128)(2,1)S(1)} %get-tuple-element.23.late_ref.refs_0_, bf16[96,128]{1,0:T(8,128)(2,1)S(1)} %collective-permute-done.2.refs_1_, ...), custom_call_target="tpu_custom_call" | custom-call | tf_op jit(solution)/shard_map/merge/pallas_call | solution.py:466
  21.5 1.6 %collective-permute-start.5 = (bf16[3,64,256]{2,1,0:T(8,128)(2,1)S(1)}, bf16[3,64,256]{2,1,0:T(8,128)(2,1)S(1)}, u32[]{:S(2)}, u32[]{:S(2)}) collective-permute-start(bf16[3,64,256]{2,1,0:T(8,128)(2,1)S(1)} %get-tuple-element.27.coarse_ref), channel_id=1, source_target_pairs={{0,2},{2,0},{1,3},{3,1},{4,6},{6,4},{5,7},{7,5},{8,10},{10,8},{9,1... | collective-permute-start | bytes 294920 | tf_op jit(solution)/shard_map/ppermute | solution.py:34
  23.1 0.4 %collective-permute-start.6 = (bf16[64,256]{1,0:T(8,128)(2,1)S(1)}, bf16[64,256]{1,0:T(8,128)(2,1)S(1)}, u32[]{:S(2)}, u32[]{:S(2)}) collective-permute-start(bf16[64,256]{1,0:T(8,128)(2,1)S(1)} %get-tuple-element.28), channel_id=1, source_target_pairs={{0,4},{4,0},{8,12},{12,8},{1,5},{5,1},{9,13},{13,9},{2,6},{6,2},{1... | collective-permute-start | bytes 98312 | tf_op jit(solution)/shard_map/ppermute | solution.py:52
  23.5 1.4 %collective-permute-start.7 = (bf16[64,256]{1,0:T(8,128)(2,1)S(1)}, bf16[64,256]{1,0:T(8,128)(2,1)S(1)}, u32[]{:S(2)}, u32[]{:S(2)}) collective-permute-start(bf16[64,256]{1,0:T(8,128)(2,1)S(1)} %get-tuple-element.29), channel_id=1, source_target_pairs={{4,8},{8,4},{12,0},{0,12},{5,9},{9,5},{13,1},{1,13},{6,10},{10,6},... | collective-permute-start | bytes 98312 | tf_op jit(solution)/shard_map/ppermute | solution.py:52
  25.0 1.2 %inside.1 = (f32[3,64,256]{2,1,0:T(8,128)S(1)}, bf16[5,256,256]{2,1,0:T(8,128)(2,1)S(1)}) custom-call(s32[3,1,3]{2,1,0:T(1,128)S(1)} %bitcast.19, bf16[3,64,256]{2,1,0:T(8,128)(2,1)S(1)} %get-tuple-element.27.coarse_ref, bf16[4,256,256]{2,1,0:T(8,128)(2,1)S(1)} %copy-done.2, bf16[4,64,64]{2,1,0:T(8,128)(2,1)S(1)} %copy-done.3), custom_call_target="tpu_custom_call" | custom-call | tf_op jit(solution)/shard_map/inside/pallas_call | solution.py:478
  26.3 0.8 %collective-permute-done.6.first_ref = bf16[64,256]{1,0:T(8,128)(2,1)S(1)} collective-permute-done((bf16[64,256]{1,0:T(8,128)(2,1)S(1)}, bf16[64,256]{1,0:T(8,128)(2,1)S(1)}, u32[]{:S(2)}, u32[]{:S(2)}) %collective-permute-start.6) | collective-permute-done | bytes 32800 | tf_op jit(solution)/shard_map/ppermute | solution.py:52
  27.0 2.2 %collective-permute-done.7.second_ref = bf16[64,256]{1,0:T(8,128)(2,1)S(1)} collective-permute-done((bf16[64,256]{1,0:T(8,128)(2,1)S(1)}, bf16[64,256]{1,0:T(8,128)(2,1)S(1)}, u32[]{:S(2)}, u32[]{:S(2)}) %collective-permute-start.7) | collective-permute-done | bytes 32800 | tf_op jit(solution)/shard_map/ppermute | solution.py:52
  29.3 1.2 %coarse.1 = bf16[3,64,256]{2,1,0:T(8,128)(2,1)} custom-call(bf16[3,64,256]{2,1,0:T(8,128)(2,1)S(1)} %collective-permute-done.5.seam_ref, bf16[64,256]{1,0:T(8,128)(2,1)S(1)} %collective-permute-done.6.first_ref, bf16[64,256]{1,0:T(8,128)(2,1)S(1)} %collective-permute-done.7.second_ref, bf16[3,64,256]{2,1,0:T(8,128)(2,1)S(1)} %get-tuple-element.27.coarse_ref, ...), custom_call_target="tpu_custom_call" | custom-call | tf_op jit(solution)/shard_map/coarse/pallas_call | solution.py:489
  (22 shorter events, 0.1 us)
Async XLA Ops:
  1.5 5.7 %copy-start = (bf16[1,1,48,64,256]{4,3,2,1,0:T(8,128)(2,1)S(1)}, bf16[1,1,48,64,256]{4,3,2,1,0:T(8,128)(2,1)}, u32[]{:S(2)}) copy-start(bf16[1,1,48,64,256]{4,3,2,1,0:T(8,128)(2,1)} %param.11) | copy-start | bytes 4718596
  1.5 5.7 %copy-start.1 = (bf16[4,256,256]{2,1,0:T(8,128)(2,1)S(1)}, bf16[4,256,256]{2,1,0:T(8,128)(2,1)}, u32[]{:S(2)}) copy-start(bf16[4,256,256]{2,1,0:T(8,128)(2,1)} %table_ref.3) | copy-start | bytes 1572868
  1.5 5.7 %copy-start.4 = (bf16[5,64,64]{2,1,0:T(8,128)(2,1)S(1)}, bf16[5,64,64]{2,1,0:T(8,128)(2,1)}, u32[]{:S(2)}) copy-start(bf16[5,64,64]{2,1,0:T(8,128)(2,1)} %mix_ref.5) | copy-start | bytes 122884
  1.6 5.7 %copy-start.5 = (bf16[4,256,16]{1,2,0:T(8,128)(2,1)S(1)}, bf16[4,256,16]{1,2,0:T(8,128)(2,1)}, u32[]{:S(2)}) copy-start(bf16[4,256,16]{1,2,0:T(8,128)(2,1)} %param.16) | copy-start | bytes 98308
  1.6 5.7 %copy-start.6 = (s32[1,192]{1,0:T(1,128)S(1)}, s32[1,192]{1,0:T(1,128)}, u32[]{:S(2)}) copy-start(s32[1,192]{1,0:T(1,128)} %route_ref.5) | copy-start | bytes 2308
  1.6 5.7 %copy-start.7 = (s32[1,48,5]{1,0,2:T(1,128)S(1)}, s32[1,48,5]{1,0,2:T(1,128)}, u32[]{:S(2)}) copy-start(s32[1,48,5]{1,0,2:T(1,128)} %param.14) | copy-start | bytes 2884
  1.6 5.7 %copy-start.8 = (s32[1,48,5]{1,0,2:T(1,128)S(1)}, s32[1,48,5]{1,0,2:T(1,128)}, u32[]{:S(2)}) copy-start(s32[1,48,5]{1,0,2:T(1,128)} %param.15) | copy-start | bytes 2884
  1.6 5.7 %copy-start.10 = (s32[1,48]{1,0:T(1,128)S(1)}, s32[1,48]{1,0:T(1,128)}, u32[]{:S(2)}) copy-start(s32[1,48]{1,0:T(1,128)} %rcode_ref.3) | copy-start | bytes 580
  1.6 10.2 %collective-permute-start = (bf16[2,64,256]{2,1,0:T(8,128)(2,1)S(1)}, bf16[2,64,256]{2,1,0:T(8,128)(2,1)S(1)}, u32[]{:S(2)}, u32[]{:S(2)}) collective-permute-start(bf16[2,64,256]{2,1,0:T(8,128)(2,1)S(1)} %get-tuple-element.17), channel_id=1, source_target_pairs={{0,4},{4,0},{8,12},{12,8},{1,5},{5,1},{9,13},{13,9},{2,6},{6,2},{1... | collective-permute-start | bytes 196616 | tf_op jit(solution)/shard_map/ppermute | solution.py:52
  4.7 7.1 %collective-permute-start.1 = (bf16[2,64,256]{2,1,0:T(8,128)(2,1)S(1)}, bf16[2,64,256]{2,1,0:T(8,128)(2,1)S(1)}, u32[]{:S(2)}, u32[]{:S(2)}) collective-permute-start(bf16[2,64,256]{2,1,0:T(8,128)(2,1)S(1)} %get-tuple-element.18), channel_id=1, source_target_pairs={{4,8},{8,4},{12,0},{0,12},{5,9},{9,5},{13,1},{1,13},{6,10},{10,6},... | collective-permute-start | bytes 196616 | tf_op jit(solution)/shard_map/ppermute | solution.py:52
  14.2 10.8 %copy-start.2 = (bf16[4,256,256]{2,1,0:T(8,128)(2,1)S(1)}, bf16[4,256,256]{2,1,0:T(8,128)(2,1)}, u32[]{:S(2)}) copy-start(bf16[4,256,256]{2,1,0:T(8,128)(2,1)} %spatial_ref.1) | copy-start | bytes 1572868
  14.2 10.8 %copy-start.3 = (bf16[4,64,64]{2,1,0:T(8,128)(2,1)S(1)}, bf16[4,64,64]{2,1,0:T(8,128)(2,1)}, u32[]{:S(2)}) copy-start(bf16[4,64,64]{2,1,0:T(8,128)(2,1)} %mix_ref.7) | copy-start | bytes 98308
  14.3 10.7 %copy-start.9 = (s32[1,3,3]{2,0,1:T(1,128)S(1)}, s32[1,3,3]{2,0,1:T(1,128)}, u32[]{:S(2)}) copy-start(s32[1,3,3]{2,0,1:T(1,128)} %param.21) | copy-start | bytes 112
  14.3 5.1 %collective-permute-start.2 = (bf16[96,128]{1,0:T(8,128)(2,1)S(1)}, bf16[96,128]{1,0:T(8,128)(2,1)S(1)}, u32[]{:S(2)}, u32[]{:S(2)}) collective-permute-start(bf16[96,128]{1,0:T(8,128)(2,1)S(1)} %get-tuple-element.24), channel_id=1, source_target_pairs={{0,8},{4,12},{8,0},{12,4},{1,9},{5,13},{9,1},{13,5},{2,10},{6,14},... | collective-permute-start | bytes 73736 | tf_op jit(solution)/shard_map/ppermute | solution.py:68
  14.5 5.6 %collective-permute-start.3 = (bf16[96,128]{1,0:T(8,128)(2,1)S(1)}, bf16[96,128]{1,0:T(8,128)(2,1)S(1)}, u32[]{:S(2)}, u32[]{:S(2)}) collective-permute-start(bf16[96,128]{1,0:T(8,128)(2,1)S(1)} %get-tuple-element.25), channel_id=1, source_target_pairs={{0,12},{4,8},{8,4},{12,0},{1,13},{5,9},{9,5},{13,1},{2,14},{6,10},... | collective-permute-start | bytes 73736 | tf_op jit(solution)/shard_map/ppermute | solution.py:68
  17.4 3.8 %collective-permute-start.4 = (bf16[96,128]{1,0:T(8,128)(2,1)S(1)}, bf16[96,128]{1,0:T(8,128)(2,1)S(1)}, u32[]{:S(2)}, u32[]{:S(2)}) collective-permute-start(bf16[96,128]{1,0:T(8,128)(2,1)S(1)} %get-tuple-element.26), channel_id=1, source_target_pairs={{0,4},{4,0},{8,12},{12,8},{1,5},{5,1},{9,13},{13,9},{2,6},{6,2},{1... | collective-permute-start | bytes 73736 | tf_op jit(solution)/shard_map/ppermute | solution.py:68
  21.5 7.7 %collective-permute-start.5 = (bf16[3,64,256]{2,1,0:T(8,128)(2,1)S(1)}, bf16[3,64,256]{2,1,0:T(8,128)(2,1)S(1)}, u32[]{:S(2)}, u32[]{:S(2)}) collective-permute-start(bf16[3,64,256]{2,1,0:T(8,128)(2,1)S(1)} %get-tuple-element.27.coarse_ref), channel_id=1, source_target_pairs={{0,2},{2,0},{1,3},{3,1},{4,6},{6,4},{5,7},{7,5},{8,10},{10,8},{9,1... | collective-permute-start | bytes 294920 | tf_op jit(solution)/shard_map/ppermute | solution.py:34
  23.1 3.9 %collective-permute-start.6 = (bf16[64,256]{1,0:T(8,128)(2,1)S(1)}, bf16[64,256]{1,0:T(8,128)(2,1)S(1)}, u32[]{:S(2)}, u32[]{:S(2)}) collective-permute-start(bf16[64,256]{1,0:T(8,128)(2,1)S(1)} %get-tuple-element.28), channel_id=1, source_target_pairs={{0,4},{4,0},{8,12},{12,8},{1,5},{5,1},{9,13},{13,9},{2,6},{6,2},{1... | collective-permute-start | bytes 98312 | tf_op jit(solution)/shard_map/ppermute | solution.py:52
  23.5 5.7 %collective-permute-start.7 = (bf16[64,256]{1,0:T(8,128)(2,1)S(1)}, bf16[64,256]{1,0:T(8,128)(2,1)S(1)}, u32[]{:S(2)}, u32[]{:S(2)}) collective-permute-start(bf16[64,256]{1,0:T(8,128)(2,1)S(1)} %get-tuple-element.29), channel_id=1, source_target_pairs={{4,8},{8,4},{12,0},{0,12},{5,9},{9,5},{13,1},{1,13},{6,10},{10,6},... | collective-permute-start | bytes 98312 | tf_op jit(solution)/shard_map/ppermute | solution.py:52

commit v6 on v5

--- a/solution.py
+++ b/solution.py
@@ -198,18 +198,10 @@
     return CHUNK <= base < min((1 + EARLY) * CHUNK, count - CHUNK)
 
 
-def put_of(done_ref, skip_ref, sems):
-    def put(base):
-        part = pl.ds(base, CHUNK)
-        return pltpu.make_async_copy(done_ref.at[part], skip_ref.at[part], sems.at[base // CHUNK])
-
-    return put
-
-
 def early_kernel(
     x_ref, table_ref, nbr_ref, code_ref, rcode_ref, route_ref, mix_ref, restrict_ref,
-    y_ref, skip_ref, acc_ref,
-    nbr, code, rcode, route, mix, restrict, done_ref, counts_ref, in_sems, out_sems,
+    y_ref, done_ref, acc_ref,
+    nbr, code, rcode, route, mix, restrict, counts_ref, in_sems,
 ):
     count, channels, cells = x_ref.shape
     rotations = table_ref.shape[0]
@@ -227,26 +219,21 @@
     for copy in copies:
         copy.wait()
     level = Level((nbr, code, rcode, route), y_ref, x_ref, mix, restrict, done_ref, acc_ref, counts_ref)
-    put = put_of(done_ref, skip_ref, out_sems)
     for base in chunks_of(count):
         if is_early(base, count):
             level.run(base)
-            put(base).start()
             level.pack(base)
         else:
             level.pass_over(base)
-    for base in chunks_of(count):
-        if is_early(base, count):
-            put(base).wait()
 
 
 def late_kernel(
     x_ref, table_ref, nbr_ref, code_ref, rcode_ref, route_ref, mix_ref, restrict_ref,
-    first_ref, second_ref, y_in_ref, skip_in_ref, acc_in_ref, y_ref, skip_ref, acc_ref, *refs,
+    first_ref, second_ref, y_in_ref, done_in_ref, acc_in_ref, y_ref, done_ref, acc_ref, *refs,
 ):
-    sent_refs, refs = refs[:-10], refs[-10:]
-    nbr, code, rcode, route, mix, restrict, done_ref, counts_ref, in_sems, out_sems = refs
-    del y_in_ref, skip_in_ref, acc_in_ref
+    sent_refs, refs = refs[:-8], refs[-8:]
+    nbr, code, rcode, route, mix, restrict, counts_ref, in_sems = refs
+    del y_in_ref, done_in_ref, acc_in_ref
     count, channels, cells = x_ref.shape
     rotations = table_ref.shape[0]
     extended = count + 2 * RIM
@@ -266,13 +253,11 @@
     for copy in copies:
         copy.wait()
     level = Level((nbr, code, rcode, route), y_ref, x_ref, mix, restrict, done_ref, acc_ref, counts_ref)
-    put = put_of(done_ref, skip_ref, out_sems)
     for base in chunks_of(count):
         if is_early(base, count):
             level.pass_over(base)
         else:
             level.run(base)
-            put(base).start()
             level.pack(base)
     packing = Packing(count // level.tiles, level.cq, channels)
     half = LANES // 2
@@ -287,13 +272,18 @@
             lower = pltpu.roll(value[channels // 2:], half, axis=1)
             joined = jnp.where(lane < half, value[:channels // 2], lower)
             out[packing.full * channels:] = joined.astype(BF16)
-    for base in chunks_of(count):
-        if not is_early(base, count):
-            put(base).wait()
-
-
-def order_kernel(count, cq, channels, route_ref, late_ref, order_ref):
-    del late_ref
+
+
+def order_kernel(cq, route_ref, done_ref, order_ref, skip_ref, sems):
+    count, channels = done_ref.shape[:2]
+    copies = [
+        pltpu.make_async_copy(
+            done_ref.at[pl.ds(base, CHUNK)], skip_ref.at[pl.ds(base, CHUNK)], sems.at[base // CHUNK]
+        )
+        for base in chunks_of(count)
+    ]
+    for copy in copies:
+        copy.start()
     blocks = route_ref.shape[1]
     tiles = blocks // count
     packing = Packing(count // tiles, cq, channels)
@@ -318,6 +308,8 @@
     for row in range(0, order_ref.shape[0], step):
         index = row + lax.broadcasted_iota(jnp.int32, (step, cells), 0)
         order_ref[row:row + step] = jnp.where(index == across, 1.0, 0.0).astype(BF16)
+    for copy in copies:
+        copy.wait()
 
 
 def merge_kernel(per, cq, order_ref, *refs):
@@ -417,10 +409,8 @@
     shared = [pltpu.SMEM(a.shape, jnp.int32) for a in tables] + [
         pltpu.VMEM(conv_mix.shape, BF16),
         pltpu.VMEM(narrow.shape, BF16),
-        pltpu.VMEM(x.shape, BF16),
         pltpu.SMEM((tiles,), jnp.int32),
         pltpu.SemaphoreType.DMA((6,)),
-        pltpu.SemaphoreType.DMA((steps,)),
     ]
     made = (
         jax.ShapeDtypeStruct(y_shape, BF16),
@@ -429,11 +419,11 @@
     )
     given = (x, conv_spatial) + tables + (conv_mix, narrow)
     given_specs = [VMEM()] * 2 + [ANY()] * 6
-    y, skip, acc = pl.pallas_call(
+    y, done, acc = pl.pallas_call(
         early_kernel,
         out_shape=made,
         in_specs=given_specs,
-        out_specs=(VMEM(), ANY(), VMEM()),
+        out_specs=(VMEM(), VMEM(), VMEM()),
         scratch_shapes=shared,
         compiler_params=params(),
         cost_estimate=pl.CostEstimate(flops=4 * 10**9, bytes_accessed=4 * 10**6, transcendentals=10**6),
@@ -441,25 +431,29 @@
     )(*given)
 
     sent_shape = jax.ShapeDtypeStruct((packing.rows, LANES), BF16)
-    _, skip, _, *sent = pl.pallas_call(
+    _, done, _, *sent = pl.pallas_call(
         late_kernel,
         out_shape=made + (sent_shape,) * tiles,
-        in_specs=given_specs + [VMEM()] * 3 + [ANY(), VMEM()],
-        out_specs=(VMEM(), ANY(), VMEM()) + (VMEM(),) * tiles,
+        in_specs=given_specs + [VMEM()] * 5,
+        out_specs=(VMEM(),) * (3 + tiles),
         scratch_shapes=shared,
         input_output_aliases={10: 0, 11: 1, 12: 2},
         compiler_params=params(),
         name="late",
-    )(*given, first, second, y, skip, acc)
-
-    order = pl.pallas_call(
-        functools.partial(order_kernel, count, cq, channels),
-        out_shape=jax.ShapeDtypeStruct((packing.width(tiles), count * cq), BF16),
+    )(*given, first, second, y, done, acc)
+
+    order, skip = pl.pallas_call(
+        functools.partial(order_kernel, cq),
+        out_shape=(
+            jax.ShapeDtypeStruct((packing.width(tiles), count * cq), BF16),
+            jax.ShapeDtypeStruct(x.shape, BF16),
+        ),
         in_specs=[VMEM(), VMEM()],
-        out_specs=VMEM(),
+        out_specs=(VMEM(), ANY()),
+        scratch_shapes=[pltpu.SemaphoreType.DMA((steps,))],
         compiler_params=params(),
         name="order",
-    )(route, sent[0])
+    )(route, done)
     arrived = [sent[0]] + [exchanged(sent[hop], "tile", hop) for hop in range(1, tiles)]
 
     block_shape = jax.ShapeDtypeStruct((channels, cells), BF16)

time: 30.6 us -> 29.3 us (0.958)
  waiting for transfers between devices: 5.79 us -> 4.53 us
  Pallas kernels: 10.3 us -> 9.65 us
  starting transfers between devices: 12.6 us -> 13.2 us
    ppermute x4, waiting for transfers between devices: 3.01 us -> 2.35 us  [swapped(): return lax.ppermute(value, axis, pairs)]
    ppermute x4, starting transfers between devices: 7.45 us -> 8.11 us  [swapped(): return lax.ppermute(value, axis, pairs)]
    pallas_call x1, Pallas kernels: 4.52 us -> 3.87 us  [per_device(): pl.pallas_call(early_kernel, out_shape=made, in_specs=given_specs, out_sp...]
    pallas_call x1, Pallas kernels: 2.41 us -> 1.77 us  [per_device(): pl.pallas_call(late_kernel, out_shape=made + (sent_shape,) * tiles, in_sp...]
    ppermute x3, waiting for transfers between devices: 2.78 us -> 2.18 us  [exchanged(): return lax.ppermute(value, axis, pairs)]
    pallas_call x1, Pallas kernels: 0.59 us -> 1.18 us  [per_device(): pl.pallas_call(functools.partial(order_kernel, cq), out_shape=(jax.ShapeD...]
  transfers between devices with their start and end apart: 8 -> 8, of which waited for: 5 -> 5; matrix products, arithmetic and copies ran while one was open for 0% -> 0% of each run, Pallas kernels for 21% -> 22%
where the time goes in v6:
time: 29.3 us; the launch traced here: 29.2 us
  starting transfers between devices  13.2 us (45%)
  Pallas kernels  9.65 us (33%)
  waiting for transfers between devices  4.53 us (15%)
  local copies, waits for them, and re-layouts  0.95 us (3%)
  between operations  0.83 us (3%)
    ppermute x4, starting transfers between devices, swapped(): return lax.ppermute(value, axis, pairs)  8.11 us
    pallas_call x1, Pallas kernels, per_device(): pl.pallas_call(early_kernel, out_shape=made, in_specs=given_specs, out_sp...  3.87 us
    ppermute x3, starting transfers between devices, exchanged(): return lax.ppermute(value, axis, pairs)  3.55 us
    ppermute x4, waiting for transfers between devices, swapped(): return lax.ppermute(value, axis, pairs)  2.35 us
    ppermute x3, waiting for transfers between devices, exchanged(): return lax.ppermute(value, axis, pairs)  2.18 us
    pallas_call x1, Pallas kernels, per_device(): pl.pallas_call(late_kernel, out_shape=made + (sent_shape,) * tiles, in_sp...  1.77 us
    ppermute x1, starting transfers between devices, shifted(): lax.ppermute(value, axis, [(i, (i + steps) % count) for i in range(count)])  1.56 us
    pallas_call x1, Pallas kernels, per_device(): pl.pallas_call(inside_kernel, out_shape=(jax.ShapeDtypeStruct(coarse.shap...  1.25 us
  transfers between devices with their start and end apart: 8, of which 5 were waited for; matrix products, arithmetic and copies ran while one was open for 0% of the time, Pallas kernels for 22%

profile of v6, /device:TPU:0, one launch (start us, length us, event | category | flops | bytes accessed | tf_op | source)
XLA Modules:
  0.0 29.2 jit_solution(2923398518854943499)
XLA Ops:
  0.6 0.9 %slice_bitcast_fusion = (bf16[2,64,256]{2,1,0:T(8,128)(2,1)S(1)}, bf16[2,64,256]{2,1,0:T(8,128)(2,1)S(1)}) fusion(bf16[1,1,48,64,256]{4,3,2,1,0:T(8,128)(2,1)} %param.11), kind=kLoop, calls=%fused_computation | loop fusion | bytes 262144 | tf_op jit(solution)/shard_map/slice | solution.py:402
  1.5 0.0 copy-start
  1.6 0.0 copy-start.5
  1.6 0.0 copy-start.6
  1.6 0.0 copy-start.8
  1.6 3.1 %collective-permute-start = (bf16[2,64,256]{2,1,0:T(8,128)(2,1)S(1)}, bf16[2,64,256]{2,1,0:T(8,128)(2,1)S(1)}, u32[]{:S(2)}, u32[]{:S(2)}) collective-permute-start(bf16[2,64,256]{2,1,0:T(8,128)(2,1)S(1)} %get-tuple-element.19), channel_id=1, source_target_pairs={{0,4},{4,0},{8,12},{12,8},{1,5},{5,1},{9,13},{13,9},{2,6},{6,2},{1... | collective-permute-start | bytes 196616 | tf_op jit(solution)/shard_map/ppermute | solution.py:52
  4.7 2.5 %collective-permute-start.1 = (bf16[2,64,256]{2,1,0:T(8,128)(2,1)S(1)}, bf16[2,64,256]{2,1,0:T(8,128)(2,1)S(1)}, u32[]{:S(2)}, u32[]{:S(2)}) collective-permute-start(bf16[2,64,256]{2,1,0:T(8,128)(2,1)S(1)} %get-tuple-element.20), channel_id=1, source_target_pairs={{4,8},{8,4},{12,0},{0,12},{5,9},{9,5},{13,1},{1,13},{6,10},{10,6},... | collective-permute-start | bytes 196616 | tf_op jit(solution)/shard_map/ppermute | solution.py:52
  7.3 3.9 %early.1 = (bf16[208,64,256]{2,1,0:T(8,128)(2,1)S(1)}, bf16[48,64,256]{2,1,0:T(8,128)(2,1)S(1)}, f32[8,64,128]{2,1,0:T(8,128)S(1)}) custom-call(bf16[48,64,256]{2,1,0:T(8,128)(2,1)S(1)} %bitcast.11, bf16[4,256,256]{2,1,0:T(8,128)(2,1)S(1)} %copy-done.1, s32[5,1,48]{2,1,0:T(1,128)S(1)} %bitcast.15, s32[5,1,48]{2,1,0:T(1,128)S(1)} %bitcast.17, ...), custom_call_target="tpu_custom_call" | custom-call | flops 4000000000 | bytes 4000000 | tf_op jit(solution)/shard_map/early/pallas_call | solution.py:422
  11.2 1.8 %late.1 = (bf16[208,64,256]{2,1,0:T(8,128)(2,1)S(1)}, bf16[48,64,256]{2,1,0:T(8,128)(2,1)S(1)}, f32[8,64,128]{2,1,0:T(8,128)S(1)}, bf16[96,128]{1,0:T(8,128)(2,1...) custom-call(bf16[48,64,256]{2,1,0:T(8,128)(2,1)S(1)} %bitcast.12, ...), custom_call_target="tpu_custom_call", output_to_operand_aliasing={{0}: (10, {}), {1}: (11, {}), {2}: (12, {})} | custom-call | tf_op jit(solution)/shard_map/late/pallas_call | solution.py:434
  13.0 0.6 %collective-permute-start.2 = (bf16[96,128]{1,0:T(8,128)(2,1)S(1)}, bf16[96,128]{1,0:T(8,128)(2,1)S(1)}, u32[]{:S(2)}, u32[]{:S(2)}) collective-permute-start(bf16[96,128]{1,0:T(8,128)(2,1)S(1)} %get-tuple-element.28), channel_id=1, source_target_pairs={{0,8},{4,12},{8,0},{12,4},{1,9},{5,13},{9,1},{13,5},{2,10},{6,14},... | collective-permute-start | bytes 73736 | tf_op jit(solution)/shard_map/ppermute | solution.py:68
  13.5 2.5 %collective-permute-start.3 = (bf16[96,128]{1,0:T(8,128)(2,1)S(1)}, bf16[96,128]{1,0:T(8,128)(2,1)S(1)}, u32[]{:S(2)}, u32[]{:S(2)}) collective-permute-start(bf16[96,128]{1,0:T(8,128)(2,1)S(1)} %get-tuple-element.29), channel_id=1, source_target_pairs={{0,12},{4,8},{8,4},{12,0},{1,13},{5,9},{9,5},{13,1},{2,14},{6,10},... | collective-permute-start | bytes 73736 | tf_op jit(solution)/shard_map/ppermute | solution.py:68
  16.1 0.5 %collective-permute-start.4 = (bf16[96,128]{1,0:T(8,128)(2,1)S(1)}, bf16[96,128]{1,0:T(8,128)(2,1)S(1)}, u32[]{:S(2)}, u32[]{:S(2)}) collective-permute-start(bf16[96,128]{1,0:T(8,128)(2,1)S(1)} %get-tuple-element.30), channel_id=1, source_target_pairs={{0,4},{4,0},{8,12},{12,8},{1,5},{5,1},{9,13},{13,9},{2,6},{6,2},{1... | collective-permute-start | bytes 73736 | tf_op jit(solution)/shard_map/ppermute | solution.py:68
  16.5 1.2 %order.1 = (bf16[768,768]{1,0:T(8,128)(2,1)S(1)}, bf16[48,64,256]{2,1,0:T(8,128)(2,1)}) custom-call(s32[1,192]{1,0:T(1,128)S(1)} %copy-done.6, bf16[48,64,256]{2,1,0:T(8,128)(2,1)S(1)} %get-tuple-element.24.done_ref), custom_call_target="tpu_custom_call" | custom-call | tf_op jit(solution)/shard_map/order/pallas_call | solution.py:445
  17.7 0.3 %collective-permute-done.2.refs_1_ = bf16[96,128]{1,0:T(8,128)(2,1)S(1)} collective-permute-done((bf16[96,128]{1,0:T(8,128)(2,1)S(1)}, bf16[96,128]{1,0:T(8,128)(2,1)S(1)}, u32[]{:S(2)}, u32[]{:S(2)}) %collective-permute-start.2) | collective-permute-done | bytes 24608 | tf_op jit(solution)/shard_map/ppermute | solution.py:68
  18.0 1.2 %collective-permute-done.3.refs_2_ = bf16[96,128]{1,0:T(8,128)(2,1)S(1)} collective-permute-done((bf16[96,128]{1,0:T(8,128)(2,1)S(1)}, bf16[96,128]{1,0:T(8,128)(2,1)S(1)}, u32[]{:S(2)}, u32[]{:S(2)}) %collective-permute-start.3) | collective-permute-done | bytes 24608 | tf_op jit(solution)/shard_map/ppermute | solution.py:68
  19.2 0.7 %collective-permute-done.4.refs_3_ = bf16[96,128]{1,0:T(8,128)(2,1)S(1)} collective-permute-done((bf16[96,128]{1,0:T(8,128)(2,1)S(1)}, bf16[96,128]{1,0:T(8,128)(2,1)S(1)}, u32[]{:S(2)}, u32[]{:S(2)}) %collective-permute-start.4) | collective-permute-done | bytes 24608 | tf_op jit(solution)/shard_map/ppermute | solution.py:68
  19.9 0.3 %merge.1 = (bf16[3,64,256]{2,1,0:T(8,128)(2,1)S(1)}, bf16[64,256]{1,0:T(8,128)(2,1)S(1)}, bf16[64,256]{1,0:T(8,128)(2,1)S(1)}) custom-call(bf16[768,768]{1,0:T(8,128)(2,1)S(1)} %get-tuple-element.26.order_ref, bf16[96,128]{1,0:T(8,128)(2,1)S(1)} %get-tuple-element.27.refs_0_, bf16[96,128]{1,0:T(8,128)(2,1)S(1)} %collective-permute-done.2.refs_1_, ...), custom_call_target="tpu_custom_call" | custom-call | tf_op jit(solution)/shard_map/merge/pallas_call | solution.py:460
  20.3 1.6 %collective-permute-start.5 = (bf16[3,64,256]{2,1,0:T(8,128)(2,1)S(1)}, bf16[3,64,256]{2,1,0:T(8,128)(2,1)S(1)}, u32[]{:S(2)}, u32[]{:S(2)}) collective-permute-start(bf16[3,64,256]{2,1,0:T(8,128)(2,1)S(1)} %get-tuple-element.31.coarse_ref), channel_id=1, source_target_pairs={{0,2},{2,0},{1,3},{3,1},{4,6},{6,4},{5,7},{7,5},{8,10},{10,8},{9,1... | collective-permute-start | bytes 294920 | tf_op jit(solution)/shard_map/ppermute | solution.py:34
  21.8 0.4 %collective-permute-start.6 = (bf16[64,256]{1,0:T(8,128)(2,1)S(1)}, bf16[64,256]{1,0:T(8,128)(2,1)S(1)}, u32[]{:S(2)}, u32[]{:S(2)}) collective-permute-start(bf16[64,256]{1,0:T(8,128)(2,1)S(1)} %get-tuple-element.32), channel_id=1, source_target_pairs={{0,4},{4,0},{8,12},{12,8},{1,5},{5,1},{9,13},{13,9},{2,6},{6,2},{1... | collective-permute-start | bytes 98312 | tf_op jit(solution)/shard_map/ppermute | solution.py:52
  22.3 2.1 %collective-permute-start.7 = (bf16[64,256]{1,0:T(8,128)(2,1)S(1)}, bf16[64,256]{1,0:T(8,128)(2,1)S(1)}, u32[]{:S(2)}, u32[]{:S(2)}) collective-permute-start(bf16[64,256]{1,0:T(8,128)(2,1)S(1)} %get-tuple-element.33), channel_id=1, source_target_pairs={{4,8},{8,4},{12,0},{0,12},{5,9},{9,5},{13,1},{1,13},{6,10},{10,6},... | collective-permute-start | bytes 98312 | tf_op jit(solution)/shard_map/ppermute | solution.py:52
  24.4 1.2 %inside.1 = (f32[3,64,256]{2,1,0:T(8,128)S(1)}, bf16[5,256,256]{2,1,0:T(8,128)(2,1)S(1)}) custom-call(s32[3,1,3]{2,1,0:T(1,128)S(1)} %bitcast.19, bf16[3,64,256]{2,1,0:T(8,128)(2,1)S(1)} %get-tuple-element.31.coarse_ref, bf16[4,256,256]{2,1,0:T(8,128)(2,1)S(1)} %copy-done.2, bf16[4,64,64]{2,1,0:T(8,128)(2,1)S(1)} %copy-done.3), custom_call_target="tpu_custom_call" | custom-call | tf_op jit(solution)/shard_map/inside/pallas_call | solution.py:472
  25.6 0.1 collective-permute-done.6.first_ref
  25.7 2.2 %collective-permute-done.7.second_ref = bf16[64,256]{1,0:T(8,128)(2,1)S(1)} collective-permute-done((bf16[64,256]{1,0:T(8,128)(2,1)S(1)}, bf16[64,256]{1,0:T(8,128)(2,1)S(1)}, u32[]{:S(2)}, u32[]{:S(2)}) %collective-permute-start.7) | collective-permute-done | bytes 32800 | tf_op jit(solution)/shard_map/ppermute | solution.py:52
  28.0 1.2 %coarse.1 = bf16[3,64,256]{2,1,0:T(8,128)(2,1)} custom-call(bf16[3,64,256]{2,1,0:T(8,128)(2,1)S(1)} %collective-permute-done.5.seam_ref, bf16[64,256]{1,0:T(8,128)(2,1)S(1)} %collective-permute-done.6.first_ref, bf16[64,256]{1,0:T(8,128)(2,1)S(1)} %collective-permute-done.7.second_ref, bf16[3,64,256]{2,1,0:T(8,128)(2,1)S(1)} %get-tuple-element.31.coarse_ref, ...), custom_call_target="tpu_custom_call" | custom-call | tf_op jit(solution)/shard_map/coarse/pallas_call | solution.py:483
  (22 shorter events, 0.1 us)
Async XLA Ops:
  1.5 5.7 %copy-start = (bf16[1,1,48,64,256]{4,3,2,1,0:T(8,128)(2,1)S(1)}, bf16[1,1,48,64,256]{4,3,2,1,0:T(8,128)(2,1)}, u32[]{:S(2)}) copy-start(bf16[1,1,48,64,256]{4,3,2,1,0:T(8,128)(2,1)} %param.11) | copy-start | bytes 4718596
  1.5 5.7 %copy-start.1 = (bf16[4,256,256]{2,1,0:T(8,128)(2,1)S(1)}, bf16[4,256,256]{2,1,0:T(8,128)(2,1)}, u32[]{:S(2)}) copy-start(bf16[4,256,256]{2,1,0:T(8,128)(2,1)} %table_ref.3) | copy-start | bytes 1572868
  1.5 5.7 %copy-start.4 = (bf16[5,64,64]{2,1,0:T(8,128)(2,1)S(1)}, bf16[5,64,64]{2,1,0:T(8,128)(2,1)}, u32[]{:S(2)}) copy-start(bf16[5,64,64]{2,1,0:T(8,128)(2,1)} %mix_ref.5) | copy-start | bytes 122884
  1.6 5.7 %copy-start.5 = (bf16[4,256,16]{1,2,0:T(8,128)(2,1)S(1)}, bf16[4,256,16]{1,2,0:T(8,128)(2,1)}, u32[]{:S(2)}) copy-start(bf16[4,256,16]{1,2,0:T(8,128)(2,1)} %param.16) | copy-start | bytes 98308
  1.6 5.7 %copy-start.6 = (s32[1,192]{1,0:T(1,128)S(1)}, s32[1,192]{1,0:T(1,128)}, u32[]{:S(2)}) copy-start(s32[1,192]{1,0:T(1,128)} %route_ref.5) | copy-start | bytes 2308
  1.6 5.7 %copy-start.7 = (s32[1,48,5]{1,0,2:T(1,128)S(1)}, s32[1,48,5]{1,0,2:T(1,128)}, u32[]{:S(2)}) copy-start(s32[1,48,5]{1,0,2:T(1,128)} %param.14) | copy-start | bytes 2884
  1.6 5.7 %copy-start.8 = (s32[1,48,5]{1,0,2:T(1,128)S(1)}, s32[1,48,5]{1,0,2:T(1,128)}, u32[]{:S(2)}) copy-start(s32[1,48,5]{1,0,2:T(1,128)} %param.15) | copy-start | bytes 2884
  1.6 5.7 %copy-start.10 = (s32[1,48]{1,0:T(1,128)S(1)}, s32[1,48]{1,0:T(1,128)}, u32[]{:S(2)}) copy-start(s32[1,48]{1,0:T(1,128)} %rcode_ref.3) | copy-start | bytes 580
  1.6 9.5 %collective-permute-start = (bf16[2,64,256]{2,1,0:T(8,128)(2,1)S(1)}, bf16[2,64,256]{2,1,0:T(8,128)(2,1)S(1)}, u32[]{:S(2)}, u32[]{:S(2)}) collective-permute-start(bf16[2,64,256]{2,1,0:T(8,128)(2,1)S(1)} %get-tuple-element.19), channel_id=1, source_target_pairs={{0,4},{4,0},{8,12},{12,8},{1,5},{5,1},{9,13},{13,9},{2,6},{6,2},{1... | collective-permute-start | bytes 196616 | tf_op jit(solution)/shard_map/ppermute | solution.py:52
  4.7 6.4 %collective-permute-start.1 = (bf16[2,64,256]{2,1,0:T(8,128)(2,1)S(1)}, bf16[2,64,256]{2,1,0:T(8,128)(2,1)S(1)}, u32[]{:S(2)}, u32[]{:S(2)}) collective-permute-start(bf16[2,64,256]{2,1,0:T(8,128)(2,1)S(1)} %get-tuple-element.20), channel_id=1, source_target_pairs={{4,8},{8,4},{12,0},{0,12},{5,9},{9,5},{13,1},{1,13},{6,10},{10,6},... | collective-permute-start | bytes 196616 | tf_op jit(solution)/shard_map/ppermute | solution.py:52
  12.9 11.4 %copy-start.2 = (bf16[4,256,256]{2,1,0:T(8,128)(2,1)S(1)}, bf16[4,256,256]{2,1,0:T(8,128)(2,1)}, u32[]{:S(2)}) copy-start(bf16[4,256,256]{2,1,0:T(8,128)(2,1)} %spatial_ref.1) | copy-start | bytes 1572868
  13.0 11.4 %copy-start.3 = (bf16[4,64,64]{2,1,0:T(8,128)(2,1)S(1)}, bf16[4,64,64]{2,1,0:T(8,128)(2,1)}, u32[]{:S(2)}) copy-start(bf16[4,64,64]{2,1,0:T(8,128)(2,1)} %mix_ref.7) | copy-start | bytes 98308
  13.0 11.4 %copy-start.9 = (s32[1,3,3]{2,0,1:T(1,128)S(1)}, s32[1,3,3]{2,0,1:T(1,128)}, u32[]{:S(2)}) copy-start(s32[1,3,3]{2,0,1:T(1,128)} %param.21) | copy-start | bytes 112
  13.0 5.1 %collective-permute-start.2 = (bf16[96,128]{1,0:T(8,128)(2,1)S(1)}, bf16[96,128]{1,0:T(8,128)(2,1)S(1)}, u32[]{:S(2)}, u32[]{:S(2)}) collective-permute-start(bf16[96,128]{1,0:T(8,128)(2,1)S(1)} %get-tuple-element.28), channel_id=1, source_target_pairs={{0,8},{4,12},{8,0},{12,4},{1,9},{5,13},{9,1},{13,5},{2,10},{6,14},... | collective-permute-start | bytes 73736 | tf_op jit(solution)/shard_map/ppermute | solution.py:68
  13.5 5.7 %collective-permute-start.3 = (bf16[96,128]{1,0:T(8,128)(2,1)S(1)}, bf16[96,128]{1,0:T(8,128)(2,1)S(1)}, u32[]{:S(2)}, u32[]{:S(2)}) collective-permute-start(bf16[96,128]{1,0:T(8,128)(2,1)S(1)} %get-tuple-element.29), channel_id=1, source_target_pairs={{0,12},{4,8},{8,4},{12,0},{1,13},{5,9},{9,5},{13,1},{2,14},{6,10},... | collective-permute-start | bytes 73736 | tf_op jit(solution)/shard_map/ppermute | solution.py:68
  16.1 3.8 %collective-permute-start.4 = (bf16[96,128]{1,0:T(8,128)(2,1)S(1)}, bf16[96,128]{1,0:T(8,128)(2,1)S(1)}, u32[]{:S(2)}, u32[]{:S(2)}) collective-permute-start(bf16[96,128]{1,0:T(8,128)(2,1)S(1)} %get-tuple-element.30), channel_id=1, source_target_pairs={{0,4},{4,0},{8,12},{12,8},{1,5},{5,1},{9,13},{13,9},{2,6},{6,2},{1... | collective-permute-start | bytes 73736 | tf_op jit(solution)/shard_map/ppermute | solution.py:68
  20.3 7.7 %collective-permute-start.5 = (bf16[3,64,256]{2,1,0:T(8,128)(2,1)S(1)}, bf16[3,64,256]{2,1,0:T(8,128)(2,1)S(1)}, u32[]{:S(2)}, u32[]{:S(2)}) collective-permute-start(bf16[3,64,256]{2,1,0:T(8,128)(2,1)S(1)} %get-tuple-element.31.coarse_ref), channel_id=1, source_target_pairs={{0,2},{2,0},{1,3},{3,1},{4,6},{6,4},{5,7},{7,5},{8,10},{10,8},{9,1... | collective-permute-start | bytes 294920 | tf_op jit(solution)/shard_map/ppermute | solution.py:34
  21.8 3.9 %collective-permute-start.6 = (bf16[64,256]{1,0:T(8,128)(2,1)S(1)}, bf16[64,256]{1,0:T(8,128)(2,1)S(1)}, u32[]{:S(2)}, u32[]{:S(2)}) collective-permute-start(bf16[64,256]{1,0:T(8,128)(2,1)S(1)} %get-tuple-element.32), channel_id=1, source_target_pairs={{0,4},{4,0},{8,12},{12,8},{1,5},{5,1},{9,13},{13,9},{2,6},{6,2},{1... | collective-permute-start | bytes 98312 | tf_op jit(solution)/shard_map/ppermute | solution.py:52
  22.3 5.7 %collective-permute-start.7 = (bf16[64,256]{1,0:T(8,128)(2,1)S(1)}, bf16[64,256]{1,0:T(8,128)(2,1)S(1)}, u32[]{:S(2)}, u32[]{:S(2)}) collective-permute-start(bf16[64,256]{1,0:T(8,128)(2,1)S(1)} %get-tuple-element.33), channel_id=1, source_target_pairs={{4,8},{8,4},{12,0},{0,12},{5,9},{9,5},{13,1},{1,13},{6,10},{10,6},... | collective-permute-start | bytes 98312 | tf_op jit(solution)/shard_map/ppermute | solution.py:52

commit v7 on v6

--- a/solution.py
+++ b/solution.py
@@ -355,7 +355,7 @@
     table_ref[1] = spatial_ref[code_ref[blocks - 1, 0, 1]]
 
 
-def coarse_kernel(seam_ref, first_ref, second_ref, coarse_ref, total_ref, table_ref, mix_ref, out_ref):
+def coarse_kernel(seam_ref, second_ref, first_ref, coarse_ref, total_ref, table_ref, mix_ref, out_ref):
     blocks = coarse_ref.shape[0]
     right = faces_right()
     left_rows = jnp.where(right, second_ref[...], first_ref[...])
@@ -487,7 +487,7 @@
         out_specs=VMEM(),
         compiler_params=params(),
         name="coarse",
-    )(seam, first, second, coarse, total, tables, coarse_mix)
+    )(seam, second, first, coarse, total, tables, coarse_mix)
     return (skip[None, None], coarse_out[None, None])
 
 

time: 29.3 us -> 29.3 us (level)
  starting transfers between devices: 13.2 us -> 12.5 us
  waiting for transfers between devices: 4.53 us -> 5.17 us
    ppermute x4, starting transfers between devices: 8.11 us -> 7.37 us  [swapped(): return lax.ppermute(value, axis, pairs)]
    ppermute x4, waiting for transfers between devices: 2.35 us -> 2.99 us  [swapped(): return lax.ppermute(value, axis, pairs)]
where the time goes in v7:
time: 29.3 us; the launch traced here: 29.1 us
  starting transfers between devices  12.5 us (43%)
  Pallas kernels  9.65 us (33%)
  waiting for transfers between devices  5.17 us (18%)
  local copies, waits for them, and re-layouts  0.95 us (3%)
  between operations  0.84 us (3%)
    ppermute x4, starting transfers between devices, swapped(): return lax.ppermute(value, axis, pairs)  7.37 us
    pallas_call x1, Pallas kernels, per_device(): pl.pallas_call(early_kernel, out_shape=made, in_specs=given_specs, out_sp...  3.87 us
    ppermute x3, starting transfers between devices, exchanged(): return lax.ppermute(value, axis, pairs)  3.55 us
    ppermute x4, waiting for transfers between devices, swapped(): return lax.ppermute(value, axis, pairs)  2.99 us
    ppermute x3, waiting for transfers between devices, exchanged(): return lax.ppermute(value, axis, pairs)  2.18 us
    pallas_call x1, Pallas kernels, per_device(): pl.pallas_call(late_kernel, out_shape=made + (sent_shape,) * tiles, in_sp...  1.77 us
    ppermute x1, starting transfers between devices, shifted(): lax.ppermute(value, axis, [(i, (i + steps) % count) for i in range(count)])  1.56 us
    pallas_call x1, Pallas kernels, per_device(): pl.pallas_call(inside_kernel, out_shape=(jax.ShapeDtypeStruct(coarse.shap...  1.25 us
  transfers between devices with their start and end apart: 8, of which 5 were waited for; matrix products, arithmetic and copies ran while one was open for 0% of the time, Pallas kernels for 22%

profile of v7, /device:TPU:0, one launch (start us, length us, event | category | flops | bytes accessed | tf_op | source)
XLA Modules:
  0.0 29.1 jit_solution(10870852710969250791)
XLA Ops:
  0.6 0.9 %slice_bitcast_fusion = (bf16[2,64,256]{2,1,0:T(8,128)(2,1)S(1)}, bf16[2,64,256]{2,1,0:T(8,128)(2,1)S(1)}) fusion(bf16[1,1,48,64,256]{4,3,2,1,0:T(8,128)(2,1)} %param.11), kind=kLoop, calls=%fused_computation | loop fusion | bytes 262144 | tf_op jit(solution)/shard_map/slice | solution.py:402
  1.5 0.0 copy-start
  1.5 0.0 copy-start.1
  1.6 0.0 copy-start.6
  1.6 0.0 copy-start.7
  1.6 0.0 copy-start.10
  1.6 3.1 %collective-permute-start = (bf16[2,64,256]{2,1,0:T(8,128)(2,1)S(1)}, bf16[2,64,256]{2,1,0:T(8,128)(2,1)S(1)}, u32[]{:S(2)}, u32[]{:S(2)}) collective-permute-start(bf16[2,64,256]{2,1,0:T(8,128)(2,1)S(1)} %get-tuple-element.19), channel_id=1, source_target_pairs={{0,4},{4,0},{8,12},{12,8},{1,5},{5,1},{9,13},{13,9},{2,6},{6,2},{1... | collective-permute-start | bytes 196616 | tf_op jit(solution)/shard_map/ppermute | solution.py:52
  4.7 2.5 %collective-permute-start.1 = (bf16[2,64,256]{2,1,0:T(8,128)(2,1)S(1)}, bf16[2,64,256]{2,1,0:T(8,128)(2,1)S(1)}, u32[]{:S(2)}, u32[]{:S(2)}) collective-permute-start(bf16[2,64,256]{2,1,0:T(8,128)(2,1)S(1)} %get-tuple-element.20), channel_id=1, source_target_pairs={{4,8},{8,4},{12,0},{0,12},{5,9},{9,5},{13,1},{1,13},{6,10},{10,6},... | collective-permute-start | bytes 196616 | tf_op jit(solution)/shard_map/ppermute | solution.py:52
  7.3 3.9 %early.1 = (bf16[208,64,256]{2,1,0:T(8,128)(2,1)S(1)}, bf16[48,64,256]{2,1,0:T(8,128)(2,1)S(1)}, f32[8,64,128]{2,1,0:T(8,128)S(1)}) custom-call(bf16[48,64,256]{2,1,0:T(8,128)(2,1)S(1)} %bitcast.11, bf16[4,256,256]{2,1,0:T(8,128)(2,1)S(1)} %copy-done.1, s32[5,1,48]{2,1,0:T(1,128)S(1)} %bitcast.15, s32[5,1,48]{2,1,0:T(1,128)S(1)} %bitcast.17, ...), custom_call_target="tpu_custom_call" | custom-call | flops 4000000000 | bytes 4000000 | tf_op jit(solution)/shard_map/early/pallas_call | solution.py:422
  11.2 1.8 %late.1 = (bf16[208,64,256]{2,1,0:T(8,128)(2,1)S(1)}, bf16[48,64,256]{2,1,0:T(8,128)(2,1)S(1)}, f32[8,64,128]{2,1,0:T(8,128)S(1)}, bf16[96,128]{1,0:T(8,128)(2,1...) custom-call(bf16[48,64,256]{2,1,0:T(8,128)(2,1)S(1)} %bitcast.12, ...), custom_call_target="tpu_custom_call", output_to_operand_aliasing={{0}: (10, {}), {1}: (11, {}), {2}: (12, {})} | custom-call | tf_op jit(solution)/shard_map/late/pallas_call | solution.py:434
  13.0 0.6 %collective-permute-start.2 = (bf16[96,128]{1,0:T(8,128)(2,1)S(1)}, bf16[96,128]{1,0:T(8,128)(2,1)S(1)}, u32[]{:S(2)}, u32[]{:S(2)}) collective-permute-start(bf16[96,128]{1,0:T(8,128)(2,1)S(1)} %get-tuple-element.28), channel_id=1, source_target_pairs={{0,8},{4,12},{8,0},{12,4},{1,9},{5,13},{9,1},{13,5},{2,10},{6,14},... | collective-permute-start | bytes 73736 | tf_op jit(solution)/shard_map/ppermute | solution.py:68
  13.5 2.5 %collective-permute-start.3 = (bf16[96,128]{1,0:T(8,128)(2,1)S(1)}, bf16[96,128]{1,0:T(8,128)(2,1)S(1)}, u32[]{:S(2)}, u32[]{:S(2)}) collective-permute-start(bf16[96,128]{1,0:T(8,128)(2,1)S(1)} %get-tuple-element.29), channel_id=1, source_target_pairs={{0,12},{4,8},{8,4},{12,0},{1,13},{5,9},{9,5},{13,1},{2,14},{6,10},... | collective-permute-start | bytes 73736 | tf_op jit(solution)/shard_map/ppermute | solution.py:68
  16.1 0.5 %collective-permute-start.4 = (bf16[96,128]{1,0:T(8,128)(2,1)S(1)}, bf16[96,128]{1,0:T(8,128)(2,1)S(1)}, u32[]{:S(2)}, u32[]{:S(2)}) collective-permute-start(bf16[96,128]{1,0:T(8,128)(2,1)S(1)} %get-tuple-element.30), channel_id=1, source_target_pairs={{0,4},{4,0},{8,12},{12,8},{1,5},{5,1},{9,13},{13,9},{2,6},{6,2},{1... | collective-permute-start | bytes 73736 | tf_op jit(solution)/shard_map/ppermute | solution.py:68
  16.5 1.2 %order.1 = (bf16[768,768]{1,0:T(8,128)(2,1)S(1)}, bf16[48,64,256]{2,1,0:T(8,128)(2,1)}) custom-call(s32[1,192]{1,0:T(1,128)S(1)} %copy-done.6, bf16[48,64,256]{2,1,0:T(8,128)(2,1)S(1)} %get-tuple-element.24.done_ref), custom_call_target="tpu_custom_call" | custom-call | tf_op jit(solution)/shard_map/order/pallas_call | solution.py:445
  17.7 0.3 %collective-permute-done.2.refs_1_ = bf16[96,128]{1,0:T(8,128)(2,1)S(1)} collective-permute-done((bf16[96,128]{1,0:T(8,128)(2,1)S(1)}, bf16[96,128]{1,0:T(8,128)(2,1)S(1)}, u32[]{:S(2)}, u32[]{:S(2)}) %collective-permute-start.2) | collective-permute-done | bytes 24608 | tf_op jit(solution)/shard_map/ppermute | solution.py:68
  18.0 1.2 %collective-permute-done.3.refs_2_ = bf16[96,128]{1,0:T(8,128)(2,1)S(1)} collective-permute-done((bf16[96,128]{1,0:T(8,128)(2,1)S(1)}, bf16[96,128]{1,0:T(8,128)(2,1)S(1)}, u32[]{:S(2)}, u32[]{:S(2)}) %collective-permute-start.3) | collective-permute-done | bytes 24608 | tf_op jit(solution)/shard_map/ppermute | solution.py:68
  19.2 0.7 %collective-permute-done.4.refs_3_ = bf16[96,128]{1,0:T(8,128)(2,1)S(1)} collective-permute-done((bf16[96,128]{1,0:T(8,128)(2,1)S(1)}, bf16[96,128]{1,0:T(8,128)(2,1)S(1)}, u32[]{:S(2)}, u32[]{:S(2)}) %collective-permute-start.4) | collective-permute-done | bytes 24608 | tf_op jit(solution)/shard_map/ppermute | solution.py:68
  19.9 0.3 %merge.1 = (bf16[3,64,256]{2,1,0:T(8,128)(2,1)S(1)}, bf16[64,256]{1,0:T(8,128)(2,1)S(1)}, bf16[64,256]{1,0:T(8,128)(2,1)S(1)}) custom-call(bf16[768,768]{1,0:T(8,128)(2,1)S(1)} %get-tuple-element.26.order_ref, bf16[96,128]{1,0:T(8,128)(2,1)S(1)} %get-tuple-element.27.refs_0_, bf16[96,128]{1,0:T(8,128)(2,1)S(1)} %collective-permute-done.2.refs_1_, ...), custom_call_target="tpu_custom_call" | custom-call | tf_op jit(solution)/shard_map/merge/pallas_call | solution.py:460
  20.3 1.6 %collective-permute-start.5 = (bf16[3,64,256]{2,1,0:T(8,128)(2,1)S(1)}, bf16[3,64,256]{2,1,0:T(8,128)(2,1)S(1)}, u32[]{:S(2)}, u32[]{:S(2)}) collective-permute-start(bf16[3,64,256]{2,1,0:T(8,128)(2,1)S(1)} %get-tuple-element.31.coarse_ref), channel_id=1, source_target_pairs={{0,2},{2,0},{1,3},{3,1},{4,6},{6,4},{5,7},{7,5},{8,10},{10,8},{9,1... | collective-permute-start | bytes 294920 | tf_op jit(solution)/shard_map/ppermute | solution.py:34
  21.8 1.8 %collective-permute-start.6 = (bf16[64,256]{1,0:T(8,128)(2,1)S(1)}, bf16[64,256]{1,0:T(8,128)(2,1)S(1)}, u32[]{:S(2)}, u32[]{:S(2)}) collective-permute-start(bf16[64,256]{1,0:T(8,128)(2,1)S(1)} %get-tuple-element.32), channel_id=1, source_target_pairs={{4,8},{8,4},{12,0},{0,12},{5,9},{9,5},{13,1},{1,13},{6,10},{10,6},... | collective-permute-start | bytes 98312 | tf_op jit(solution)/shard_map/ppermute | solution.py:52
  23.6 1.3 %inside.1 = (f32[3,64,256]{2,1,0:T(8,128)S(1)}, bf16[5,256,256]{2,1,0:T(8,128)(2,1)S(1)}) custom-call(s32[3,1,3]{2,1,0:T(1,128)S(1)} %bitcast.19, bf16[3,64,256]{2,1,0:T(8,128)(2,1)S(1)} %get-tuple-element.31.coarse_ref, bf16[4,256,256]{2,1,0:T(8,128)(2,1)S(1)} %copy-done.2, bf16[4,64,64]{2,1,0:T(8,128)(2,1)S(1)} %copy-done.3), custom_call_target="tpu_custom_call" | custom-call | tf_op jit(solution)/shard_map/inside/pallas_call | solution.py:472
  24.9 2.7 %collective-permute-done.6.second_ref = bf16[64,256]{1,0:T(8,128)(2,1)S(1)} collective-permute-done((bf16[64,256]{1,0:T(8,128)(2,1)S(1)}, bf16[64,256]{1,0:T(8,128)(2,1)S(1)}, u32[]{:S(2)}, u32[]{:S(2)}) %collective-permute-start.6) | collective-permute-done | bytes 32800 | tf_op jit(solution)/shard_map/ppermute | solution.py:52
  27.6 0.3 %collective-permute-done.7.first_ref = bf16[64,256]{1,0:T(8,128)(2,1)S(1)} collective-permute-done((bf16[64,256]{1,0:T(8,128)(2,1)S(1)}, bf16[64,256]{1,0:T(8,128)(2,1)S(1)}, u32[]{:S(2)}, u32[]{:S(2)}) %collective-permute-start.7) | collective-permute-done | bytes 32800 | tf_op jit(solution)/shard_map/ppermute | solution.py:52
  27.9 1.2 %coarse.1 = bf16[3,64,256]{2,1,0:T(8,128)(2,1)} custom-call(bf16[3,64,256]{2,1,0:T(8,128)(2,1)S(1)} %collective-permute-done.5.seam_ref, bf16[64,256]{1,0:T(8,128)(2,1)S(1)} %collective-permute-done.6.second_ref, bf16[64,256]{1,0:T(8,128)(2,1)S(1)} %collective-permute-done.7.first_ref, bf16[3,64,256]{2,1,0:T(8,128)(2,1)S(1)} %get-tuple-element.31.coarse_ref, ...), custom_call_target="tpu_custom_call" | custom-call | tf_op jit(solution)/shard_map/coarse/pallas_call | solution.py:483
  (22 shorter events, 0.1 us)
Async XLA Ops:
  1.5 5.7 %copy-start = (bf16[1,1,48,64,256]{4,3,2,1,0:T(8,128)(2,1)S(1)}, bf16[1,1,48,64,256]{4,3,2,1,0:T(8,128)(2,1)}, u32[]{:S(2)}) copy-start(bf16[1,1,48,64,256]{4,3,2,1,0:T(8,128)(2,1)} %param.11) | copy-start | bytes 4718596
  1.5 5.7 %copy-start.1 = (bf16[4,256,256]{2,1,0:T(8,128)(2,1)S(1)}, bf16[4,256,256]{2,1,0:T(8,128)(2,1)}, u32[]{:S(2)}) copy-start(bf16[4,256,256]{2,1,0:T(8,128)(2,1)} %table_ref.3) | copy-start | bytes 1572868
  1.5 5.7 %copy-start.4 = (bf16[5,64,64]{2,1,0:T(8,128)(2,1)S(1)}, bf16[5,64,64]{2,1,0:T(8,128)(2,1)}, u32[]{:S(2)}) copy-start(bf16[5,64,64]{2,1,0:T(8,128)(2,1)} %mix_ref.5) | copy-start | bytes 122884
  1.6 5.7 %copy-start.5 = (bf16[4,256,16]{1,2,0:T(8,128)(2,1)S(1)}, bf16[4,256,16]{1,2,0:T(8,128)(2,1)}, u32[]{:S(2)}) copy-start(bf16[4,256,16]{1,2,0:T(8,128)(2,1)} %param.16) | copy-start | bytes 98308
  1.6 5.7 %copy-start.6 = (s32[1,192]{1,0:T(1,128)S(1)}, s32[1,192]{1,0:T(1,128)}, u32[]{:S(2)}) copy-start(s32[1,192]{1,0:T(1,128)} %route_ref.5) | copy-start | bytes 2308
  1.6 5.7 %copy-start.7 = (s32[1,48,5]{1,0,2:T(1,128)S(1)}, s32[1,48,5]{1,0,2:T(1,128)}, u32[]{:S(2)}) copy-start(s32[1,48,5]{1,0,2:T(1,128)} %param.14) | copy-start | bytes 2884
  1.6 5.7 %copy-start.8 = (s32[1,48,5]{1,0,2:T(1,128)S(1)}, s32[1,48,5]{1,0,2:T(1,128)}, u32[]{:S(2)}) copy-start(s32[1,48,5]{1,0,2:T(1,128)} %param.15) | copy-start | bytes 2884
  1.6 5.7 %copy-start.10 = (s32[1,48]{1,0:T(1,128)S(1)}, s32[1,48]{1,0:T(1,128)}, u32[]{:S(2)}) copy-start(s32[1,48]{1,0:T(1,128)} %rcode_ref.3) | copy-start | bytes 580
  1.6 9.5 %collective-permute-start = (bf16[2,64,256]{2,1,0:T(8,128)(2,1)S(1)}, bf16[2,64,256]{2,1,0:T(8,128)(2,1)S(1)}, u32[]{:S(2)}, u32[]{:S(2)}) collective-permute-start(bf16[2,64,256]{2,1,0:T(8,128)(2,1)S(1)} %get-tuple-element.19), channel_id=1, source_target_pairs={{0,4},{4,0},{8,12},{12,8},{1,5},{5,1},{9,13},{13,9},{2,6},{6,2},{1... | collective-permute-start | bytes 196616 | tf_op jit(solution)/shard_map/ppermute | solution.py:52
  4.7 6.4 %collective-permute-start.1 = (bf16[2,64,256]{2,1,0:T(8,128)(2,1)S(1)}, bf16[2,64,256]{2,1,0:T(8,128)(2,1)S(1)}, u32[]{:S(2)}, u32[]{:S(2)}) collective-permute-start(bf16[2,64,256]{2,1,0:T(8,128)(2,1)S(1)} %get-tuple-element.20), channel_id=1, source_target_pairs={{4,8},{8,4},{12,0},{0,12},{5,9},{9,5},{13,1},{1,13},{6,10},{10,6},... | collective-permute-start | bytes 196616 | tf_op jit(solution)/shard_map/ppermute | solution.py:52
  12.9 10.7 %copy-start.2 = (bf16[4,256,256]{2,1,0:T(8,128)(2,1)S(1)}, bf16[4,256,256]{2,1,0:T(8,128)(2,1)}, u32[]{:S(2)}) copy-start(bf16[4,256,256]{2,1,0:T(8,128)(2,1)} %spatial_ref.1) | copy-start | bytes 1572868
  13.0 10.7 %copy-start.3 = (bf16[4,64,64]{2,1,0:T(8,128)(2,1)S(1)}, bf16[4,64,64]{2,1,0:T(8,128)(2,1)}, u32[]{:S(2)}) copy-start(bf16[4,64,64]{2,1,0:T(8,128)(2,1)} %mix_ref.7) | copy-start | bytes 98308
  13.0 10.7 %copy-start.9 = (s32[1,3,3]{2,0,1:T(1,128)S(1)}, s32[1,3,3]{2,0,1:T(1,128)}, u32[]{:S(2)}) copy-start(s32[1,3,3]{2,0,1:T(1,128)} %param.21) | copy-start | bytes 112
  13.0 5.1 %collective-permute-start.2 = (bf16[96,128]{1,0:T(8,128)(2,1)S(1)}, bf16[96,128]{1,0:T(8,128)(2,1)S(1)}, u32[]{:S(2)}, u32[]{:S(2)}) collective-permute-start(bf16[96,128]{1,0:T(8,128)(2,1)S(1)} %get-tuple-element.28), channel_id=1, source_target_pairs={{0,8},{4,12},{8,0},{12,4},{1,9},{5,13},{9,1},{13,5},{2,10},{6,14},... | collective-permute-start | bytes 73736 | tf_op jit(solution)/shard_map/ppermute | solution.py:68
  13.5 5.7 %collective-permute-start.3 = (bf16[96,128]{1,0:T(8,128)(2,1)S(1)}, bf16[96,128]{1,0:T(8,128)(2,1)S(1)}, u32[]{:S(2)}, u32[]{:S(2)}) collective-permute-start(bf16[96,128]{1,0:T(8,128)(2,1)S(1)} %get-tuple-element.29), channel_id=1, source_target_pairs={{0,12},{4,8},{8,4},{12,0},{1,13},{5,9},{9,5},{13,1},{2,14},{6,10},... | collective-permute-start | bytes 73736 | tf_op jit(solution)/shard_map/ppermute | solution.py:68
  16.1 3.8 %collective-permute-start.4 = (bf16[96,128]{1,0:T(8,128)(2,1)S(1)}, bf16[96,128]{1,0:T(8,128)(2,1)S(1)}, u32[]{:S(2)}, u32[]{:S(2)}) collective-permute-start(bf16[96,128]{1,0:T(8,128)(2,1)S(1)} %get-tuple-element.30), channel_id=1, source_target_pairs={{0,4},{4,0},{8,12},{12,8},{1,5},{5,1},{9,13},{13,9},{2,6},{6,2},{1... | collective-permute-start | bytes 73736 | tf_op jit(solution)/shard_map/ppermute | solution.py:68
  20.3 7.6 %collective-permute-start.5 = (bf16[3,64,256]{2,1,0:T(8,128)(2,1)S(1)}, bf16[3,64,256]{2,1,0:T(8,128)(2,1)S(1)}, u32[]{:S(2)}, u32[]{:S(2)}) collective-permute-start(bf16[3,64,256]{2,1,0:T(8,128)(2,1)S(1)} %get-tuple-element.31.coarse_ref), channel_id=1, source_target_pairs={{0,2},{2,0},{1,3},{3,1},{4,6},{6,4},{5,7},{7,5},{8,10},{10,8},{9,1... | collective-permute-start | bytes 294920 | tf_op jit(solution)/shard_map/ppermute | solution.py:34
  21.8 5.7 %collective-permute-start.6 = (bf16[64,256]{1,0:T(8,128)(2,1)S(1)}, bf16[64,256]{1,0:T(8,128)(2,1)S(1)}, u32[]{:S(2)}, u32[]{:S(2)}) collective-permute-start(bf16[64,256]{1,0:T(8,128)(2,1)S(1)} %get-tuple-element.32), channel_id=1, source_target_pairs={{4,8},{8,4},{12,0},{0,12},{5,9},{9,5},{13,1},{1,13},{6,10},{10,6},... | collective-permute-start | bytes 98312 | tf_op jit(solution)/shard_map/ppermute | solution.py:52
  23.6 4.3 %collective-permute-start.7 = (bf16[64,256]{1,0:T(8,128)(2,1)S(1)}, bf16[64,256]{1,0:T(8,128)(2,1)S(1)}, u32[]{:S(2)}, u32[]{:S(2)}) collective-permute-start(bf16[64,256]{1,0:T(8,128)(2,1)S(1)} %get-tuple-element.33), channel_id=1, source_target_pairs={{0,4},{4,0},{8,12},{12,8},{1,5},{5,1},{9,13},{13,9},{2,6},{6,2},{1... | collective-permute-start | bytes 98312 | tf_op jit(solution)/shard_map/ppermute | solution.py:52

commit v8 on v7

--- a/solution.py
+++ b/solution.py
@@ -211,11 +211,10 @@
         (nbr, code, rcode, route, mix, restrict), in_sems,
     )
     acc_ref[...] = jnp.zeros(acc_ref.shape, F32)
-    for base in chunks_of(count):
-        rows = x_ref[base:base + CHUNK].reshape(CHUNK * channels, cells)
-        for r in range(rotations):
-            product = dot(rows, table_ref[r]).astype(BF16)
-            y_ref[pl.ds(r * extended + RIM + base, CHUNK)] = product.reshape(CHUNK, channels, cells)
+    rows = x_ref[...].reshape(count * channels, cells)
+    for r in range(rotations):
+        product = dot(rows, table_ref[r]).astype(BF16)
+        y_ref[pl.ds(r * extended + RIM, count)] = product.reshape(count, channels, cells)
     for copy in copies:
         copy.wait()
     level = Level((nbr, code, rcode, route), y_ref, x_ref, mix, restrict, done_ref, acc_ref, counts_ref)

time: 29.3 us -> 29.3 us (level)
  no operation moved by 1% of the time
where the time goes in v8:
time: 29.3 us; the launch traced here: 29.1 us
  starting transfers between devices  12.5 us (43%)
  Pallas kernels  9.65 us (33%)
  waiting for transfers between devices  5.17 us (18%)
  local copies, waits for them, and re-layouts  0.95 us (3%)
  between operations  0.84 us (3%)
    ppermute x4, starting transfers between devices, swapped(): return lax.ppermute(value, axis, pairs)  7.37 us
    pallas_call x1, Pallas kernels, per_device(): pl.pallas_call(early_kernel, out_shape=made, in_specs=given_specs, out_sp...  3.87 us
    ppermute x3, starting transfers between devices, exchanged(): return lax.ppermute(value, axis, pairs)  3.55 us
    ppermute x4, waiting for transfers between devices, swapped(): return lax.ppermute(value, axis, pairs)  2.99 us
    ppermute x3, waiting for transfers between devices, exchanged(): return lax.ppermute(value, axis, pairs)  2.18 us
    pallas_call x1, Pallas kernels, per_device(): pl.pallas_call(late_kernel, out_shape=made + (sent_shape,) * tiles, in_sp...  1.77 us
    ppermute x1, starting transfers between devices, shifted(): lax.ppermute(value, axis, [(i, (i + steps) % count) for i in range(count)])  1.56 us
    pallas_call x1, Pallas kernels, per_device(): pl.pallas_call(inside_kernel, out_shape=(jax.ShapeDtypeStruct(coarse.shap...  1.25 us
  transfers between devices with their start and end apart: 8, of which 5 were waited for; matrix products, arithmetic and copies ran while one was open for 0% of the time, Pallas kernels for 22%

profile of v8, /device:TPU:0, one launch (start us, length us, event | category | flops | bytes accessed | tf_op | source)
XLA Modules:
  0.0 29.1 jit_solution(964120273130603143)
XLA Ops:
  0.6 0.9 %slice_bitcast_fusion = (bf16[2,64,256]{2,1,0:T(8,128)(2,1)S(1)}, bf16[2,64,256]{2,1,0:T(8,128)(2,1)S(1)}) fusion(bf16[1,1,48,64,256]{4,3,2,1,0:T(8,128)(2,1)} %param.11), kind=kLoop, calls=%fused_computation | loop fusion | bytes 262144 | tf_op jit(solution)/shard_map/slice | solution.py:401
  1.5 0.0 copy-start
  1.5 0.0 copy-start.1
  1.6 0.0 copy-start.6
  1.6 0.0 copy-start.7
  1.6 0.0 copy-start.10
  1.6 3.1 %collective-permute-start = (bf16[2,64,256]{2,1,0:T(8,128)(2,1)S(1)}, bf16[2,64,256]{2,1,0:T(8,128)(2,1)S(1)}, u32[]{:S(2)}, u32[]{:S(2)}) collective-permute-start(bf16[2,64,256]{2,1,0:T(8,128)(2,1)S(1)} %get-tuple-element.19), channel_id=1, source_target_pairs={{0,4},{4,0},{8,12},{12,8},{1,5},{5,1},{9,13},{13,9},{2,6},{6,2},{1... | collective-permute-start | bytes 196616 | tf_op jit(solution)/shard_map/ppermute | solution.py:52
  4.7 2.5 %collective-permute-start.1 = (bf16[2,64,256]{2,1,0:T(8,128)(2,1)S(1)}, bf16[2,64,256]{2,1,0:T(8,128)(2,1)S(1)}, u32[]{:S(2)}, u32[]{:S(2)}) collective-permute-start(bf16[2,64,256]{2,1,0:T(8,128)(2,1)S(1)} %get-tuple-element.20), channel_id=1, source_target_pairs={{4,8},{8,4},{12,0},{0,12},{5,9},{9,5},{13,1},{1,13},{6,10},{10,6},... | collective-permute-start | bytes 196616 | tf_op jit(solution)/shard_map/ppermute | solution.py:52
  7.3 3.9 %early.1 = (bf16[208,64,256]{2,1,0:T(8,128)(2,1)S(1)}, bf16[48,64,256]{2,1,0:T(8,128)(2,1)S(1)}, f32[8,64,128]{2,1,0:T(8,128)S(1)}) custom-call(bf16[48,64,256]{2,1,0:T(8,128)(2,1)S(1)} %bitcast.11, bf16[4,256,256]{2,1,0:T(8,128)(2,1)S(1)} %copy-done.1, s32[5,1,48]{2,1,0:T(1,128)S(1)} %bitcast.15, s32[5,1,48]{2,1,0:T(1,128)S(1)} %bitcast.17, ...), custom_call_target="tpu_custom_call" | custom-call | flops 4000000000 | bytes 4000000 | tf_op jit(solution)/shard_map/early/pallas_call | solution.py:421
  11.2 1.8 %late.1 = (bf16[208,64,256]{2,1,0:T(8,128)(2,1)S(1)}, bf16[48,64,256]{2,1,0:T(8,128)(2,1)S(1)}, f32[8,64,128]{2,1,0:T(8,128)S(1)}, bf16[96,128]{1,0:T(8,128)(2,1...) custom-call(bf16[48,64,256]{2,1,0:T(8,128)(2,1)S(1)} %bitcast.12, ...), custom_call_target="tpu_custom_call", output_to_operand_aliasing={{0}: (10, {}), {1}: (11, {}), {2}: (12, {})} | custom-call | tf_op jit(solution)/shard_map/late/pallas_call | solution.py:433
  13.0 0.6 %collective-permute-start.2 = (bf16[96,128]{1,0:T(8,128)(2,1)S(1)}, bf16[96,128]{1,0:T(8,128)(2,1)S(1)}, u32[]{:S(2)}, u32[]{:S(2)}) collective-permute-start(bf16[96,128]{1,0:T(8,128)(2,1)S(1)} %get-tuple-element.28), channel_id=1, source_target_pairs={{0,8},{4,12},{8,0},{12,4},{1,9},{5,13},{9,1},{13,5},{2,10},{6,14},... | collective-permute-start | bytes 73736 | tf_op jit(solution)/shard_map/ppermute | solution.py:68
  13.5 2.5 %collective-permute-start.3 = (bf16[96,128]{1,0:T(8,128)(2,1)S(1)}, bf16[96,128]{1,0:T(8,128)(2,1)S(1)}, u32[]{:S(2)}, u32[]{:S(2)}) collective-permute-start(bf16[96,128]{1,0:T(8,128)(2,1)S(1)} %get-tuple-element.29), channel_id=1, source_target_pairs={{0,12},{4,8},{8,4},{12,0},{1,13},{5,9},{9,5},{13,1},{2,14},{6,10},... | collective-permute-start | bytes 73736 | tf_op jit(solution)/shard_map/ppermute | solution.py:68
  16.1 0.5 %collective-permute-start.4 = (bf16[96,128]{1,0:T(8,128)(2,1)S(1)}, bf16[96,128]{1,0:T(8,128)(2,1)S(1)}, u32[]{:S(2)}, u32[]{:S(2)}) collective-permute-start(bf16[96,128]{1,0:T(8,128)(2,1)S(1)} %get-tuple-element.30), channel_id=1, source_target_pairs={{0,4},{4,0},{8,12},{12,8},{1,5},{5,1},{9,13},{13,9},{2,6},{6,2},{1... | collective-permute-start | bytes 73736 | tf_op jit(solution)/shard_map/ppermute | solution.py:68
  16.5 1.2 %order.1 = (bf16[768,768]{1,0:T(8,128)(2,1)S(1)}, bf16[48,64,256]{2,1,0:T(8,128)(2,1)}) custom-call(s32[1,192]{1,0:T(1,128)S(1)} %copy-done.6, bf16[48,64,256]{2,1,0:T(8,128)(2,1)S(1)} %get-tuple-element.24.done_ref), custom_call_target="tpu_custom_call" | custom-call | tf_op jit(solution)/shard_map/order/pallas_call | solution.py:444
  17.7 0.3 %collective-permute-done.2.refs_1_ = bf16[96,128]{1,0:T(8,128)(2,1)S(1)} collective-permute-done((bf16[96,128]{1,0:T(8,128)(2,1)S(1)}, bf16[96,128]{1,0:T(8,128)(2,1)S(1)}, u32[]{:S(2)}, u32[]{:S(2)}) %collective-permute-start.2) | collective-permute-done | bytes 24608 | tf_op jit(solution)/shard_map/ppermute | solution.py:68
  18.0 1.2 %collective-permute-done.3.refs_2_ = bf16[96,128]{1,0:T(8,128)(2,1)S(1)} collective-permute-done((bf16[96,128]{1,0:T(8,128)(2,1)S(1)}, bf16[96,128]{1,0:T(8,128)(2,1)S(1)}, u32[]{:S(2)}, u32[]{:S(2)}) %collective-permute-start.3) | collective-permute-done | bytes 24608 | tf_op jit(solution)/shard_map/ppermute | solution.py:68
  19.2 0.7 %collective-permute-done.4.refs_3_ = bf16[96,128]{1,0:T(8,128)(2,1)S(1)} collective-permute-done((bf16[96,128]{1,0:T(8,128)(2,1)S(1)}, bf16[96,128]{1,0:T(8,128)(2,1)S(1)}, u32[]{:S(2)}, u32[]{:S(2)}) %collective-permute-start.4) | collective-permute-done | bytes 24608 | tf_op jit(solution)/shard_map/ppermute | solution.py:68
  19.9 0.3 %merge.1 = (bf16[3,64,256]{2,1,0:T(8,128)(2,1)S(1)}, bf16[64,256]{1,0:T(8,128)(2,1)S(1)}, bf16[64,256]{1,0:T(8,128)(2,1)S(1)}) custom-call(bf16[768,768]{1,0:T(8,128)(2,1)S(1)} %get-tuple-element.26.order_ref, bf16[96,128]{1,0:T(8,128)(2,1)S(1)} %get-tuple-element.27.refs_0_, bf16[96,128]{1,0:T(8,128)(2,1)S(1)} %collective-permute-done.2.refs_1_, ...), custom_call_target="tpu_custom_call" | custom-call | tf_op jit(solution)/shard_map/merge/pallas_call | solution.py:459
  20.3 1.6 %collective-permute-start.5 = (bf16[3,64,256]{2,1,0:T(8,128)(2,1)S(1)}, bf16[3,64,256]{2,1,0:T(8,128)(2,1)S(1)}, u32[]{:S(2)}, u32[]{:S(2)}) collective-permute-start(bf16[3,64,256]{2,1,0:T(8,128)(2,1)S(1)} %get-tuple-element.31.coarse_ref), channel_id=1, source_target_pairs={{0,2},{2,0},{1,3},{3,1},{4,6},{6,4},{5,7},{7,5},{8,10},{10,8},{9,1... | collective-permute-start | bytes 294920 | tf_op jit(solution)/shard_map/ppermute | solution.py:34
  21.8 1.8 %collective-permute-start.6 = (bf16[64,256]{1,0:T(8,128)(2,1)S(1)}, bf16[64,256]{1,0:T(8,128)(2,1)S(1)}, u32[]{:S(2)}, u32[]{:S(2)}) collective-permute-start(bf16[64,256]{1,0:T(8,128)(2,1)S(1)} %get-tuple-element.32), channel_id=1, source_target_pairs={{4,8},{8,4},{12,0},{0,12},{5,9},{9,5},{13,1},{1,13},{6,10},{10,6},... | collective-permute-start | bytes 98312 | tf_op jit(solution)/shard_map/ppermute | solution.py:52
  23.6 1.3 %inside.1 = (f32[3,64,256]{2,1,0:T(8,128)S(1)}, bf16[5,256,256]{2,1,0:T(8,128)(2,1)S(1)}) custom-call(s32[3,1,3]{2,1,0:T(1,128)S(1)} %bitcast.19, bf16[3,64,256]{2,1,0:T(8,128)(2,1)S(1)} %get-tuple-element.31.coarse_ref, bf16[4,256,256]{2,1,0:T(8,128)(2,1)S(1)} %copy-done.2, bf16[4,64,64]{2,1,0:T(8,128)(2,1)S(1)} %copy-done.3), custom_call_target="tpu_custom_call" | custom-call | tf_op jit(solution)/shard_map/inside/pallas_call | solution.py:471
  24.9 2.7 %collective-permute-done.6.second_ref = bf16[64,256]{1,0:T(8,128)(2,1)S(1)} collective-permute-done((bf16[64,256]{1,0:T(8,128)(2,1)S(1)}, bf16[64,256]{1,0:T(8,128)(2,1)S(1)}, u32[]{:S(2)}, u32[]{:S(2)}) %collective-permute-start.6) | collective-permute-done | bytes 32800 | tf_op jit(solution)/shard_map/ppermute | solution.py:52
  27.6 0.3 %collective-permute-done.7.first_ref = bf16[64,256]{1,0:T(8,128)(2,1)S(1)} collective-permute-done((bf16[64,256]{1,0:T(8,128)(2,1)S(1)}, bf16[64,256]{1,0:T(8,128)(2,1)S(1)}, u32[]{:S(2)}, u32[]{:S(2)}) %collective-permute-start.7) | collective-permute-done | bytes 32800 | tf_op jit(solution)/shard_map/ppermute | solution.py:52
  27.9 1.2 %coarse.1 = bf16[3,64,256]{2,1,0:T(8,128)(2,1)} custom-call(bf16[3,64,256]{2,1,0:T(8,128)(2,1)S(1)} %collective-permute-done.5.seam_ref, bf16[64,256]{1,0:T(8,128)(2,1)S(1)} %collective-permute-done.6.second_ref, bf16[64,256]{1,0:T(8,128)(2,1)S(1)} %collective-permute-done.7.first_ref, bf16[3,64,256]{2,1,0:T(8,128)(2,1)S(1)} %get-tuple-element.31.coarse_ref, ...), custom_call_target="tpu_custom_call" | custom-call | tf_op jit(solution)/shard_map/coarse/pallas_call | solution.py:482
  (22 shorter events, 0.1 us)
Async XLA Ops:
  1.5 5.7 %copy-start = (bf16[1,1,48,64,256]{4,3,2,1,0:T(8,128)(2,1)S(1)}, bf16[1,1,48,64,256]{4,3,2,1,0:T(8,128)(2,1)}, u32[]{:S(2)}) copy-start(bf16[1,1,48,64,256]{4,3,2,1,0:T(8,128)(2,1)} %param.11) | copy-start | bytes 4718596
  1.5 5.7 %copy-start.1 = (bf16[4,256,256]{2,1,0:T(8,128)(2,1)S(1)}, bf16[4,256,256]{2,1,0:T(8,128)(2,1)}, u32[]{:S(2)}) copy-start(bf16[4,256,256]{2,1,0:T(8,128)(2,1)} %table_ref.3) | copy-start | bytes 1572868
  1.5 5.7 %copy-start.4 = (bf16[5,64,64]{2,1,0:T(8,128)(2,1)S(1)}, bf16[5,64,64]{2,1,0:T(8,128)(2,1)}, u32[]{:S(2)}) copy-start(bf16[5,64,64]{2,1,0:T(8,128)(2,1)} %mix_ref.5) | copy-start | bytes 122884
  1.6 5.7 %copy-start.5 = (bf16[4,256,16]{1,2,0:T(8,128)(2,1)S(1)}, bf16[4,256,16]{1,2,0:T(8,128)(2,1)}, u32[]{:S(2)}) copy-start(bf16[4,256,16]{1,2,0:T(8,128)(2,1)} %param.16) | copy-start | bytes 98308
  1.6 5.7 %copy-start.6 = (s32[1,192]{1,0:T(1,128)S(1)}, s32[1,192]{1,0:T(1,128)}, u32[]{:S(2)}) copy-start(s32[1,192]{1,0:T(1,128)} %route_ref.5) | copy-start | bytes 2308
  1.6 5.7 %copy-start.7 = (s32[1,48,5]{1,0,2:T(1,128)S(1)}, s32[1,48,5]{1,0,2:T(1,128)}, u32[]{:S(2)}) copy-start(s32[1,48,5]{1,0,2:T(1,128)} %param.14) | copy-start | bytes 2884
  1.6 5.7 %copy-start.8 = (s32[1,48,5]{1,0,2:T(1,128)S(1)}, s32[1,48,5]{1,0,2:T(1,128)}, u32[]{:S(2)}) copy-start(s32[1,48,5]{1,0,2:T(1,128)} %param.15) | copy-start | bytes 2884
  1.6 5.7 %copy-start.10 = (s32[1,48]{1,0:T(1,128)S(1)}, s32[1,48]{1,0:T(1,128)}, u32[]{:S(2)}) copy-start(s32[1,48]{1,0:T(1,128)} %rcode_ref.3) | copy-start | bytes 580
  1.6 9.5 %collective-permute-start = (bf16[2,64,256]{2,1,0:T(8,128)(2,1)S(1)}, bf16[2,64,256]{2,1,0:T(8,128)(2,1)S(1)}, u32[]{:S(2)}, u32[]{:S(2)}) collective-permute-start(bf16[2,64,256]{2,1,0:T(8,128)(2,1)S(1)} %get-tuple-element.19), channel_id=1, source_target_pairs={{0,4},{4,0},{8,12},{12,8},{1,5},{5,1},{9,13},{13,9},{2,6},{6,2},{1... | collective-permute-start | bytes 196616 | tf_op jit(solution)/shard_map/ppermute | solution.py:52
  4.7 6.4 %collective-permute-start.1 = (bf16[2,64,256]{2,1,0:T(8,128)(2,1)S(1)}, bf16[2,64,256]{2,1,0:T(8,128)(2,1)S(1)}, u32[]{:S(2)}, u32[]{:S(2)}) collective-permute-start(bf16[2,64,256]{2,1,0:T(8,128)(2,1)S(1)} %get-tuple-element.20), channel_id=1, source_target_pairs={{4,8},{8,4},{12,0},{0,12},{5,9},{9,5},{13,1},{1,13},{6,10},{10,6},... | collective-permute-start | bytes 196616 | tf_op jit(solution)/shard_map/ppermute | solution.py:52
  12.9 10.7 %copy-start.2 = (bf16[4,256,256]{2,1,0:T(8,128)(2,1)S(1)}, bf16[4,256,256]{2,1,0:T(8,128)(2,1)}, u32[]{:S(2)}) copy-start(bf16[4,256,256]{2,1,0:T(8,128)(2,1)} %spatial_ref.1) | copy-start | bytes 1572868
  13.0 10.7 %copy-start.3 = (bf16[4,64,64]{2,1,0:T(8,128)(2,1)S(1)}, bf16[4,64,64]{2,1,0:T(8,128)(2,1)}, u32[]{:S(2)}) copy-start(bf16[4,64,64]{2,1,0:T(8,128)(2,1)} %mix_ref.7) | copy-start | bytes 98308
  13.0 10.7 %copy-start.9 = (s32[1,3,3]{2,0,1:T(1,128)S(1)}, s32[1,3,3]{2,0,1:T(1,128)}, u32[]{:S(2)}) copy-start(s32[1,3,3]{2,0,1:T(1,128)} %param.21) | copy-start | bytes 112
  13.0 5.1 %collective-permute-start.2 = (bf16[96,128]{1,0:T(8,128)(2,1)S(1)}, bf16[96,128]{1,0:T(8,128)(2,1)S(1)}, u32[]{:S(2)}, u32[]{:S(2)}) collective-permute-start(bf16[96,128]{1,0:T(8,128)(2,1)S(1)} %get-tuple-element.28), channel_id=1, source_target_pairs={{0,8},{4,12},{8,0},{12,4},{1,9},{5,13},{9,1},{13,5},{2,10},{6,14},... | collective-permute-start | bytes 73736 | tf_op jit(solution)/shard_map/ppermute | solution.py:68
  13.5 5.7 %collective-permute-start.3 = (bf16[96,128]{1,0:T(8,128)(2,1)S(1)}, bf16[96,128]{1,0:T(8,128)(2,1)S(1)}, u32[]{:S(2)}, u32[]{:S(2)}) collective-permute-start(bf16[96,128]{1,0:T(8,128)(2,1)S(1)} %get-tuple-element.29), channel_id=1, source_target_pairs={{0,12},{4,8},{8,4},{12,0},{1,13},{5,9},{9,5},{13,1},{2,14},{6,10},... | collective-permute-start | bytes 73736 | tf_op jit(solution)/shard_map/ppermute | solution.py:68
  16.1 3.8 %collective-permute-start.4 = (bf16[96,128]{1,0:T(8,128)(2,1)S(1)}, bf16[96,128]{1,0:T(8,128)(2,1)S(1)}, u32[]{:S(2)}, u32[]{:S(2)}) collective-permute-start(bf16[96,128]{1,0:T(8,128)(2,1)S(1)} %get-tuple-element.30), channel_id=1, source_target_pairs={{0,4},{4,0},{8,12},{12,8},{1,5},{5,1},{9,13},{13,9},{2,6},{6,2},{1... | collective-permute-start | bytes 73736 | tf_op jit(solution)/shard_map/ppermute | solution.py:68
  20.3 7.6 %collective-permute-start.5 = (bf16[3,64,256]{2,1,0:T(8,128)(2,1)S(1)}, bf16[3,64,256]{2,1,0:T(8,128)(2,1)S(1)}, u32[]{:S(2)}, u32[]{:S(2)}) collective-permute-start(bf16[3,64,256]{2,1,0:T(8,128)(2,1)S(1)} %get-tuple-element.31.coarse_ref), channel_id=1, source_target_pairs={{0,2},{2,0},{1,3},{3,1},{4,6},{6,4},{5,7},{7,5},{8,10},{10,8},{9,1... | collective-permute-start | bytes 294920 | tf_op jit(solution)/shard_map/ppermute | solution.py:34
  21.8 5.7 %collective-permute-start.6 = (bf16[64,256]{1,0:T(8,128)(2,1)S(1)}, bf16[64,256]{1,0:T(8,128)(2,1)S(1)}, u32[]{:S(2)}, u32[]{:S(2)}) collective-permute-start(bf16[64,256]{1,0:T(8,128)(2,1)S(1)} %get-tuple-element.32), channel_id=1, source_target_pairs={{4,8},{8,4},{12,0},{0,12},{5,9},{9,5},{13,1},{1,13},{6,10},{10,6},... | collective-permute-start | bytes 98312 | tf_op jit(solution)/shard_map/ppermute | solution.py:52
  23.6 4.3 %collective-permute-start.7 = (bf16[64,256]{1,0:T(8,128)(2,1)S(1)}, bf16[64,256]{1,0:T(8,128)(2,1)S(1)}, u32[]{:S(2)}, u32[]{:S(2)}) collective-permute-start(bf16[64,256]{1,0:T(8,128)(2,1)S(1)} %get-tuple-element.33), channel_id=1, source_target_pairs={{0,4},{4,0},{8,12},{12,8},{1,5},{5,1},{9,13},{13,9},{2,6},{6,2},{1... | collective-permute-start | bytes 98312 | tf_op jit(solution)/shard_map/ppermute | solution.py:52

commit v9 on v8

--- a/solution.py
+++ b/solution.py
@@ -354,7 +354,7 @@
     table_ref[1] = spatial_ref[code_ref[blocks - 1, 0, 1]]
 
 
-def coarse_kernel(seam_ref, second_ref, first_ref, coarse_ref, total_ref, table_ref, mix_ref, out_ref):
+def coarse_kernel(second_ref, seam_ref, first_ref, coarse_ref, total_ref, table_ref, mix_ref, out_ref):
     blocks = coarse_ref.shape[0]
     right = faces_right()
     left_rows = jnp.where(right, second_ref[...], first_ref[...])
@@ -486,7 +486,7 @@
         out_specs=VMEM(),
         compiler_params=params(),
         name="coarse",
-    )(seam, second, first, coarse, total, tables, coarse_mix)
+    )(second, seam, first, coarse, total, tables, coarse_mix)
     return (skip[None, None], coarse_out[None, None])
 
 

time: 29.3 us -> 29.3 us (level)
  no operation moved by 1% of the time
where the time goes in v9:
time: 29.3 us; the launch traced here: 29.1 us
  starting transfers between devices  12.5 us (43%)
  Pallas kernels  9.64 us (33%)
  waiting for transfers between devices  5.17 us (18%)
  local copies, waits for them, and re-layouts  0.95 us (3%)
  between operations  0.84 us (3%)
    ppermute x4, starting transfers between devices, swapped(): return lax.ppermute(value, axis, pairs)  7.37 us
    pallas_call x1, Pallas kernels, per_device(): pl.pallas_call(early_kernel, out_shape=made, in_specs=given_specs, out_sp...  3.87 us
    ppermute x3, starting transfers between devices, exchanged(): return lax.ppermute(value, axis, pairs)  3.55 us
    ppermute x4, waiting for transfers between devices, swapped(): return lax.ppermute(value, axis, pairs)  2.99 us
    ppermute x3, waiting for transfers between devices, exchanged(): return lax.ppermute(value, axis, pairs)  2.18 us
    pallas_call x1, Pallas kernels, per_device(): pl.pallas_call(late_kernel, out_shape=made + (sent_shape,) * tiles, in_sp...  1.77 us
    ppermute x1, starting transfers between devices, shifted(): lax.ppermute(value, axis, [(i, (i + steps) % count) for i in range(count)])  1.57 us
    pallas_call x1, Pallas kernels, per_device(): pl.pallas_call(inside_kernel, out_shape=(jax.ShapeDtypeStruct(coarse.shap...  1.25 us
  transfers between devices with their start and end apart: 8, of which 5 were waited for; matrix products, arithmetic and copies ran while one was open for 0% of the time, Pallas kernels for 22%

profile of v9, /device:TPU:0, one launch (start us, length us, event | category | flops | bytes accessed | tf_op | source)
XLA Modules:
  0.0 29.1 jit_solution(6242029102066565600)
XLA Ops:
  0.6 0.9 %slice_bitcast_fusion = (bf16[2,64,256]{2,1,0:T(8,128)(2,1)S(1)}, bf16[2,64,256]{2,1,0:T(8,128)(2,1)S(1)}) fusion(bf16[1,1,48,64,256]{4,3,2,1,0:T(8,128)(2,1)} %param.11), kind=kLoop, calls=%fused_computation | loop fusion | bytes 262144 | tf_op jit(solution)/shard_map/slice | solution.py:401
  1.5 0.0 copy-start
  1.5 0.0 copy-start.1
  1.6 0.0 copy-start.6
  1.6 0.0 copy-start.7
  1.6 0.0 copy-start.10
  1.6 3.1 %collective-permute-start = (bf16[2,64,256]{2,1,0:T(8,128)(2,1)S(1)}, bf16[2,64,256]{2,1,0:T(8,128)(2,1)S(1)}, u32[]{:S(2)}, u32[]{:S(2)}) collective-permute-start(bf16[2,64,256]{2,1,0:T(8,128)(2,1)S(1)} %get-tuple-element.19), channel_id=1, source_target_pairs={{0,4},{4,0},{8,12},{12,8},{1,5},{5,1},{9,13},{13,9},{2,6},{6,2},{1... | collective-permute-start | bytes 196616 | tf_op jit(solution)/shard_map/ppermute | solution.py:52
  4.7 2.5 %collective-permute-start.1 = (bf16[2,64,256]{2,1,0:T(8,128)(2,1)S(1)}, bf16[2,64,256]{2,1,0:T(8,128)(2,1)S(1)}, u32[]{:S(2)}, u32[]{:S(2)}) collective-permute-start(bf16[2,64,256]{2,1,0:T(8,128)(2,1)S(1)} %get-tuple-element.20), channel_id=1, source_target_pairs={{4,8},{8,4},{12,0},{0,12},{5,9},{9,5},{13,1},{1,13},{6,10},{10,6},... | collective-permute-start | bytes 196616 | tf_op jit(solution)/shard_map/ppermute | solution.py:52
  7.3 3.9 %early.1 = (bf16[208,64,256]{2,1,0:T(8,128)(2,1)S(1)}, bf16[48,64,256]{2,1,0:T(8,128)(2,1)S(1)}, f32[8,64,128]{2,1,0:T(8,128)S(1)}) custom-call(bf16[48,64,256]{2,1,0:T(8,128)(2,1)S(1)} %bitcast.11, bf16[4,256,256]{2,1,0:T(8,128)(2,1)S(1)} %copy-done.1, s32[5,1,48]{2,1,0:T(1,128)S(1)} %bitcast.15, s32[5,1,48]{2,1,0:T(1,128)S(1)} %bitcast.17, ...), custom_call_target="tpu_custom_call" | custom-call | flops 4000000000 | bytes 4000000 | tf_op jit(solution)/shard_map/early/pallas_call | solution.py:421
  11.2 1.8 %late.1 = (bf16[208,64,256]{2,1,0:T(8,128)(2,1)S(1)}, bf16[48,64,256]{2,1,0:T(8,128)(2,1)S(1)}, f32[8,64,128]{2,1,0:T(8,128)S(1)}, bf16[96,128]{1,0:T(8,128)(2,1...) custom-call(bf16[48,64,256]{2,1,0:T(8,128)(2,1)S(1)} %bitcast.12, ...), custom_call_target="tpu_custom_call", output_to_operand_aliasing={{0}: (10, {}), {1}: (11, {}), {2}: (12, {})} | custom-call | tf_op jit(solution)/shard_map/late/pallas_call | solution.py:433
  13.0 0.6 %collective-permute-start.2 = (bf16[96,128]{1,0:T(8,128)(2,1)S(1)}, bf16[96,128]{1,0:T(8,128)(2,1)S(1)}, u32[]{:S(2)}, u32[]{:S(2)}) collective-permute-start(bf16[96,128]{1,0:T(8,128)(2,1)S(1)} %get-tuple-element.28), channel_id=1, source_target_pairs={{0,8},{4,12},{8,0},{12,4},{1,9},{5,13},{9,1},{13,5},{2,10},{6,14},... | collective-permute-start | bytes 73736 | tf_op jit(solution)/shard_map/ppermute | solution.py:68
  13.5 2.5 %collective-permute-start.3 = (bf16[96,128]{1,0:T(8,128)(2,1)S(1)}, bf16[96,128]{1,0:T(8,128)(2,1)S(1)}, u32[]{:S(2)}, u32[]{:S(2)}) collective-permute-start(bf16[96,128]{1,0:T(8,128)(2,1)S(1)} %get-tuple-element.29), channel_id=1, source_target_pairs={{0,12},{4,8},{8,4},{12,0},{1,13},{5,9},{9,5},{13,1},{2,14},{6,10},... | collective-permute-start | bytes 73736 | tf_op jit(solution)/shard_map/ppermute | solution.py:68
  16.1 0.5 %collective-permute-start.4 = (bf16[96,128]{1,0:T(8,128)(2,1)S(1)}, bf16[96,128]{1,0:T(8,128)(2,1)S(1)}, u32[]{:S(2)}, u32[]{:S(2)}) collective-permute-start(bf16[96,128]{1,0:T(8,128)(2,1)S(1)} %get-tuple-element.30), channel_id=1, source_target_pairs={{0,4},{4,0},{8,12},{12,8},{1,5},{5,1},{9,13},{13,9},{2,6},{6,2},{1... | collective-permute-start | bytes 73736 | tf_op jit(solution)/shard_map/ppermute | solution.py:68
  16.5 1.2 %order.1 = (bf16[768,768]{1,0:T(8,128)(2,1)S(1)}, bf16[48,64,256]{2,1,0:T(8,128)(2,1)}) custom-call(s32[1,192]{1,0:T(1,128)S(1)} %copy-done.6, bf16[48,64,256]{2,1,0:T(8,128)(2,1)S(1)} %get-tuple-element.24.done_ref), custom_call_target="tpu_custom_call" | custom-call | tf_op jit(solution)/shard_map/order/pallas_call | solution.py:444
  17.7 0.3 %collective-permute-done.2.refs_1_ = bf16[96,128]{1,0:T(8,128)(2,1)S(1)} collective-permute-done((bf16[96,128]{1,0:T(8,128)(2,1)S(1)}, bf16[96,128]{1,0:T(8,128)(2,1)S(1)}, u32[]{:S(2)}, u32[]{:S(2)}) %collective-permute-start.2) | collective-permute-done | bytes 24608 | tf_op jit(solution)/shard_map/ppermute | solution.py:68
  18.0 1.2 %collective-permute-done.3.refs_2_ = bf16[96,128]{1,0:T(8,128)(2,1)S(1)} collective-permute-done((bf16[96,128]{1,0:T(8,128)(2,1)S(1)}, bf16[96,128]{1,0:T(8,128)(2,1)S(1)}, u32[]{:S(2)}, u32[]{:S(2)}) %collective-permute-start.3) | collective-permute-done | bytes 24608 | tf_op jit(solution)/shard_map/ppermute | solution.py:68
  19.2 0.7 %collective-permute-done.4.refs_3_ = bf16[96,128]{1,0:T(8,128)(2,1)S(1)} collective-permute-done((bf16[96,128]{1,0:T(8,128)(2,1)S(1)}, bf16[96,128]{1,0:T(8,128)(2,1)S(1)}, u32[]{:S(2)}, u32[]{:S(2)}) %collective-permute-start.4) | collective-permute-done | bytes 24608 | tf_op jit(solution)/shard_map/ppermute | solution.py:68
  19.9 0.3 %merge.1 = (bf16[3,64,256]{2,1,0:T(8,128)(2,1)S(1)}, bf16[64,256]{1,0:T(8,128)(2,1)S(1)}, bf16[64,256]{1,0:T(8,128)(2,1)S(1)}) custom-call(bf16[768,768]{1,0:T(8,128)(2,1)S(1)} %get-tuple-element.26.order_ref, bf16[96,128]{1,0:T(8,128)(2,1)S(1)} %get-tuple-element.27.refs_0_, bf16[96,128]{1,0:T(8,128)(2,1)S(1)} %collective-permute-done.2.refs_1_, ...), custom_call_target="tpu_custom_call" | custom-call | tf_op jit(solution)/shard_map/merge/pallas_call | solution.py:459
  20.3 1.6 %collective-permute-start.6 = (bf16[3,64,256]{2,1,0:T(8,128)(2,1)S(1)}, bf16[3,64,256]{2,1,0:T(8,128)(2,1)S(1)}, u32[]{:S(2)}, u32[]{:S(2)}) collective-permute-start(bf16[3,64,256]{2,1,0:T(8,128)(2,1)S(1)} %get-tuple-element.32.coarse_ref), channel_id=1, source_target_pairs={{0,2},{2,0},{1,3},{3,1},{4,6},{6,4},{5,7},{7,5},{8,10},{10,8},{9,1... | collective-permute-start | bytes 294920 | tf_op jit(solution)/shard_map/ppermute | solution.py:34
  21.8 1.8 %collective-permute-start.5 = (bf16[64,256]{1,0:T(8,128)(2,1)S(1)}, bf16[64,256]{1,0:T(8,128)(2,1)S(1)}, u32[]{:S(2)}, u32[]{:S(2)}) collective-permute-start(bf16[64,256]{1,0:T(8,128)(2,1)S(1)} %get-tuple-element.31), channel_id=1, source_target_pairs={{4,8},{8,4},{12,0},{0,12},{5,9},{9,5},{13,1},{1,13},{6,10},{10,6},... | collective-permute-start | bytes 98312 | tf_op jit(solution)/shard_map/ppermute | solution.py:52
  23.6 1.2 %inside.1 = (f32[3,64,256]{2,1,0:T(8,128)S(1)}, bf16[5,256,256]{2,1,0:T(8,128)(2,1)S(1)}) custom-call(s32[3,1,3]{2,1,0:T(1,128)S(1)} %bitcast.19, bf16[3,64,256]{2,1,0:T(8,128)(2,1)S(1)} %get-tuple-element.32.coarse_ref, bf16[4,256,256]{2,1,0:T(8,128)(2,1)S(1)} %copy-done.2, bf16[4,64,64]{2,1,0:T(8,128)(2,1)S(1)} %copy-done.3), custom_call_target="tpu_custom_call" | custom-call | tf_op jit(solution)/shard_map/inside/pallas_call | solution.py:471
  24.9 2.7 %collective-permute-done.5.second_ref = bf16[64,256]{1,0:T(8,128)(2,1)S(1)} collective-permute-done((bf16[64,256]{1,0:T(8,128)(2,1)S(1)}, bf16[64,256]{1,0:T(8,128)(2,1)S(1)}, u32[]{:S(2)}, u32[]{:S(2)}) %collective-permute-start.5) | collective-permute-done | bytes 32800 | tf_op jit(solution)/shard_map/ppermute | solution.py:52
  27.6 0.3 %collective-permute-done.7.first_ref = bf16[64,256]{1,0:T(8,128)(2,1)S(1)} collective-permute-done((bf16[64,256]{1,0:T(8,128)(2,1)S(1)}, bf16[64,256]{1,0:T(8,128)(2,1)S(1)}, u32[]{:S(2)}, u32[]{:S(2)}) %collective-permute-start.7) | collective-permute-done | bytes 32800 | tf_op jit(solution)/shard_map/ppermute | solution.py:52
  27.9 1.2 %coarse.1 = bf16[3,64,256]{2,1,0:T(8,128)(2,1)} custom-call(bf16[64,256]{1,0:T(8,128)(2,1)S(1)} %collective-permute-done.5.second_ref, bf16[3,64,256]{2,1,0:T(8,128)(2,1)S(1)} %collective-permute-done.6.seam_ref, bf16[64,256]{1,0:T(8,128)(2,1)S(1)} %collective-permute-done.7.first_ref, bf16[3,64,256]{2,1,0:T(8,128)(2,1)S(1)} %get-tuple-element.32.coarse_ref, ...), custom_call_target="tpu_custom_call" | custom-call | tf_op jit(solution)/shard_map/coarse/pallas_call | solution.py:482
  (22 shorter events, 0.1 us)
Async XLA Ops:
  1.5 5.7 %copy-start = (bf16[1,1,48,64,256]{4,3,2,1,0:T(8,128)(2,1)S(1)}, bf16[1,1,48,64,256]{4,3,2,1,0:T(8,128)(2,1)}, u32[]{:S(2)}) copy-start(bf16[1,1,48,64,256]{4,3,2,1,0:T(8,128)(2,1)} %param.11) | copy-start | bytes 4718596
  1.5 5.7 %copy-start.1 = (bf16[4,256,256]{2,1,0:T(8,128)(2,1)S(1)}, bf16[4,256,256]{2,1,0:T(8,128)(2,1)}, u32[]{:S(2)}) copy-start(bf16[4,256,256]{2,1,0:T(8,128)(2,1)} %table_ref.3) | copy-start | bytes 1572868
  1.5 5.7 %copy-start.4 = (bf16[5,64,64]{2,1,0:T(8,128)(2,1)S(1)}, bf16[5,64,64]{2,1,0:T(8,128)(2,1)}, u32[]{:S(2)}) copy-start(bf16[5,64,64]{2,1,0:T(8,128)(2,1)} %mix_ref.5) | copy-start | bytes 122884
  1.6 5.7 %copy-start.5 = (bf16[4,256,16]{1,2,0:T(8,128)(2,1)S(1)}, bf16[4,256,16]{1,2,0:T(8,128)(2,1)}, u32[]{:S(2)}) copy-start(bf16[4,256,16]{1,2,0:T(8,128)(2,1)} %param.16) | copy-start | bytes 98308
  1.6 5.7 %copy-start.6 = (s32[1,192]{1,0:T(1,128)S(1)}, s32[1,192]{1,0:T(1,128)}, u32[]{:S(2)}) copy-start(s32[1,192]{1,0:T(1,128)} %route_ref.5) | copy-start | bytes 2308
  1.6 5.7 %copy-start.7 = (s32[1,48,5]{1,0,2:T(1,128)S(1)}, s32[1,48,5]{1,0,2:T(1,128)}, u32[]{:S(2)}) copy-start(s32[1,48,5]{1,0,2:T(1,128)} %param.14) | copy-start | bytes 2884
  1.6 5.7 %copy-start.8 = (s32[1,48,5]{1,0,2:T(1,128)S(1)}, s32[1,48,5]{1,0,2:T(1,128)}, u32[]{:S(2)}) copy-start(s32[1,48,5]{1,0,2:T(1,128)} %param.15) | copy-start | bytes 2884
  1.6 5.7 %copy-start.10 = (s32[1,48]{1,0:T(1,128)S(1)}, s32[1,48]{1,0:T(1,128)}, u32[]{:S(2)}) copy-start(s32[1,48]{1,0:T(1,128)} %rcode_ref.3) | copy-start | bytes 580
  1.6 9.5 %collective-permute-start = (bf16[2,64,256]{2,1,0:T(8,128)(2,1)S(1)}, bf16[2,64,256]{2,1,0:T(8,128)(2,1)S(1)}, u32[]{:S(2)}, u32[]{:S(2)}) collective-permute-start(bf16[2,64,256]{2,1,0:T(8,128)(2,1)S(1)} %get-tuple-element.19), channel_id=1, source_target_pairs={{0,4},{4,0},{8,12},{12,8},{1,5},{5,1},{9,13},{13,9},{2,6},{6,2},{1... | collective-permute-start | bytes 196616 | tf_op jit(solution)/shard_map/ppermute | solution.py:52
  4.7 6.4 %collective-permute-start.1 = (bf16[2,64,256]{2,1,0:T(8,128)(2,1)S(1)}, bf16[2,64,256]{2,1,0:T(8,128)(2,1)S(1)}, u32[]{:S(2)}, u32[]{:S(2)}) collective-permute-start(bf16[2,64,256]{2,1,0:T(8,128)(2,1)S(1)} %get-tuple-element.20), channel_id=1, source_target_pairs={{4,8},{8,4},{12,0},{0,12},{5,9},{9,5},{13,1},{1,13},{6,10},{10,6},... | collective-permute-start | bytes 196616 | tf_op jit(solution)/shard_map/ppermute | solution.py:52
  12.9 10.7 %copy-start.2 = (bf16[4,256,256]{2,1,0:T(8,128)(2,1)S(1)}, bf16[4,256,256]{2,1,0:T(8,128)(2,1)}, u32[]{:S(2)}) copy-start(bf16[4,256,256]{2,1,0:T(8,128)(2,1)} %spatial_ref.1) | copy-start | bytes 1572868
  13.0 10.7 %copy-start.3 = (bf16[4,64,64]{2,1,0:T(8,128)(2,1)S(1)}, bf16[4,64,64]{2,1,0:T(8,128)(2,1)}, u32[]{:S(2)}) copy-start(bf16[4,64,64]{2,1,0:T(8,128)(2,1)} %mix_ref.7) | copy-start | bytes 98308
  13.0 10.7 %copy-start.9 = (s32[1,3,3]{2,0,1:T(1,128)S(1)}, s32[1,3,3]{2,0,1:T(1,128)}, u32[]{:S(2)}) copy-start(s32[1,3,3]{2,0,1:T(1,128)} %param.21) | copy-start | bytes 112
  13.0 5.1 %collective-permute-start.2 = (bf16[96,128]{1,0:T(8,128)(2,1)S(1)}, bf16[96,128]{1,0:T(8,128)(2,1)S(1)}, u32[]{:S(2)}, u32[]{:S(2)}) collective-permute-start(bf16[96,128]{1,0:T(8,128)(2,1)S(1)} %get-tuple-element.28), channel_id=1, source_target_pairs={{0,8},{4,12},{8,0},{12,4},{1,9},{5,13},{9,1},{13,5},{2,10},{6,14},... | collective-permute-start | bytes 73736 | tf_op jit(solution)/shard_map/ppermute | solution.py:68
  13.5 5.7 %collective-permute-start.3 = (bf16[96,128]{1,0:T(8,128)(2,1)S(1)}, bf16[96,128]{1,0:T(8,128)(2,1)S(1)}, u32[]{:S(2)}, u32[]{:S(2)}) collective-permute-start(bf16[96,128]{1,0:T(8,128)(2,1)S(1)} %get-tuple-element.29), channel_id=1, source_target_pairs={{0,12},{4,8},{8,4},{12,0},{1,13},{5,9},{9,5},{13,1},{2,14},{6,10},... | collective-permute-start | bytes 73736 | tf_op jit(solution)/shard_map/ppermute | solution.py:68
  16.1 3.8 %collective-permute-start.4 = (bf16[96,128]{1,0:T(8,128)(2,1)S(1)}, bf16[96,128]{1,0:T(8,128)(2,1)S(1)}, u32[]{:S(2)}, u32[]{:S(2)}) collective-permute-start(bf16[96,128]{1,0:T(8,128)(2,1)S(1)} %get-tuple-element.30), channel_id=1, source_target_pairs={{0,4},{4,0},{8,12},{12,8},{1,5},{5,1},{9,13},{13,9},{2,6},{6,2},{1... | collective-permute-start | bytes 73736 | tf_op jit(solution)/shard_map/ppermute | solution.py:68
  20.3 7.6 %collective-permute-start.6 = (bf16[3,64,256]{2,1,0:T(8,128)(2,1)S(1)}, bf16[3,64,256]{2,1,0:T(8,128)(2,1)S(1)}, u32[]{:S(2)}, u32[]{:S(2)}) collective-permute-start(bf16[3,64,256]{2,1,0:T(8,128)(2,1)S(1)} %get-tuple-element.32.coarse_ref), channel_id=1, source_target_pairs={{0,2},{2,0},{1,3},{3,1},{4,6},{6,4},{5,7},{7,5},{8,10},{10,8},{9,1... | collective-permute-start | bytes 294920 | tf_op jit(solution)/shard_map/ppermute | solution.py:34
  21.8 5.7 %collective-permute-start.5 = (bf16[64,256]{1,0:T(8,128)(2,1)S(1)}, bf16[64,256]{1,0:T(8,128)(2,1)S(1)}, u32[]{:S(2)}, u32[]{:S(2)}) collective-permute-start(bf16[64,256]{1,0:T(8,128)(2,1)S(1)} %get-tuple-element.31), channel_id=1, source_target_pairs={{4,8},{8,4},{12,0},{0,12},{5,9},{9,5},{13,1},{1,13},{6,10},{10,6},... | collective-permute-start | bytes 98312 | tf_op jit(solution)/shard_map/ppermute | solution.py:52
  23.6 4.3 %collective-permute-start.7 = (bf16[64,256]{1,0:T(8,128)(2,1)S(1)}, bf16[64,256]{1,0:T(8,128)(2,1)S(1)}, u32[]{:S(2)}, u32[]{:S(2)}) collective-permute-start(bf16[64,256]{1,0:T(8,128)(2,1)S(1)} %get-tuple-element.33), channel_id=1, source_target_pairs={{0,4},{4,0},{8,12},{12,8},{1,5},{5,1},{9,13},{13,9},{2,6},{6,2},{1... | collective-permute-start | bytes 98312 | tf_op jit(solution)/shard_map/ppermute | solution.py:52
